TPU v7x, 32 devices: a whole 2x2x4 slice. The times are simulated.
32 devices in a mesh: dp: 8 (over y, x, core), tensor: 4 (over z).
Axes of the slice: x: 2, y: 2, z: 4, core: 2. Of those that a mesh axis runs over, the one named last changes fastest.
Arguments:
- tokens: bfloat16 [16384, 1024], P(('dp', 'tensor')), may hold values from -6 to 6
- cotangent: bfloat16 [16384, 1024], P(('dp', 'tensor')), may hold values from -6 to 6
- segments: int32 [16384], P('dp'), may hold values from 0 to 18, as said below
- attn_w: float32 [4, 1024, 1024], P(None, 'dp', 'tensor')
- mlp_w: float32 [2, 1024, 4096], P(None, 'dp', 'tensor')
- vectors: float32 [12, 1024], replicated
- attn_mom: float32 [4, 1024, 1024], P(None, 'dp', 'tensor')
- mlp_mom: float32 [2, 1024, 4096], P(None, 'dp', 'tensor')
- vector_mom: float32 [12, 1024], replicated, may hold values from -768 to 768
Outputs:
- block_out: bfloat16 [16384, 1024], P(('dp', 'tensor'))
- dx: float32 [16384, 1024], P(('dp', 'tensor'))
- attn_mom_new: float32 [4, 1024, 1024], P(None, 'dp', 'tensor')
- attn_new: float32 [4, 1024, 1024], P(None, 'dp', 'tensor')
- mlp_mom_new: float32 [2, 1024, 4096], P(None, 'dp', 'tensor')
- mlp_new: float32 [2, 1024, 4096], P(None, 'dp', 'tensor')
- vector_mom_new: float32 [12, 1024], replicated
- vector_new: float32 [12, 1024], replicated
Inputs may be any that keep to these rules, and one draw needn't show every extreme that they name: `segments`: within each sequence of 1024 tokens the ids above zero never fall; an id above zero is one document of 60 to 800 tokens, the last document of a sequence possibly cut shorter, and the last document of every sequence has the id 1024 // 60 + 1; zero marks padding of fewer than 60 tokens at a sequence's end.
All inputs are finite; a program needn't handle non-finite values.
Results may differ from a plain program's by a relative error of at most 0.033.
Values may be sent and summed in bfloat16 or wider, within the bound.
A program may use at most 128 MiB of HBM per device.

v0:
```python
import math

import jax
import jax.numpy as jnp
from jax import lax
from jax.sharding import PartitionSpec as P

D = 1024
HEADS = 16
HD = 64
FF = 4096
SEQ = 1024
NS_STEPS = 5


coeff_a = 3.4445
coeff_b = -4.775
coeff_c = 2.0315


def norm_rows(row_data, gain, shift):
    center = jnp.mean(row_data, axis=-1, keepdims=True)
    centred = row_data - center
    spread = jnp.mean(centred * centred, axis=-1, keepdims=True)
    return centred * lax.rsqrt(spread + 1e-05) * gain + shift


def gelu_tanh(values):
    return jax.nn.gelu(values, approximate=True)


def contract_last(left, right):
    return lax.dot_general(
        left, right, (((1,), (1,)), ((), ())), preferred_element_type=jnp.float32
    )


def contract_first(left, right):
    return lax.dot_general(
        left, right, (((0,), (0,)), ((), ())), preferred_element_type=jnp.float32
    )


def head_slopes(first_head, head_count):
    head_ids = (first_head + jnp.arange(head_count)).astype(jnp.float32)
    return jnp.exp2(-(8.0 / HEADS) * (head_ids + 1.0))


def masked_scores(row_query, key_rows, row_segs, seg_ids, row_start, slopes):
    scores = jnp.einsum("qhd,khd->hqk", row_query, key_rows, preferred_element_type=jnp.float32) * (
        1.0 / math.sqrt(HD)
    )
    query_pos = row_start + jnp.arange(row_query.shape[0])
    key_pos = jnp.arange(key_rows.shape[0])
    distance = (query_pos[:, None] - key_pos[None, :]).astype(jnp.float32)
    scores = scores - slopes[:, None, None] * distance[None]
    same_doc = (
        (row_segs[:, None] == seg_ids[None, :])
        & (row_segs[:, None] > 0)
        & (key_pos[None, :] <= query_pos[:, None])
    )
    allowed = same_doc | (key_pos[None, :] == query_pos[:, None])
    return jnp.where(allowed[None], scores, -1e30)


def attend_forward(query, key_rows, value_rows, seg_ids, slopes, row_block):
    length = key_rows.shape[0]

    def one_block(row_start):
        row_query = lax.dynamic_slice_in_dim(query, row_start, row_block, 0)
        row_segs = lax.dynamic_slice_in_dim(seg_ids, row_start, row_block, 0)
        scores = masked_scores(row_query, key_rows, row_segs, seg_ids, row_start, slopes)
        row_max = jnp.max(scores, axis=-1, keepdims=True)
        exp_scores = jnp.exp(scores - row_max)
        row_total = jnp.sum(exp_scores, axis=-1, keepdims=True)
        attn_probs = (exp_scores / row_total).astype(jnp.bfloat16)
        mixed = jnp.einsum(
            "hqk,khd->qhd", attn_probs, value_rows, preferred_element_type=jnp.float32
        )
        return (mixed.astype(jnp.bfloat16), (row_max + jnp.log(row_total))[..., 0])

    block_starts = jnp.arange(length // row_block) * row_block
    mixed, log_sums = lax.map(one_block, block_starts)
    return (mixed.reshape(length, -1), log_sums)


def attend_backward(query, key_rows, value_rows, seg_ids, log_sums, grad_mixed, slopes, row_block):
    length, head_count, head_dim = key_rows.shape
    factor = 1.0 / math.sqrt(HD)

    def one_block(carry, pieces):
        row_start, row_lse = pieces
        row_query = lax.dynamic_slice_in_dim(query, row_start, row_block, 0)
        row_grad = lax.dynamic_slice_in_dim(grad_mixed, row_start, row_block, 0)
        row_segs = lax.dynamic_slice_in_dim(seg_ids, row_start, row_block, 0)
        scores = masked_scores(row_query, key_rows, row_segs, seg_ids, row_start, slopes)
        attn_probs = jnp.exp(scores - row_lse[:, :, None])
        grad_probs = jnp.einsum(
            "qhd,khd->hqk", row_grad, value_rows, preferred_element_type=jnp.float32
        )
        inner = jnp.sum(grad_probs * attn_probs, axis=-1, keepdims=True)
        grad_scores = (attn_probs * (grad_probs - inner)).astype(jnp.bfloat16)
        grad_query = (
            jnp.einsum("hqk,khd->qhd", grad_scores, key_rows, preferred_element_type=jnp.float32)
            * factor
        )
        grad_keys = (
            carry[0]
            + jnp.einsum("hqk,qhd->khd", grad_scores, row_query, preferred_element_type=jnp.float32)
            * factor
        )
        grad_values = carry[1] + jnp.einsum(
            "hqk,qhd->khd",
            attn_probs.astype(jnp.bfloat16),
            row_grad,
            preferred_element_type=jnp.float32,
        )
        return ((grad_keys, grad_values), grad_query)

    empty = jnp.zeros((length, head_count, head_dim), jnp.float32)
    block_starts = jnp.arange(length // row_block) * row_block
    (grad_keys, grad_values), grad_query = lax.scan(
        one_block, (empty, empty), (block_starts, log_sums)
    )
    return (
        grad_query.reshape(length, -1),
        grad_keys.reshape(length, -1),
        grad_values.reshape(length, -1),
    )


def newton_rows(row_iterate):
    for repeat in range(NS_STEPS + 1):
        whole_iterate = lax.all_gather(row_iterate, "tensor", axis=0, tiled=True)
        if repeat == NS_STEPS:
            break
        square_rows = contract_last(row_iterate, whole_iterate).astype(jnp.bfloat16)
        whole_square = lax.all_gather(square_rows, "tensor", axis=0, tiled=True)
        poly_rows = (
            coeff_b * square_rows.astype(jnp.float32)
            + coeff_c * jnp.dot(square_rows, whole_square, preferred_element_type=jnp.float32)
        ).astype(jnp.bfloat16)
        row_iterate = (
            coeff_a * row_iterate.astype(jnp.float32)
            + jnp.dot(poly_rows, whole_iterate, preferred_element_type=jnp.float32)
        ).astype(jnp.bfloat16)
    return whole_iterate


def on_device(tokens, cotangent, segments, attn_w, mlp_w, vectors, attn_mom, mlp_mom, vector_mom):
    tensor_size = lax.axis_size("tensor")
    dp_size = lax.axis_size("dp")
    tensor_index = lax.axis_index("tensor")
    dp_index = lax.axis_index("dp")
    row_count = tokens.shape[0]
    model_width = tokens.shape[1]
    local_width = attn_w.shape[2]
    local_hidden = mlp_w.shape[2]
    head_count = local_width // HD
    row_block = min(512, SEQ)
    total_tokens = row_count * tensor_size * dp_size
    gathered_attn, gathered_mlp = (
        lax.all_gather(attn_w.astype(jnp.bfloat16), "dp", axis=1, tiled=True),
        lax.all_gather(mlp_w.astype(jnp.bfloat16), "dp", axis=1, tiled=True),
    )
    hidden_bias = vectors[8:].reshape(-1)
    query_bias = lax.dynamic_slice_in_dim(vectors[2], tensor_index * local_width, local_width)
    value_bias = lax.dynamic_slice_in_dim(vectors[3], tensor_index * local_width, local_width)
    x_rows = tokens.astype(jnp.float32)
    normed, pull_first = jax.vjp(norm_rows, x_rows, vectors[0], vectors[1])
    all_normed = lax.all_gather(normed.astype(jnp.bfloat16), "tensor", axis=0, tiled=True)
    seq_count = all_normed.shape[0] // SEQ
    projected = jnp.einsum(
        "td,mdc->mtc", all_normed, gathered_attn[:3], preferred_element_type=jnp.float32
    )
    query = (projected[0] + query_bias).astype(jnp.bfloat16)
    key_rows = projected[1].astype(jnp.bfloat16)
    value_rows = (projected[2] + value_bias).astype(jnp.bfloat16)
    slopes = head_slopes(tensor_index * head_count, head_count)
    seq_shape = (seq_count, SEQ, head_count, HD)
    seq_segs = segments.reshape(seq_count, SEQ)

    def forward_seq(pieces):
        return attend_forward(pieces[0], pieces[1], pieces[2], pieces[3], slopes, row_block)

    mixed, log_sums = lax.map(
        forward_seq,
        (
            query.reshape(seq_shape),
            key_rows.reshape(seq_shape),
            value_rows.reshape(seq_shape),
            seq_segs,
        ),
    )
    mixed = mixed.reshape(-1, local_width)
    w_out = gathered_attn[3]
    middle = (
        x_rows
        + lax.psum_scatter(
            contract_last(mixed, w_out).astype(jnp.bfloat16),
            "tensor",
            scatter_dimension=0,
            tiled=True,
        ).astype(jnp.float32)
        + vectors[4]
    )
    hidden_normed, pull_second = jax.vjp(norm_rows, middle, vectors[5], vectors[6])
    hidden_low = hidden_normed.astype(jnp.bfloat16)
    grad_rows = cotangent.astype(jnp.float32)
    all_hidden = lax.all_gather(hidden_low, "tensor", axis=0, tiled=True)
    w_up = gathered_mlp[0]
    w_down = gathered_mlp[1]
    bias_local = lax.dynamic_slice_in_dim(hidden_bias, tensor_index * local_hidden, local_hidden)
    hidden_pre = jnp.dot(all_hidden, w_up, preferred_element_type=jnp.float32) + bias_local
    act_float, gelu_pull = jax.vjp(gelu_tanh, hidden_pre)
    hidden_act = act_float.astype(jnp.bfloat16)
    output = (
        middle
        + lax.psum_scatter(
            contract_last(hidden_act, w_down).astype(jnp.bfloat16),
            "tensor",
            scatter_dimension=0,
            tiled=True,
        ).astype(jnp.float32)
        + vectors[7]
    )
    all_grad = lax.all_gather(grad_rows.astype(jnp.bfloat16), "tensor", axis=0, tiled=True)
    grad_down = contract_first(all_grad, hidden_act)
    grad_act = jnp.dot(all_grad, w_down, preferred_element_type=jnp.float32)
    grad_pre = gelu_pull(grad_act)[0].astype(jnp.bfloat16)
    grad_up = contract_first(all_hidden, grad_pre)
    bias_part = jnp.sum(grad_pre, axis=0, dtype=jnp.float32)
    hidden_grad = lax.dynamic_update_slice_in_dim(
        jnp.zeros(hidden_bias.shape, jnp.float32), bias_part, tensor_index * local_hidden, 0
    )
    grad_hidden_in = lax.psum_scatter(
        contract_last(grad_pre, w_up).astype(jnp.bfloat16),
        "tensor",
        scatter_dimension=0,
        tiled=True,
    ).astype(jnp.float32)
    mlp_grads = jnp.stack([grad_up, grad_down])
    second_grads = pull_second(grad_hidden_in)
    grad_middle = grad_rows + second_grads[0]
    all_grad_mid = lax.all_gather(grad_middle.astype(jnp.bfloat16), "tensor", axis=0, tiled=True)
    grad_out_w = contract_first(all_grad_mid, mixed)
    grad_mixed = jnp.dot(all_grad_mid, w_out, preferred_element_type=jnp.float32).astype(
        jnp.bfloat16
    )

    def backward_seq(pieces):
        return attend_backward(
            pieces[0], pieces[1], pieces[2], pieces[3], pieces[4], pieces[5], slopes, row_block
        )

    grad_query, grad_keys, grad_values = lax.map(
        backward_seq,
        (
            query.reshape(seq_shape),
            key_rows.reshape(seq_shape),
            value_rows.reshape(seq_shape),
            seq_segs,
            log_sums,
            grad_mixed.reshape(seq_shape),
        ),
    )
    grad_qkv = (
        jnp.stack([grad_query, grad_keys, grad_values])
        .reshape(3, -1, local_width)
        .astype(jnp.bfloat16)
    )
    grad_proj_w = jnp.einsum(
        "td,mtc->mdc", all_normed, grad_qkv, preferred_element_type=jnp.float32
    )
    bias_sums = jnp.sum(grad_qkv, axis=1, dtype=jnp.float32)
    grad_normed = lax.psum_scatter(
        jnp.einsum(
            "mtc,mdc->td", grad_qkv, gathered_attn[:3], preferred_element_type=jnp.float32
        ).astype(jnp.bfloat16),
        "tensor",
        scatter_dimension=0,
        tiled=True,
    ).astype(jnp.float32)
    first_grads = pull_first(grad_normed)
    grad_tokens = grad_middle + first_grads[0]

    def placed(piece, full_size, offset):
        return lax.dynamic_update_slice_in_dim(
            jnp.zeros((full_size,), jnp.float32), piece, offset, 0
        )

    width_offset = tensor_index * local_width
    vector_rows = jnp.stack(
        [
            first_grads[1],
            first_grads[2],
            placed(bias_sums[0], model_width, width_offset),
            placed(bias_sums[2], model_width, width_offset),
            jnp.sum(grad_middle, axis=0),
            second_grads[1],
            second_grads[2],
            jnp.sum(grad_rows, axis=0),
        ]
    )
    vector_local = jnp.concatenate([vector_rows, hidden_grad.reshape(4, model_width)], axis=0)
    attn_grads = jnp.concatenate([grad_proj_w, grad_out_w[None]], axis=0)
    attn_sum, mlp_sum = (
        lax.psum_scatter(
            attn_grads.astype(jnp.bfloat16), "dp", scatter_dimension=1, tiled=True
        ).astype(jnp.float32),
        lax.psum_scatter(
            mlp_grads.astype(jnp.bfloat16), "dp", scatter_dimension=1, tiled=True
        ).astype(jnp.float32),
    )
    attn_mom_new = 0.5 * attn_mom + attn_sum
    mlp_mom_new = 0.5 * mlp_mom + mlp_sum
    attn_round = attn_mom_new.astype(jnp.bfloat16)
    mlp_round = mlp_mom_new.astype(jnp.bfloat16)
    attn_float = attn_round.astype(jnp.float32)
    mlp_float = mlp_round.astype(jnp.float32)
    norm_parts = jnp.concatenate(
        [jnp.sum(attn_float * attn_float, axis=(1, 2)), jnp.sum(mlp_float * mlp_float, axis=(1, 2))]
    )
    vector_grads, norm_sums = lax.psum((vector_local, norm_parts), ("dp", "tensor"))
    frob_norms = jnp.sqrt(norm_sums)
    owners = [order * dp_size // 6 for order in range(6)]
    owned_norm = jnp.zeros((), jnp.float32)
    for order in range(6):
        owned_norm = owned_norm + jnp.where(dp_index == owners[order], frob_norms[order], 0.0)
    block_rows = attn_w.shape[1]
    slice_rows = model_width // tensor_size
    full_cols = local_hidden * tensor_size
    rows_attn, rows_mlp = (
        lax.all_gather(attn_round, "tensor", axis=2, tiled=True),
        lax.all_gather(mlp_round, "tensor", axis=2, tiled=True),
    )
    padded_attn = jnp.pad(rows_attn, ((0, 0), (0, 0), (0, full_cols - model_width)))
    all_rows = jnp.concatenate([padded_attn, rows_mlp], axis=0)
    outgoing = jnp.zeros((dp_size, block_rows, full_cols), jnp.bfloat16)
    for order in range(6):
        outgoing = outgoing.at[owners[order]].set(all_rows[order])
    incoming = lax.all_to_all(outgoing, "dp", split_axis=0, concat_axis=0, tiled=True)
    owned_whole = incoming.reshape(model_width, full_cols)
    mine = lax.dynamic_slice_in_dim(owned_whole, tensor_index * slice_rows, slice_rows, 0)
    attn_col = tensor_index * local_width
    row_iterate = (mine.astype(jnp.float32) / (owned_norm + 1e-06)).astype(jnp.bfloat16)
    result = newton_rows(row_iterate)
    returned = lax.all_to_all(
        result.reshape(dp_size, block_rows, full_cols),
        "dp",
        split_axis=0,
        concat_axis=0,
        tiled=True,
    )
    attn_blocks = []
    for order in range(4):
        piece = lax.dynamic_slice_in_dim(returned[owners[order]], attn_col, local_width, 1)
        attn_blocks.append(attn_w[order] - piece.astype(jnp.float32))
    mlp_blocks = []
    for order in range(2):
        piece = lax.dynamic_slice_in_dim(
            returned[owners[4 + order]], tensor_index * local_hidden, local_hidden, 1
        )
        mlp_blocks.append(mlp_w[order] - math.sqrt(FF / D) * piece.astype(jnp.float32))
    attn_new = jnp.stack(attn_blocks)
    mlp_new = jnp.stack(mlp_blocks)
    vector_mom_new = 0.5 * vector_mom + vector_grads
    vector_new = vectors - 0.1 / math.sqrt(total_tokens) * vector_mom_new
    return (
        output.astype(jnp.bfloat16),
        grad_tokens,
        attn_mom_new,
        attn_new,
        mlp_mom_new,
        mlp_new,
        vector_mom_new,
        vector_new,
    )


def solution(mesh):
    in_specs = (
        P(("dp", "tensor"), None),
        P(("dp", "tensor"), None),
        P("dp"),
        P(None, "dp", "tensor"),
        P(None, "dp", "tensor"),
        P(),
        P(None, "dp", "tensor"),
        P(None, "dp", "tensor"),
        P(),
    )
    out_specs = (
        P(("dp", "tensor"), None),
        P(("dp", "tensor"), None),
        P(None, "dp", "tensor"),
        P(None, "dp", "tensor"),
        P(None, "dp", "tensor"),
        P(None, "dp", "tensor"),
        P(),
        P(),
    )
    return jax.shard_map(
        on_device, mesh=mesh, in_specs=in_specs, out_specs=out_specs, check_vma=False
    )
```

profile of v0, /device:TPU:0, one launch (start us, length us, event | category | flops | bytes accessed | tf_op | source)
XLA Modules:
  0.0 2540.8 jit_solution(13351415526446475659)
XLA Ops:
  41.1 82.9 %all-gather.20.cloned.1.call-done = bf16[2048,1024]{1,0:T(8,128)(2,1)} async-done(((bf16[512,1024]{1,0:T(8,128)(2,1)}), bf16[2048,1024]{1,0:T(8,128)(2,1)}) %all-gather.20.cloned.1.call-update) | async-done | bytes 4194320 | tf_op jit(solution)/shard_map/all_gather | solution.py:171
  149.7 65.2 %while.64 = (s32[]{:T(128)}, bf16[2,1024,256]{2,1,0:T(8,128)(2,1)S(1)}, f32[2,2,4,512]{3,2,1,0:T(4,128)S(1)}, bf16[2,1024,4,64]{1,3,2,0:T(8,128)(2,1)}, s32[2,10...) while((s32[]{:T(128)}, ...), condition=%wide.region_7.8_spmd.clone, body=%wide.region_2.7_spmd.clone.sunk | while | flops 578944000 | bytes 43641320 | solution.py:186
  221.8 73.3 %reduce-scatter.11.cloned.1.call-done = bf16[512,1024]{1,0:T(8,128)(2,1)} async-done(((bf16[2048,1024]{1,0:T(8,128)(2,1)}), bf16[512,1024]{1,0:T(8,128)(2,1)}) %reduce-scatter.11.cloned.1.call-update) | async-done | bytes 1048592 | tf_op jit(solution)/shard_map/reduce_scatter | solution.py:199
  334.8 82.9 %all-gather.24.cloned.1.call-done = bf16[2048,1024]{1,0:T(8,128)(2,1)} async-done(((bf16[512,1024]{1,0:T(8,128)(2,1)}), bf16[2048,1024]{1,0:T(8,128)(2,1)}) %all-gather.24.cloned.1.call-update) | async-done | bytes 4194320 | tf_op jit(solution)/shard_map/all_gather | solution.py:210
  428.5 70.1 %all-gather.28.cloned.1.call-done = bf16[2048,1024]{1,0:T(8,128)(2,1)} async-done(((bf16[512,1024]{1,0:T(8,128)(2,1)}), bf16[2048,1024]{1,0:T(8,128)(2,1)}) %all-gather.28.cloned.1.call-update) | async-done | bytes 4194320 | tf_op jit(solution)/shard_map/all_gather | solution.py:227
  533.9 63.2 %reduce-scatter.15.cloned.1.call-done = bf16[512,1024]{1,0:T(8,128)(2,1)} async-done(((bf16[2048,1024]{1,0:T(8,128)(2,1)}), bf16[512,1024]{1,0:T(8,128)(2,1)}) %reduce-scatter.15.cloned.1.call-update) | async-done | bytes 1048592 | tf_op jit(solution)/shard_map/reduce_scatter | solution.py:236
  603.1 73.6 %reduce-scatter.13.cloned.1.call-done = bf16[512,1024]{1,0:T(8,128)(2,1)} async-done(((bf16[2048,1024]{1,0:T(8,128)(2,1)}), bf16[512,1024]{1,0:T(8,128)(2,1)}) %reduce-scatter.13.cloned.1.call-update) | async-done | bytes 1048592 | tf_op jit(solution)/shard_map/reduce_scatter | solution.py:219
  683.4 81.4 %all-gather.30.cloned.1.call-done = bf16[2048,1024]{1,0:T(8,128)(2,1)} async-done(((bf16[512,1024]{1,0:T(8,128)(2,1)}), bf16[2048,1024]{1,0:T(8,128)(2,1)}) %all-gather.30.cloned.1.call-update) | async-done | bytes 4194320 | tf_op jit(solution)/shard_map/all_gather | solution.py:245
  771.7 129.1 %while.66 = (s32[]{:T(128)}, bf16[2,1024,256]{1,2,0:T(8,128)(2,1)}, bf16[2,1024,256]{1,2,0:T(8,128)(2,1)}, bf16[2,1024,256]{1,2,0:T(8,128)(2,1)}, f32[2,2,4,512]...) while((s32[]{:T(128)}, bf16[2,1024,256]{1,2,0:T(8,128)(2,1)}, ...), condition=%wide.region_19.20_spmd.clone, body=%wide.region_15.19_spmd.clone.sunk | while | flops 1371012096 | bytes 86869576 | solution.py:256
  776.2 56.1 %while.68 = (s32[]{:T(128)}, f32[1024,4,64]{0,2,1:T(8,128)S(1)}, f32[1024,4,64]{0,2,1:T(8,128)S(1)}, bf16[2,512,4,64]{1,0,3,2:T(2,128)(2,1)}, s32[2]{0:T(128)S(1...) while((s32[]{:T(128)}, f32[1024,4,64]{0,2,1:T(8,128)S(1)}, ...), condition=%wide.region_18.18_spmd.clone, body=%wide.region_16.17_spmd.clone.sunk | while | flops 1371012096 | bytes 76342528 | solution.py:122
  840.7 56.1 %while.68 = (s32[]{:T(128)}, f32[1024,4,64]{0,2,1:T(8,128)S(1)}, f32[1024,4,64]{0,2,1:T(8,128)S(1)}, bf16[2,512,4,64]{1,0,3,2:T(2,128)(2,1)}, s32[2]{0:T(128)S(1...) while((s32[]{:T(128)}, f32[1024,4,64]{0,2,1:T(8,128)S(1)}, ...), condition=%wide.region_18.18_spmd.clone, body=%wide.region_16.17_spmd.clone.sunk | while | flops 1371012096 | bytes 76342528 | solution.py:122
  962.9 51.5 %reduce-scatter.21.cloned.1.call-done = bf16[128,2048]{1,0:T(8,128)(2,1)} async-done(((bf16[1024,2048]{1,0:T(8,128)(2,1)}), bf16[128,2048]{1,0:T(8,128)(2,1)}) %reduce-scatter.21.cloned.1.call-update) | async-done | bytes 524304
  1104.4 65.4 %reduce-scatter.17.cloned.1.call-done = bf16[512,1024]{1,0:T(8,128)(2,1)} async-done(((bf16[2048,1024]{1,0:T(8,128)(2,1)}), bf16[512,1024]{1,0:T(8,128)(2,1)}) %reduce-scatter.17.cloned.1.call-update) | async-done | bytes 1048592 | tf_op jit(solution)/shard_map/reduce_scatter | solution.py:276
  1174.3 53.5 %all-reduce.2 = (f32[6]{0:T(128)S(1)}, f32[12,1024]{1,0:T(8,128)S(1)}) all-reduce(f32[6]{0:T(128)S(1)} %pad_maximum_fusion.5, f32[12,1024]{1,0:T(8,128)S(1)} %concatenate.26), channel_id=1, replica_groups=mesh['dp'=8,'tensor'=4] {'dp','tensor'}, use_global_device_ids=true, to_apply=%region_27.28 | all-reduce | flops 12294 | bytes 98352 | tf_op jit(solution)/shard_map/psum | solution.py:324
  1235.9 150.3 %all-gather.36.cloned.1.call-done = bf16[1024,4096]{1,0:T(8,128)(2,1)} async-done(((bf16[256,4096]{1,0:T(8,128)(2,1)}), bf16[1024,4096]{1,0:T(8,128)(2,1)}) %all-gather.36.cloned.1.call-update) | async-done | bytes 8388624 | tf_op jit(solution)/shard_map/all_gather | solution.py:134
  1393.4 44.3 %all-gather.38.cloned.1.call-done = bf16[1024,1024]{1,0:T(8,128)(2,1)} async-done(((bf16[256,1024]{1,0:T(8,128)(2,1)}), bf16[1024,1024]{1,0:T(8,128)(2,1)}) %all-gather.38.cloned.1.call-update) | async-done | bytes 2097168 | tf_op jit(solution)/shard_map/all_gather | solution.py:138
  1446.3 148.4 %all-gather.40.cloned.1.call-done = bf16[1024,4096]{1,0:T(8,128)(2,1)} async-done(((bf16[256,4096]{1,0:T(8,128)(2,1)}), bf16[1024,4096]{1,0:T(8,128)(2,1)}) %all-gather.40.cloned.1.call-update) | async-done | bytes 8388624 | tf_op jit(solution)/shard_map/all_gather | solution.py:134
  1655.4 148.0 %all-gather.44.cloned.1.call-done = bf16[1024,4096]{1,0:T(8,128)(2,1)} async-done(((bf16[256,4096]{1,0:T(8,128)(2,1)}), bf16[1024,4096]{1,0:T(8,128)(2,1)}) %all-gather.44.cloned.1.call-update) | async-done | bytes 8388624 | tf_op jit(solution)/shard_map/all_gather | solution.py:134
  1810.7 44.3 %all-gather.46.cloned.1.call-done = bf16[1024,1024]{1,0:T(8,128)(2,1)} async-done(((bf16[256,1024]{1,0:T(8,128)(2,1)}), bf16[1024,1024]{1,0:T(8,128)(2,1)}) %all-gather.46.cloned.1.call-update) | async-done | bytes 2097168 | tf_op jit(solution)/shard_map/all_gather | solution.py:138
  1863.7 148.4 %all-gather.48.cloned.1.call-done = bf16[1024,4096]{1,0:T(8,128)(2,1)} async-done(((bf16[256,4096]{1,0:T(8,128)(2,1)}), bf16[1024,4096]{1,0:T(8,128)(2,1)}) %all-gather.48.cloned.1.call-update) | async-done | bytes 8388624 | tf_op jit(solution)/shard_map/all_gather | solution.py:134
  2072.5 148.3 %all-gather.52.cloned.1.call-done = bf16[1024,4096]{1,0:T(8,128)(2,1)} async-done(((bf16[256,4096]{1,0:T(8,128)(2,1)}), bf16[1024,4096]{1,0:T(8,128)(2,1)}) %all-gather.52.cloned.1.call-update) | async-done | bytes 8388624 | tf_op jit(solution)/shard_map/all_gather | solution.py:134
  2228.1 44.3 %all-gather.54.cloned.1.call-done = bf16[1024,1024]{1,0:T(8,128)(2,1)} async-done(((bf16[256,1024]{1,0:T(8,128)(2,1)}), bf16[1024,1024]{1,0:T(8,128)(2,1)}) %all-gather.54.cloned.1.call-update) | async-done | bytes 2097168 | tf_op jit(solution)/shard_map/all_gather | solution.py:138
  2281.0 148.5 %all-gather.56.cloned.1.call-done = bf16[1024,4096]{1,0:T(8,128)(2,1)} async-done(((bf16[256,4096]{1,0:T(8,128)(2,1)}), bf16[1024,4096]{1,0:T(8,128)(2,1)}) %all-gather.56.cloned.1.call-update) | async-done | bytes 8388624 | tf_op jit(solution)/shard_map/all_gather | solution.py:134
  2438.6 90.1 %all-to-all-done.1 = bf16[8,128,4096]{2,1,0:T(8,128)(2,1)} async-done(((bf16[8,128,4096]{2,1,0:T(8,128)(2,1)}), bf16[8,128,4096]{2,1,0:T(8,128)(2,1)}, u32[]{:S(2)}, u32[]{:S(2)}) %all-to-all-start.1) | async-done | bytes 8388640 | tf_op jit(solution)/shard_map/all_to_all | solution.py:348
  (407 shorter events, 749.7 us)
Async XLA Ops:
  9.0 115.0 %all-gather.20.cloned.1.call-start = ((), (), s32[]{:S(2)}) async-start(), calls=%async_computation.8 | async-start | bytes 5242880 | tf_op jit(solution)/shard_map/all_gather | solution.py:171
  17.7 277.4 %reduce-scatter.11.cloned.1.call-start = ((), (), s32[]{:S(2)}) async-start(), calls=%async_computation.10 | async-start | bytes 5242880 | tf_op jit(solution)/shard_map/reduce_scatter | solution.py:199
  219.6 115.2 %all-gather.26.cloned.1.call-start = ((), (), s32[]{:S(2)}) async-start(), calls=%async_computation.12 | async-start | bytes 4718592 | tf_op jit(solution)/shard_map/all_gather | solution.py:164
  221.7 196.0 %all-gather.24.cloned.1.call-start = ((), (), s32[]{:S(2)}) async-start(), calls=%async_computation.11 | async-start | bytes 5242880 | tf_op jit(solution)/shard_map/all_gather | solution.py:210
  300.2 198.3 %all-gather.28.cloned.1.call-start = ((), (), s32[]{:S(2)}) async-start(), calls=%async_computation.14 | async-start | bytes 5242880 | tf_op jit(solution)/shard_map/all_gather | solution.py:227
  300.8 296.3 %reduce-scatter.15.cloned.1.call-start = ((), (), s32[]{:S(2)}) async-start(), calls=%async_computation.15 | async-start | bytes 5242880 | tf_op jit(solution)/shard_map/reduce_scatter | solution.py:236
  521.7 155.0 %reduce-scatter.13.cloned.1.call-start = ((), (), s32[]{:S(2)}) async-start(), calls=%async_computation.13 | async-start | bytes 5242880 | tf_op jit(solution)/shard_map/reduce_scatter | solution.py:219
  533.9 230.9 %all-gather.30.cloned.1.call-start = ((), (), s32[]{:S(2)}) async-start(), calls=%async_computation.16 | async-start | bytes 5242880 | tf_op jit(solution)/shard_map/all_gather | solution.py:245
  683.3 276.4 %reduce-scatter.19.cloned.1.call-start = ((), (), s32[]{:S(2)}) async-start(), calls=%async_computation.31 | async-start | bytes 2359296
  962.9 129.2 %all-gather.34.cloned.1.call-start = ((), (), s32[]{:S(2)}) async-start(), calls=%async_computation.19 | async-start | bytes 2621440 | tf_op jit(solution)/shard_map/all_gather | solution.py:335
  1019.5 150.3 %reduce-scatter.17.cloned.1.call-start = ((), (), s32[]{:S(2)}) async-start(), calls=%async_computation.17 | async-start | bytes 5242880 | tf_op jit(solution)/shard_map/reduce_scatter | solution.py:276
  1096.7 135.7 %all-to-all-start = ((bf16[8,128,4096]{2,1,0:T(8,128)(2,1)}), bf16[8,128,4096]{2,1,0:T(8,128)(2,1)}, u32[]{:S(2)}, u32[]{:S(2)}) async-start(bf16[8,128,4096]{2,1,0:T(8,128)(2,1)} %slice_dynamic-update-slice_fusion), calls=%async_computation.4 | async-start | bytes 16777216 | tf_op jit(solution)/shard_map/all_to_all | solution.py:342
  1102.2 283.9 %all-gather.36.cloned.1.call-start = ((), (), s32[]{:S(2)}) async-start(), calls=%async_computation.20 | async-start | bytes 10485760 | tf_op jit(solution)/shard_map/all_gather | solution.py:134
  1235.8 201.8 %all-gather.38.cloned.1.call-start = ((), (), s32[]{:S(2)}) async-start(), calls=%async_computation.21 | async-start | bytes 2621440 | tf_op jit(solution)/shard_map/all_gather | solution.py:138
  1393.3 201.5 %all-gather.40.cloned.1.call-start = ((), (), s32[]{:S(2)}) async-start(), calls=%async_computation.22 | async-start | bytes 10485760 | tf_op jit(solution)/shard_map/all_gather | solution.py:134
  1446.3 200.0 %all-gather.42.cloned.1.call-start = ((), (), s32[]{:S(2)}) async-start(), calls=%async_computation.23 | async-start | bytes 2621440 | tf_op jit(solution)/shard_map/all_gather | solution.py:138
  1602.0 201.5 %all-gather.44.cloned.1.call-start = ((), (), s32[]{:S(2)}) async-start(), calls=%async_computation.24 | async-start | bytes 10485760 | tf_op jit(solution)/shard_map/all_gather | solution.py:134
  1655.0 200.0 %all-gather.46.cloned.1.call-start = ((), (), s32[]{:S(2)}) async-start(), calls=%async_computation.25 | async-start | bytes 2621440 | tf_op jit(solution)/shard_map/all_gather | solution.py:138
  1810.7 201.5 %all-gather.48.cloned.1.call-start = ((), (), s32[]{:S(2)}) async-start(), calls=%async_computation.26 | async-start | bytes 10485760 | tf_op jit(solution)/shard_map/all_gather | solution.py:134
  1863.6 200.0 %all-gather.50.cloned.1.call-start = ((), (), s32[]{:S(2)}) async-start(), calls=%async_computation.27 | async-start | bytes 2621440 | tf_op jit(solution)/shard_map/all_gather | solution.py:138
  2019.3 201.5 %all-gather.52.cloned.1.call-start = ((), (), s32[]{:S(2)}) async-start(), calls=%async_computation.28 | async-start | bytes 10485760 | tf_op jit(solution)/shard_map/all_gather | solution.py:134
  2072.3 200.0 %all-gather.54.cloned.1.call-start = ((), (), s32[]{:S(2)}) async-start(), calls=%async_computation.29 | async-start | bytes 2621440 | tf_op jit(solution)/shard_map/all_gather | solution.py:138
  2228.0 201.5 %all-gather.56.cloned.1.call-start = ((), (), s32[]{:S(2)}) async-start(), calls=%async_computation.30 | async-start | bytes 10485760 | tf_op jit(solution)/shard_map/all_gather | solution.py:134
  2429.5 99.1 %all-to-all-start.1 = ((bf16[8,128,4096]{2,1,0:T(8,128)(2,1)}), bf16[8,128,4096]{2,1,0:T(8,128)(2,1)}, u32[]{:S(2)}, u32[]{:S(2)}) async-start(bf16[8,128,4096]{2,1,0:T(8,128)(2,1)} %bitcast.228), calls=%async_computation.5 | async-start | bytes 16777216 | tf_op jit(solution)/shard_map/all_to_all | solution.py:348
  (50 other events, 2969.4 us)
Sparse Core Ops, SparseCore 0:
  10.5 30.5 all-gather.21
  43.3 80.7 all-gather.19
  219.7 75.2 reduce-scatter.10
  297.6 37.2 all-gather.25
  336.9 80.7 all-gather.23
  419.2 79.2 all-gather.27
  521.8 75.2 reduce-scatter.14
  599.4 77.2 reduce-scatter.12
  683.5 81.2 all-gather.29
  919.9 39.7 reduce-scatter.18
  963.1 51.3 reduce-scatter.20
  1047.8 44.2 all-gather.33
  1094.3 75.4 reduce-scatter.16
  1235.9 150.1 all-gather.35
  1393.4 44.1 all-gather.37
  1446.4 148.3 all-gather.39
  1602.1 44.1 all-gather.41
  1655.1 148.3 all-gather.43
  1810.8 44.1 all-gather.45
  1863.8 148.3 all-gather.47
  2019.5 44.1 all-gather.49
  2072.4 148.3 all-gather.51
  2228.1 44.1 all-gather.53
  2281.1 148.3 all-gather.55
  (1 shorter events, 30.1 us)
where the time goes:
time: 2550 us; the launch traced here: 2540 us
  waiting for transfers between devices  1970 us (77%)
  matrix products  245 us (10%)
  local copies, waits for them, and re-layouts  144 us (6%)
  other arithmetic  78 us (3%)
  blocking collectives  53.5 us (2%)
    all_gather x6, waiting for transfers between devices, newton_rows(): whole_iterate = lax.all_gather(row_iterate, 'tensor', axis=0, tiled=True)  892 us
    all_gather x5, waiting for transfers between devices, newton_rows(): whole_square = lax.all_gather(square_rows, 'tensor', axis=0, tiled=True)  221 us
    all_to_all x1, waiting for transfers between devices, on_device(): lax.all_to_all(result.reshape(dp_size, block_rows, full_cols), 'dp', spli...  90.1 us
    all_gather x1, waiting for transfers between devices, on_device(): lax.all_gather(normed.astype(jnp.bfloat16), 'tensor', axis=0, tiled=True)  82.9 us
    all_gather x1, waiting for transfers between devices, on_device(): all_hidden = lax.all_gather(hidden_low, 'tensor', axis=0, tiled=True)  82.9 us
    all_gather x1, waiting for transfers between devices, on_device(): lax.all_gather(grad_middle.astype(jnp.bfloat16), 'tensor', axis=0, tiled=...  81.4 us
    reduce_scatter x1, waiting for transfers between devices, on_device(): lax.psum_scatter(contract_last(hidden_act, w_down).astype(jnp.bfloat16),...  73.6 us
    reduce_scatter x1, waiting for transfers between devices, on_device(): lax.psum_scatter(contract_last(mixed, w_out).astype(jnp.bfloat16), 'tenso...  73.3 us
  transfers between devices with their start and end apart: 27, of which 26 were waited for; matrix products, arithmetic and copies ran while one was open for 4% of the time, Pallas kernels for 0%

commit v1 on v0

--- a/solution.py
+++ b/solution.py
@@ -1,8 +1,11 @@
+import functools
 import math
 
 import jax
 import jax.numpy as jnp
 from jax import lax
+from jax.experimental import pallas as pl
+from jax.experimental.pallas import tpu as pltpu
 from jax.sharding import PartitionSpec as P
 
 D = 1024
@@ -11,6 +14,7 @@
 FF = 4096
 SEQ = 1024
 NS_STEPS = 5
+MESH = pl.DeviceIdType.MESH
 
 
 coeff_a = 3.4445
@@ -378,6 +382,1043 @@
     )
 
 
+CORES = 2
+
+
+class Place:
+    def __init__(self):
+        self.dp = lax.axis_index("dp")
+        self.tensor = lax.axis_index("tensor")
+        self.core = lax.rem(self.dp, 2)
+        self.chip = self.dp // 2
+        self.x = lax.rem(self.chip, 2)
+        self.y = self.chip // 2
+        self.twin = (self.dp + 1 - 2 * self.core, self.tensor)
+        self.across_x = (self.dp + 2 - 4 * self.x, self.tensor)
+        self.across_y = (self.dp + 4 - 8 * self.y, self.tensor)
+        self.right = (self.dp, self.tensor + 1)
+        self.left = (self.dp, self.tensor - 1)
+
+
+def greet(place, line):
+    barrier = pltpu.get_barrier_semaphore()
+
+    def signal(device):
+        pl.semaphore_signal(barrier, inc=1, device_id=device, device_id_type=MESH)
+
+    signal(place.twin)
+    signal(place.across_x)
+    signal(place.across_y)
+
+    for other in range(line):
+
+        @pl.when(place.tensor != other)
+        def _():
+            signal((place.dp, other))
+
+    pl.semaphore_wait(barrier, 3 + line - 1)
+
+
+def columns(start, size):
+    return pl.ds(pl.multiple_of(start, 128), size)
+
+
+def gather_kernel(line, attn_ref, mlp_ref, qkv_ref, out_ref, up_ref, down_ref, own_sem, send_sem, recv_sem):
+    place = Place()
+    x, y, t = place.x, place.y, place.tensor
+    narrow = attn_ref.shape[2] // 2
+    wide = mlp_ref.shape[2] // 4
+
+    def attn_source(lo, hi):
+        return lambda core: attn_ref.at[lo:hi, :, columns(core * narrow, narrow)]
+
+    def mlp_source(index, part):
+        return lambda core: mlp_ref.at[index : index + 1, :, columns((2 * core + part) * wide, wide)]
+
+    groups = [
+        (qkv_ref, narrow, attn_source(0, 3)),
+        (out_ref, narrow, attn_source(3, 4)),
+        (up_ref.at[0:1], wide, mlp_source(0, 0)),
+        (up_ref.at[1:2], wide, mlp_source(0, 1)),
+        (down_ref.at[0:1], wide, mlp_source(1, 0)),
+        (down_ref.at[1:2], wide, mlp_source(1, 1)),
+    ]
+    greet(place, line)
+
+    def copy(group, slot, source, target, device):
+        return pltpu.make_async_remote_copy(
+            src_ref=source,
+            dst_ref=target,
+            send_sem=send_sem.at[group, slot],
+            recv_sem=recv_sem.at[group, slot],
+            device_id=device,
+            device_id_type=MESH,
+        )
+
+    def same(group, slot, region, device):
+        return copy(group, slot, region, region, device)
+
+    def chunk(group, index):
+        ref, width, _ = groups[group]
+        return ref.at[:, y, x, :, :, columns(index * width, width)]
+
+    def corner(group, ys, xs, half):
+        return groups[group][0].at[:, ys, xs, half]
+
+    def entry(group, half):
+        ref, width, _ = groups[group]
+        return ref.at[:, y, x, half, :, columns(t * width, width)]
+
+    both = pl.ds(0, 2)
+    steps = range(1, line)
+    to_right, to_left, half_x, half_y, rest_y, rest_x = 1, line, 2 * line - 1, 2 * line, 2 * line + 1, 2 * line + 2
+
+    def own(group):
+        return pltpu.make_async_copy(
+            groups[group][2](place.core), entry(group, place.core), own_sem.at[group]
+        )
+
+    def first(group):
+        target = entry(group, place.core)
+        return copy(group, 0, groups[group][2](1 - place.core), target, place.twin)
+
+    def start_line(group):
+        own(group).wait()
+        same(group, 0, entry(group, 1 - place.core), place.twin).wait_recv()
+
+        @pl.when(t < line - 1)
+        def _():
+            same(group, to_right, chunk(group, t), place.right).start()
+
+        @pl.when(t > 0)
+        def _():
+            same(group, to_left, chunk(group, t), place.left).start()
+
+    def run_line(group):
+        for step in steps:
+
+            @pl.when(t >= step)
+            def _():
+                same(group, to_right + step - 1, chunk(group, t - step), place.left).wait_recv()
+                if step < line - 1:
+
+                    @pl.when(t < line - 1)
+                    def _():
+                        same(group, to_right + step, chunk(group, t - step), place.right).start()
+
+            @pl.when(t + step <= line - 1)
+            def _():
+                same(group, to_left + step - 1, chunk(group, t + step), place.right).wait_recv()
+                if step < line - 1:
+
+                    @pl.when(t > 0)
+                    def _():
+                        same(group, to_left + step, chunk(group, t + step), place.left).start()
+
+    def start_plane(group):
+        same(group, half_x, corner(group, y, x, 0), place.across_x).start()
+        same(group, half_y, corner(group, y, x, 1), place.across_y).start()
+
+    def run_plane(group):
+        same(group, half_x, corner(group, y, 1 - x, 0), place.across_x).wait_recv()
+        same(group, rest_y, corner(group, y, both, 0), place.across_y).start()
+        same(group, half_y, corner(group, 1 - y, x, 1), place.across_y).wait_recv()
+        same(group, rest_x, corner(group, both, x, 1), place.across_x).start()
+
+    def end_plane(group):
+        same(group, rest_y, corner(group, 1 - y, both, 0), place.across_y).wait_recv()
+        same(group, rest_x, corner(group, both, 1 - x, 1), place.across_x).wait_recv()
+
+    def wait_sends(group):
+        first(group).wait_send()
+        for step in steps:
+
+            @pl.when((t - step + 1 >= 0) & (t < line - 1))
+            def _():
+                same(group, to_right + step - 1, chunk(group, t - step + 1), place.right).wait_send()
+
+            @pl.when((t + step - 1 <= line - 1) & (t > 0))
+            def _():
+                same(group, to_left + step - 1, chunk(group, t + step - 1), place.left).wait_send()
+
+        same(group, half_x, corner(group, y, x, 0), place.across_x).wait_send()
+        same(group, half_y, corner(group, y, x, 1), place.across_y).wait_send()
+        same(group, rest_y, corner(group, y, both, 0), place.across_y).wait_send()
+        same(group, rest_x, corner(group, both, x, 1), place.across_x).wait_send()
+
+    count = len(groups)
+    for group in range(count):
+        own(group).start()
+        first(group).start()
+    for group in range(count):
+        start_line(group)
+    for group in range(count + 1):
+        if group < count:
+            run_line(group)
+            start_plane(group)
+        if group >= 1:
+            run_plane(group - 1)
+    for group in range(count):
+        end_plane(group)
+    for group in range(count):
+        wait_sends(group)
+
+
+def gather_weights(attn_low, mlp_low, line):
+    narrow = attn_low.shape[2] // 2 * line
+    wide = mlp_low.shape[2] // 4 * line
+    rows = attn_low.shape[1]
+    shapes = [(3, narrow), (1, narrow), (2, wide), (2, wide)]
+    slots = 2 * line + 3
+    gathered = pl.pallas_call(
+        functools.partial(gather_kernel, line),
+        out_shape=[
+            jax.ShapeDtypeStruct((count, 2, 2, 2, rows, width), jnp.bfloat16) for count, width in shapes
+        ],
+        in_specs=[pl.BlockSpec(memory_space=pl.ANY)] * 2,
+        out_specs=[pl.BlockSpec(memory_space=pl.ANY)] * 4,
+        scratch_shapes=[
+            pltpu.SemaphoreType.DMA((6,)),
+            pltpu.SemaphoreType.DMA((6, slots)),
+            pltpu.SemaphoreType.DMA((6, slots)),
+        ],
+        compiler_params=pltpu.CompilerParams(collective_id=1, has_side_effects=True),
+        name="gather_weights",
+    )(attn_low, mlp_low)
+    return [whole.reshape(whole.shape[0], 8 * rows, -1) for whole in gathered]
+
+
+def add_blocks(target, sources):
+    count, rows = target.shape[0], target.shape[1]
+    per = rows // 32
+
+    def body(step, carry):
+        at = (step // per, pl.ds(pl.multiple_of(lax.rem(step, per) * 32, 32), 32))
+        total = sources[0][at].astype(jnp.float32)
+        for source in sources[1:]:
+            total = total + source[at].astype(jnp.float32)
+        target[at] = total.astype(target.dtype)
+        return carry
+
+    lax.fori_loop(0, count * per, body, 0)
+
+
+def sum_kernel(line, down_ref, up_ref, out_ref, qkv_ref, vec_ref, attn_home, mlp_home, vec_out, *scratch):
+    place = Place()
+    x, y, t, core = place.x, place.y, place.tensor, place.core
+    group_count = 6
+    names = ("own_a", "own_b", "got_a", "got_b", "last_a", "last_b", "plane", "from_left", "from_right", "done")
+    buffers = []
+    for group in range(group_count):
+        start = group * len(names)
+        buffers.append(dict(zip(names, scratch[start : start + len(names)])))
+    own_sem, send_sem, recv_sem, vec_sum, vec_got, vec_line, vec_sem = scratch[group_count * len(names) :]
+    narrow = attn_home.shape[2] // 2
+    wide = mlp_home.shape[2] // 4
+
+    def attn_target(lo, hi):
+        return lambda: attn_home.at[lo:hi, :, columns(core * narrow, narrow)]
+
+    def mlp_target(index, part):
+        return lambda: mlp_home.at[index : index + 1, :, columns((2 * core + part) * wide, wide)]
+
+    groups = [
+        (down_ref.at[0:1], wide, mlp_target(1, 0)),
+        (down_ref.at[1:2], wide, mlp_target(1, 1)),
+        (up_ref.at[0:1], wide, mlp_target(0, 0)),
+        (up_ref.at[1:2], wide, mlp_target(0, 1)),
+        (out_ref, narrow, attn_target(3, 4)),
+        (qkv_ref, narrow, attn_target(0, 3)),
+    ]
+    greet(place, line)
+    both = pl.ds(0, 2)
+    one_a, one_b, two_a, two_b, home_slot = 0, 1, 2, 3, 4
+    rightward, leftward = 5, 5 + line
+
+    def copy(group, slot, source, target, device):
+        return pltpu.make_async_remote_copy(
+            src_ref=source,
+            dst_ref=target,
+            send_sem=send_sem.at[group, slot],
+            recv_sem=recv_sem.at[group, slot],
+            device_id=device,
+            device_id_type=MESH,
+        )
+
+    def loads(group):
+        ref, held = groups[group][0], buffers[group]
+        return (
+            pltpu.make_async_copy(ref.at[:, y, both, 0], held["own_a"], own_sem.at[group, 0]),
+            pltpu.make_async_copy(ref.at[:, both, x, 1], held["own_b"], own_sem.at[group, 1]),
+        )
+
+    def first_copies(group):
+        ref, held = groups[group][0], buffers[group]
+        return (
+            copy(group, one_a, ref.at[:, 1 - y, both, 0], held["got_a"], place.across_y),
+            copy(group, one_b, ref.at[:, both, 1 - x, 1], held["got_b"], place.across_x),
+        )
+
+    def second_copies(group):
+        held = buffers[group]
+        return (
+            copy(group, two_a, held["own_a"].at[:, 1 - x], held["last_a"], place.across_x),
+            copy(group, two_b, held["own_b"].at[:, 1 - y], held["last_b"], place.across_y),
+        )
+
+    def start(group):
+        for each in first_copies(group) + loads(group):
+            each.start()
+
+    def plane_one(group):
+        held = buffers[group]
+        sends = second_copies(group)
+        for part, other, mine in (("a", 1 - x, x), ("b", 1 - y, y)):
+            index = 0 if part == "a" else 1
+            loads(group)[index].wait()
+            first_copies(group)[index].wait_recv()
+            own, got = held["own_" + part], held["got_" + part]
+            add_blocks(own.at[:, other], (own.at[:, other], got.at[:, other]))
+            sends[index].start()
+            add_blocks(own.at[:, mine], (own.at[:, mine], got.at[:, mine]))
+
+    def plane_two(group):
+        held = buffers[group]
+        for index, (part, mine) in enumerate((("a", x), ("b", y))):
+            second_copies(group)[index].wait_recv()
+            add_blocks(held["plane"].at[:, index], (held["own_" + part].at[:, mine], held["last_" + part]))
+
+    def piece(group, name, index, half):
+        width = groups[group][1]
+        return buffers[group][name].at[:, half, :, index * width : (index + 1) * width]
+
+    def hop(group, index, right):
+        width = groups[group][1]
+        cut = slice(index * width, (index + 1) * width)
+        held = buffers[group]
+        slot = (rightward if right else leftward) + index
+        target = held["from_left" if right else "from_right"]
+        return copy(
+            group, slot, held["plane"].at[:, :, :, cut], target.at[:, :, :, cut], place.right if right else place.left
+        )
+
+    def run_line(group):
+        for step in range(line - 1):
+            for right in (True, False):
+                index = line - 1 - step if right else step
+                name = "from_left" if right else "from_right"
+
+                @pl.when((t < index) if right else (t > index))
+                def _():
+                    @pl.when((t > 0) if right else (t < line - 1))
+                    def _():
+                        hop(group, index, right).wait_recv()
+                        for half in range(2):
+                            plane = piece(group, "plane", index, half)
+                            add_blocks(plane, (plane, piece(group, name, index, half)))
+
+                    hop(group, index, right).start()
+
+    def end_line(group):
+        held = buffers[group]
+        for index in range(line):
+
+            @pl.when(t == index)
+            def _():
+                names = ["plane"]
+                if index > 0:
+                    hop(group, index, True).wait_recv()
+                    names.append("from_left")
+                if index < line - 1:
+                    hop(group, index, False).wait_recv()
+                    names.append("from_right")
+                for half in range(2):
+                    add_blocks(held["done"].at[:, half], [piece(group, name, index, half) for name in names])
+
+        for each in homes(group):
+            each.start()
+
+    def homes(group):
+        done, target = buffers[group]["done"], groups[group][2]
+        return (
+            pltpu.make_async_copy(done.at[:, core], target(), own_sem.at[group, 2]),
+            copy(group, home_slot, done.at[:, 1 - core], target(), place.twin),
+        )
+
+    def finish(group):
+        local, remote = homes(group)
+        local.wait()
+        remote.wait()
+        for each in first_copies(group) + second_copies(group):
+            each.wait_send()
+        for step in range(line - 1):
+            for right in (True, False):
+                index = line - 1 - step if right else step
+
+                @pl.when((t < index) if right else (t > index))
+                def _():
+                    hop(group, index, right).wait_send()
+
+    partners = (place.twin, place.across_x, place.across_y)
+
+    def vec_copy(stage):
+        return pltpu.make_async_remote_copy(
+            src_ref=vec_sum.at[stage],
+            dst_ref=vec_got.at[stage],
+            send_sem=vec_sem.at[0, stage],
+            recv_sem=vec_sem.at[1, stage],
+            device_id=partners[stage],
+            device_id_type=MESH,
+        )
+
+    def vec_hop(other, source):
+        return pltpu.make_async_remote_copy(
+            src_ref=vec_sum.at[3],
+            dst_ref=vec_line.at[source],
+            send_sem=vec_sem.at[2, other],
+            recv_sem=vec_sem.at[3, source],
+            device_id=(place.dp, other),
+            device_id_type=MESH,
+        )
+
+    def vec_step(stage):
+        if 0 < stage <= 3:
+            vec_copy(stage - 1).wait()
+            vec_sum[stage] = vec_sum[stage - 1] + vec_got[stage - 1]
+        if stage < 3:
+            vec_copy(stage).start()
+        if stage == 3:
+            vec_line[t] = vec_sum[3]
+        for other in range(line):
+
+            @pl.when(t != other)
+            def _():
+                if stage == 3:
+                    vec_hop(other, t).start()
+                if stage == 4:
+                    vec_hop(other, t).wait_send()
+                    vec_hop(t, other).wait_recv()
+
+        if stage == 4:
+            total = vec_line[0]
+            for other in range(1, line):
+                total = total + vec_line[other]
+            vec_out[...] = total
+
+    vec_sum[0] = vec_ref[...]
+    for group in range(group_count):
+        start(group)
+    for group in range(group_count + 2):
+        if group < 5:
+            vec_step(group)
+        if group < group_count:
+            plane_one(group)
+        if 1 <= group <= group_count:
+            plane_two(group - 1)
+            run_line(group - 1)
+        if group >= 2:
+            end_line(group - 2)
+    for group in range(group_count):
+        finish(group)
+
+
+def sum_gradients(down, up, out, qkv, vec, line):
+    rows = qkv.shape[1] // 8
+    narrow, wide = qkv.shape[2], down.shape[2]
+    counts = [(1, wide)] * 4 + [(1, narrow), (3, narrow)]
+    scratch = []
+    for count, width in counts:
+        pair = pltpu.VMEM((count, 2, rows, width), jnp.bfloat16)
+        single = pltpu.VMEM((count, rows, width), jnp.bfloat16)
+        done = pltpu.VMEM((count, 2, rows, width // line), jnp.bfloat16)
+        scratch += [pair] * 4 + [single] * 2 + [pair] * 3 + [done]
+    slots = 5 + 2 * line
+    return pl.pallas_call(
+        functools.partial(sum_kernel, line),
+        out_shape=[
+            jax.ShapeDtypeStruct((4, rows, 2 * narrow // line), jnp.bfloat16),
+            jax.ShapeDtypeStruct((2, rows, 4 * wide // line), jnp.bfloat16),
+            jax.ShapeDtypeStruct(vec.shape, jnp.float32),
+        ],
+        in_specs=[pl.BlockSpec(memory_space=pl.ANY)] * 4 + [pl.BlockSpec(memory_space=pltpu.VMEM)],
+        out_specs=[pl.BlockSpec(memory_space=pl.ANY)] * 2 + [pl.BlockSpec(memory_space=pltpu.VMEM)],
+        scratch_shapes=scratch
+        + [
+            pltpu.SemaphoreType.DMA((6, 3)),
+            pltpu.SemaphoreType.DMA((6, slots)),
+            pltpu.SemaphoreType.DMA((6, slots)),
+            pltpu.VMEM((4,) + vec.shape, jnp.float32),
+            pltpu.VMEM((3,) + vec.shape, jnp.float32),
+            pltpu.VMEM((line,) + vec.shape, jnp.float32),
+            pltpu.SemaphoreType.DMA((4, max(line, 3))),
+        ],
+        compiler_params=pltpu.CompilerParams(
+            collective_id=2, has_side_effects=True, vmem_limit_bytes=48 * 1024 * 1024
+        ),
+        name="sum_gradients",
+    )(*(each.reshape(each.shape[0], 2, 2, 2, rows, each.shape[2]) for each in (down, up, out, qkv)), vec)
+
+
+LOG2E = 1.4426950408889634
+FAR = 1e32
+ROW_BLOCK = 256
+
+
+def fill_distance(seg_rows, seg_cols, distance):
+    def body(step, carry):
+        start = pl.multiple_of(step * 64, 64)
+        shape = (64, distance.shape[1])
+        row = lax.broadcasted_iota(jnp.int32, shape, 0) + start
+        col = lax.broadcasted_iota(jnp.int32, shape, 1)
+        segs = seg_rows[pl.ds(start, 64), :]
+        same = (segs == seg_cols[...]) & (segs > 0) & (col <= row)
+        allowed = same | (col == row)
+        distance[pl.ds(start, 64), :] = jnp.where(allowed, (row - col).astype(jnp.float32), FAR)
+        return carry
+
+    lax.fori_loop(0, distance.shape[0] // 64, body, 0)
+
+
+def head_lanes(dtype):
+    lane = lax.broadcasted_iota(jnp.int32, (1, 2 * HD), 1)
+    first = (lane < HD).astype(jnp.float32)
+    return (first.astype(dtype), (1.0 - first).astype(dtype))
+
+
+def attend_kernel(slopes, seg_rows, seg_cols, qkv, mixed, lse, distance):
+    group = pl.program_id(0)
+    length = qkv.shape[1]
+
+    @pl.when(group == 0)
+    def _():
+        fill_distance(seg_rows, seg_cols, distance)
+
+    masks = head_lanes(jnp.bfloat16)
+    first = head_lanes(jnp.float32)[0] > 0.5
+    factor = LOG2E / math.sqrt(HD)
+    keys_t = qkv[1].T
+    for start in range(0, length, ROW_BLOCK):
+        stop = start + ROW_BLOCK
+        rows = slice(start, stop)
+        parts, sums = [], []
+        for head in range(2):
+            slope = slopes[2 * group + head] * LOG2E
+            scores = jnp.dot(
+                qkv[0, rows, :] * masks[head], keys_t[:, :stop], preferred_element_type=jnp.float32
+            )
+            scores = scores * factor - slope * distance[rows, :stop]
+            top = jnp.max(scores, axis=1, keepdims=True)
+            probs = jnp.exp2(scores - top)
+            total = jnp.sum(probs, axis=1, keepdims=True)
+            out = jnp.dot(probs.astype(jnp.bfloat16), qkv[2, :stop, :], preferred_element_type=jnp.float32)
+            parts.append(out / total)
+            sums.append(top + jnp.log2(total))
+        mixed[rows, :] = jnp.where(first, parts[0], parts[1]).astype(jnp.bfloat16)
+        lse[rows, :] = jnp.where(first, sums[0], sums[1])
+
+
+def attend_back_kernel(slopes, seg_rows, seg_cols, qkv, grad, mixed, lse, out, distance, dk_acc, dv_acc):
+    group = pl.program_id(0)
+    length = qkv.shape[1]
+
+    @pl.when(group == 0)
+    def _():
+        fill_distance(seg_rows, seg_cols, distance)
+
+    masks = head_lanes(jnp.bfloat16)
+    wide_masks = head_lanes(jnp.float32)
+    first = wide_masks[0] > 0.5
+    factor = LOG2E / math.sqrt(HD)
+    shrink = 1.0 / math.sqrt(HD)
+    keys_t = qkv[1].T
+    values_t = qkv[2].T
+    dk_acc[...] = jnp.zeros_like(dk_acc)
+    dv_acc[...] = jnp.zeros_like(dv_acc)
+    for start in range(0, length, ROW_BLOCK):
+        stop = start + ROW_BLOCK
+        rows = slice(start, stop)
+        query, grads = qkv[0, rows, :], grad[rows, :]
+        query_t, grads_t = query.T, grads.T
+        product = grads.astype(jnp.float32) * mixed[rows, :].astype(jnp.float32)
+        parts = []
+        for head in range(2):
+            slope = slopes[2 * group + head] * LOG2E
+            lanes = slice(head * HD, (head + 1) * HD)
+            scores = jnp.dot(query * masks[head], keys_t[:, :stop], preferred_element_type=jnp.float32)
+            log_sum = lse[rows, head * HD : head * HD + 1]
+            probs = jnp.exp2(scores * factor - slope * distance[rows, :stop] - log_sum)
+            grad_probs = jnp.dot(grads * masks[head], values_t[:, :stop], preferred_element_type=jnp.float32)
+            inner = jnp.sum(product * wide_masks[head], axis=1, keepdims=True)
+            grad_scores = (probs * (grad_probs - inner)).astype(jnp.bfloat16)
+            parts.append(jnp.dot(grad_scores, qkv[1, :stop, :], preferred_element_type=jnp.float32))
+            dk_acc[lanes, :stop] += jnp.dot(query_t[lanes, :], grad_scores, preferred_element_type=jnp.float32)
+            dv_acc[lanes, :stop] += jnp.dot(
+                grads_t[lanes, :], probs.astype(jnp.bfloat16), preferred_element_type=jnp.float32
+            )
+        out[0, rows, :] = (jnp.where(first, parts[0], parts[1]) * shrink).astype(jnp.bfloat16)
+    out[1] = (dk_acc[...].T * shrink).astype(jnp.bfloat16)
+    out[2] = dv_acc[...].T.astype(jnp.bfloat16)
+
+
+def attention_specs(length):
+    return [
+        pl.BlockSpec(memory_space=pltpu.SMEM),
+        pl.BlockSpec((length, 1), lambda g: (0, 0)),
+        pl.BlockSpec((1, length), lambda g: (0, 0)),
+        pl.BlockSpec((3, length, 2 * HD), lambda g: (0, 0, g)),
+    ]
+
+
+def attend(slopes, seg_ids, qkv):
+    _, length, width = qkv.shape
+    rows = pl.BlockSpec((length, 2 * HD), lambda g: (0, g))
+    return pl.pallas_call(
+        attend_kernel,
+        grid=(width // (2 * HD),),
+        out_shape=[
+            jax.ShapeDtypeStruct((length, width), jnp.bfloat16),
+            jax.ShapeDtypeStruct((length, width), jnp.float32),
+        ],
+        in_specs=attention_specs(length),
+        out_specs=[rows, rows],
+        scratch_shapes=[pltpu.VMEM((length, length), jnp.float32)],
+        compiler_params=pltpu.CompilerParams(vmem_limit_bytes=48 * 1024 * 1024),
+        name="attend",
+    )(slopes, seg_ids.reshape(-1, 1), seg_ids.reshape(1, -1), qkv)
+
+
+def attend_back(slopes, seg_ids, qkv, grad, mixed, lse):
+    _, length, width = qkv.shape
+    rows = pl.BlockSpec((length, 2 * HD), lambda g: (0, g))
+    return pl.pallas_call(
+        attend_back_kernel,
+        grid=(width // (2 * HD),),
+        out_shape=jax.ShapeDtypeStruct(qkv.shape, jnp.bfloat16),
+        in_specs=attention_specs(length) + [rows] * 3,
+        out_specs=pl.BlockSpec((3, length, 2 * HD), lambda g: (0, 0, g)),
+        scratch_shapes=[
+            pltpu.VMEM((length, length), jnp.float32),
+            pltpu.VMEM((2 * HD, length), jnp.float32),
+            pltpu.VMEM((2 * HD, length), jnp.float32),
+        ],
+        compiler_params=pltpu.CompilerParams(vmem_limit_bytes=48 * 1024 * 1024),
+        name="attend_back",
+    )(slopes, seg_ids.reshape(-1, 1), seg_ids.reshape(1, -1), qkv, grad, mixed, lse)
+
+
+OWNERS = ((0, 0), (3, 0), (1, 3), (2, 3), (0, 1), (3, 2))
+
+
+def newton_kernel(line, attn_ref, mlp_ref, attn_home, mlp_home, thin, full, gram, sent, got, poly, norm_own, norm_got,
+                  home_sem, start_sem, send_sem, back_sem, norm_sem, block_send, block_recv):
+    place = Place()
+    d, t, core = place.dp, place.tensor, place.core
+    me = d * line + t
+    devices = 8 * line
+    rows = attn_ref.shape[1]
+    narrow, wide = attn_ref.shape[2] // 2, mlp_ref.shape[2] // 2
+    barrier = pltpu.get_barrier_semaphore()
+
+    def place_of(index):
+        return (index // line, lax.rem(index, line))
+
+    def meet(step, carry):
+        pl.semaphore_signal(
+            barrier, inc=1, device_id=place_of(lax.rem(me + step, devices)), device_id_type=MESH
+        )
+        return carry
+
+    lax.fori_loop(1, devices, meet, 0)
+    pl.semaphore_wait(barrier, devices - 1)
+
+    jobs = []
+    for order, (chip, z) in enumerate(OWNERS):
+        for half in range(2):
+            jobs.append((order, half, (2 * chip + half) * line + min(z, line - 1)))
+
+    def source(order, half):
+        if order < 4:
+            return attn_ref.at[order, :, half * narrow : (half + 1) * narrow]
+        return mlp_ref.at[order - 4, :, half * wide : (half + 1) * wide]
+
+    def held(order, index):
+        dp, tensor = place_of(index)
+        row = pl.ds(pl.multiple_of(dp * rows, rows), rows)
+        if order < 4:
+            return thin.at[row, columns(tensor * narrow, narrow)]
+        return full.at[row, columns(tensor * wide, wide)]
+
+    def target(order, half):
+        if order < 4:
+            return attn_home.at[order, :, half * narrow : (half + 1) * narrow]
+        return mlp_home.at[order - 4, :, half * wide : (half + 1) * wide]
+
+    def remote(order, half, index):
+        return pltpu.make_async_remote_copy(
+            src_ref=source(order, half),
+            dst_ref=held(order, me),
+            send_sem=home_sem.at[order, half],
+            recv_sem=start_sem.at[0],
+            device_id=place_of(index),
+            device_id_type=MESH,
+        )
+
+    def local(order, half):
+        return pltpu.make_async_copy(source(order, half), held(order, me), start_sem.at[0])
+
+    for order, half, owner in jobs:
+
+        @pl.when(me == owner)
+        def _():
+            local(order, half).start()
+
+        @pl.when(me != owner)
+        def _():
+            remote(order, half, owner).start()
+
+    def contract_rows(left, right):
+        return lax.dot_general(left, right, (((1,), (1,)), ((), ())), preferred_element_type=jnp.float32)
+
+    def orthogonalize(matrix):
+        size, width = matrix.shape
+        block = 256
+        pltpu.make_async_copy(matrix, matrix, start_sem.at[0]).wait()
+
+        def add_squares(step, total):
+            piece = matrix[pl.ds(pl.multiple_of(step * 32, 32), 32), :].astype(jnp.float32)
+            piece = piece * piece
+            return total + jnp.sum(piece.reshape(4, 8, width // 128, 128), axis=(0, 2))
+
+        squares = lax.fori_loop(0, size // 32, add_squares, jnp.zeros((8, 128), jnp.float32))
+        norm_own[...] = jnp.zeros((8, 128), jnp.float32) + jnp.sum(squares)
+        swap = pltpu.make_async_remote_copy(
+            src_ref=norm_own,
+            dst_ref=norm_got,
+            send_sem=norm_sem.at[0],
+            recv_sem=norm_sem.at[1],
+            device_id=place.twin,
+            device_id_type=MESH,
+        )
+        swap.start()
+        swap.wait()
+        scale = 1.0 / (jnp.sqrt(norm_own[...] + norm_got[...]) + 1e-06)
+        scale = scale[0:1, 0:1]
+
+        def scale_rows(step, carry):
+            at = pl.ds(pl.multiple_of(step * 32, 32), 32)
+            matrix[at, :] = (matrix[at, :].astype(jnp.float32) * scale).astype(jnp.bfloat16)
+            return carry
+
+        lax.fori_loop(0, size // 32, scale_rows, 0)
+        blocks = size // block
+
+        def swap_block(slot, index):
+            return pltpu.make_async_remote_copy(
+                src_ref=sent.at[index],
+                dst_ref=got.at[slot, index],
+                send_sem=block_send.at[index],
+                recv_sem=block_recv.at[slot, index],
+                device_id=place.twin,
+                device_id_type=MESH,
+            )
+
+        for repeat in range(NS_STEPS):
+            slot = repeat % 2
+
+            def share(index, carry):
+                at = pl.ds(pl.multiple_of(index * block, block), block)
+                sent[index] = contract_rows(matrix[at, :], matrix[...]).astype(jnp.bfloat16)
+                swap_block(slot, index).start()
+                return carry
+
+            lax.fori_loop(0, blocks, share, 0)
+
+            def add(index, carry):
+                at = pl.ds(pl.multiple_of(index * block, block), block)
+                swap_block(slot, index).wait()
+                total = sent[index].astype(jnp.float32) + got[slot, index].astype(jnp.float32)
+                gram[at, :] = total.astype(jnp.bfloat16)
+                return carry
+
+            lax.fori_loop(0, blocks, add, 0)
+
+            def polynomial(index, carry):
+                at = pl.ds(pl.multiple_of(index * block, block), block)
+                square = jnp.dot(gram[at, :], gram[...], preferred_element_type=jnp.float32)
+                poly[at, :] = (coeff_b * gram[at, :].astype(jnp.float32) + coeff_c * square).astype(jnp.bfloat16)
+                return carry
+
+            lax.fori_loop(0, blocks, polynomial, 0)
+
+            def advance(index, carry):
+                at = columns(index * block, block)
+                piece = matrix[:, at]
+                moved = jnp.dot(poly[...], piece, preferred_element_type=jnp.float32)
+                matrix[:, at] = (coeff_a * piece.astype(jnp.float32) + moved).astype(jnp.bfloat16)
+                return carry
+
+            lax.fori_loop(0, width // block, advance, 0)
+
+    def back(order, half, index):
+        return pltpu.make_async_remote_copy(
+            src_ref=held(order, index),
+            dst_ref=target(order, half),
+            send_sem=send_sem.at[0],
+            recv_sem=back_sem.at[order, half],
+            device_id=place_of(index),
+            device_id_type=MESH,
+        )
+
+    def keep(order, half):
+        return pltpu.make_async_copy(held(order, me), target(order, half), back_sem.at[order, half])
+
+    for kind, orders in ((thin, range(4)), (full, range(4, 6))):
+        owns = functools.reduce(lambda a, b: a | b, [me == owner for order, _, owner in jobs if order in orders])
+
+        @pl.when(owns)
+        def _():
+            orthogonalize(kind)
+
+    for order, half, owner in jobs:
+
+        @pl.when(me == owner)
+        def _():
+            def send(step, carry):
+                back(order, half, lax.rem(me + step, devices)).start()
+                return carry
+
+            keep(order, half).start()
+            lax.fori_loop(1, devices, send, 0)
+
+    for order, half, owner in jobs:
+        keep(order, half).wait()
+
+    for order, half, owner in jobs:
+
+        @pl.when(me == owner)
+        def _():
+            def sent_one(step, carry):
+                back(order, half, lax.rem(me + step, devices)).wait_send()
+                return carry
+
+            lax.fori_loop(1, devices, sent_one, 0)
+
+        @pl.when(me != owner)
+        def _():
+            remote(order, half, owner).wait_send()
+
+
+def newton_schulz(attn_round, mlp_round, line):
+    rows = attn_round.shape[1] * 8
+    narrow, wide = attn_round.shape[2] // 2 * line, mlp_round.shape[2] // 2 * line
+    low, dma = jnp.bfloat16, pltpu.SemaphoreType.DMA
+    return pl.pallas_call(
+        functools.partial(newton_kernel, line),
+        out_shape=[
+            jax.ShapeDtypeStruct(attn_round.shape, low),
+            jax.ShapeDtypeStruct(mlp_round.shape, low),
+        ],
+        in_specs=[pl.BlockSpec(memory_space=pl.ANY)] * 2,
+        out_specs=[pl.BlockSpec(memory_space=pl.ANY)] * 2,
+        scratch_shapes=[
+            pltpu.VMEM((rows, narrow), low),
+            pltpu.VMEM((rows, wide), low),
+            pltpu.VMEM((rows, rows), low),
+            pltpu.VMEM((rows // 256, 256, rows), low),
+            pltpu.VMEM((2, rows // 256, 256, rows), low),
+            pltpu.VMEM((rows, rows), low),
+            pltpu.VMEM((8, 128), jnp.float32),
+            pltpu.VMEM((8, 128), jnp.float32),
+            dma((6, 2)),
+            dma((1,)),
+            dma((1,)),
+            dma((6, 2)),
+            dma((2,)),
+            dma((rows // 256,)),
+            dma((2, rows // 256)),
+        ],
+        compiler_params=pltpu.CompilerParams(
+            collective_id=3, has_side_effects=True, vmem_limit_bytes=48 * 1024 * 1024
+        ),
+        name="newton_schulz",
+    )(attn_round, mlp_round)
+
+
+def pair_swap(value):
+    dp, line = lax.axis_size("dp"), lax.axis_size("tensor")
+    pairs = [(i * line + k, (i ^ 1) * line + k) for i in range(dp) for k in range(line)]
+    return lax.ppermute(value, ("dp", "tensor"), pairs)
+
+
+def corner_swap(value, place):
+    dp, line = lax.axis_size("dp"), lax.axis_size("tensor")
+    pairs = []
+    for i in range(1, dp, 2):
+        for k in range(0, line, 2):
+            pairs += [(i * line + k, (i - 1) * line + k + 1), ((i - 1) * line + k + 1, i * line + k)]
+    moved = lax.ppermute(value, ("dp", "tensor"), pairs)
+    return jnp.where(place.core == lax.rem(place.tensor, 2), value, moved)
+
+
+def both_halves(value, place):
+    other = pair_swap(value)
+    first = place.core == 0
+    return jnp.concatenate([jnp.where(first, value, other), jnp.where(first, other, value)], axis=0)
+
+
+def my_half(whole, place):
+    size = whole.shape[0] // CORES
+    return lax.dynamic_slice_in_dim(whole, place.core * size, size, 0)
+
+
+def sum_rows(partial, place):
+    size = partial.shape[0] // CORES
+    away = lax.dynamic_slice_in_dim(partial, (1 - place.core) * size, size, 0)
+    return my_half(partial, place).astype(jnp.float32) + pair_swap(away).astype(jnp.float32)
+
+
+def sum_whole(partial):
+    return partial.astype(jnp.float32) + pair_swap(partial).astype(jnp.float32)
+
+
+def norm_parts(rows):
+    centred = rows - jnp.mean(rows, axis=-1, keepdims=True)
+    spread = lax.rsqrt(jnp.mean(centred * centred, axis=-1, keepdims=True) + 1e-05)
+    return centred * spread, spread
+
+
+def norm_back(grad, gain, xhat, spread):
+    scaled = grad * gain
+    return spread * (
+        scaled
+        - jnp.mean(scaled, axis=-1, keepdims=True)
+        - xhat * jnp.mean(scaled * xhat, axis=-1, keepdims=True)
+    )
+
+
+def on_chip_pair(tokens, cotangent, segments, attn_w, mlp_w, vectors, attn_mom, mlp_mom, vector_mom):
+    line = lax.axis_size("tensor")
+    place = Place()
+    core, t = place.core, place.tensor
+    width = tokens.shape[1]
+    narrow, wide = attn_w.shape[2] // 2, mlp_w.shape[2] // 4
+    total_tokens = tokens.shape[0] * line * lax.axis_size("dp")
+
+    wqkv, wout, w_up, w_down = gather_weights(
+        attn_w.astype(jnp.bfloat16), mlp_w.astype(jnp.bfloat16), line
+    )
+    wout = wout[0]
+
+    def my_columns(row):
+        return lax.dynamic_index_in_dim(row.reshape(line, 2, narrow), core, 1, False).reshape(-1)
+
+    def place_columns(piece):
+        spread = jnp.zeros((line, 2, narrow), jnp.float32)
+        return lax.dynamic_update_slice(spread, piece.reshape(line, 1, narrow), (0, core, 0)).reshape(-1)
+
+    hidden_bias = lax.dynamic_index_in_dim(vectors[8:].reshape(line, 2, 2, wide), core, 1, False)
+    hidden_bias = hidden_bias.transpose(1, 0, 2).reshape(2, line * wide)
+
+    x_rows = both_halves(corner_swap(tokens, place), place).astype(jnp.float32)
+    grad_low = both_halves(corner_swap(cotangent, place), place)
+    seg_pairs = segments.reshape(-1, SEQ)
+    seg_own = lax.dynamic_index_in_dim(seg_pairs, t // 2, 0, False)
+    seg_ids = jnp.where(core == lax.rem(t, 2), seg_own, pair_swap(seg_own))
+
+    xhat_one, spread_one = norm_parts(x_rows)
+    normed = (xhat_one * vectors[0] + vectors[1]).astype(jnp.bfloat16)
+    projected = jnp.einsum("td,mdc->mtc", normed, wqkv, preferred_element_type=jnp.float32)
+    biases = jnp.stack([my_columns(vectors[2]), jnp.zeros((narrow * line,), jnp.float32), my_columns(vectors[3])])
+    qkv = (projected + biases[:, None]).astype(jnp.bfloat16)
+    local_heads = qkv.shape[2] // HD
+    per = narrow // HD
+    local_ids = jnp.arange(local_heads)
+    head_ids = (local_ids // per) * (2 * per) + core * per + local_ids % per
+    slopes = jnp.exp2(-(8.0 / HEADS) * (head_ids.astype(jnp.float32) + 1.0))
+    mixed, log_sums = attend(slopes, seg_ids, qkv)
+    branch = sum_whole(contract_last(mixed, wout).astype(jnp.bfloat16))
+    middle = x_rows + branch + vectors[4]
+    xhat_two, spread_two = norm_parts(middle)
+    hidden_low = (xhat_two * vectors[5] + vectors[6]).astype(jnp.bfloat16)
+    hidden_pre = (
+        jnp.einsum("td,sdc->stc", hidden_low, w_up, preferred_element_type=jnp.float32) + hidden_bias[:, None]
+    )
+    act_float, gelu_pull = jax.vjp(gelu_tanh, hidden_pre)
+    hidden_act = act_float.astype(jnp.bfloat16)
+    out_part = jnp.einsum("stc,sdc->td", hidden_act, w_down, preferred_element_type=jnp.float32)
+    output = my_half(middle, place) + sum_rows(out_part.astype(jnp.bfloat16), place) + vectors[7]
+    output = corner_swap(output.astype(jnp.bfloat16), place)
+
+    grad_down = jnp.einsum("td,stc->sdc", grad_low, hidden_act, preferred_element_type=jnp.float32)
+    grad_act = jnp.einsum("td,sdc->stc", grad_low, w_down, preferred_element_type=jnp.float32)
+    grad_pre = gelu_pull(grad_act)[0].astype(jnp.bfloat16)
+    grad_up = jnp.einsum("td,stc->sdc", hidden_low, grad_pre, preferred_element_type=jnp.float32)
+    hidden_sums = jnp.sum(grad_pre, axis=1, dtype=jnp.float32)
+    hidden_part = jnp.einsum("stc,sdc->td", grad_pre, w_up, preferred_element_type=jnp.float32)
+    grad_hidden = sum_whole(hidden_part.astype(jnp.bfloat16))
+    grad_middle = grad_low.astype(jnp.float32) + norm_back(grad_hidden, vectors[5], xhat_two, spread_two)
+    grad_mid_low = grad_middle.astype(jnp.bfloat16)
+    grad_out = contract_first(grad_mid_low, mixed)
+    grad_mixed = jnp.dot(grad_mid_low, wout, preferred_element_type=jnp.float32).astype(jnp.bfloat16)
+    grad_qkv = attend_back(slopes, seg_ids, qkv, grad_mixed, mixed, log_sums)
+    grad_proj = jnp.einsum("td,mtc->mdc", normed, grad_qkv, preferred_element_type=jnp.float32)
+    bias_sums = jnp.sum(grad_qkv, axis=1, dtype=jnp.float32)
+    normed_part = jnp.einsum("mtc,mdc->td", grad_qkv, wqkv, preferred_element_type=jnp.float32)
+    grad_normed = sum_rows(normed_part.astype(jnp.bfloat16), place)
+    xhat_mine, spread_mine = my_half(xhat_one, place), my_half(spread_one, place)
+    grad_mid_mine = my_half(grad_middle, place)
+    grad_tokens = grad_mid_mine + norm_back(grad_normed, vectors[0], xhat_mine, spread_mine)
+    grad_tokens = corner_swap(grad_tokens.astype(jnp.bfloat16), place).astype(jnp.float32)
+
+    hidden_mine = my_half(grad_hidden, place)
+    hidden_grad = lax.dynamic_update_slice(
+        jnp.zeros((line, 2, 2, wide), jnp.float32),
+        hidden_sums.reshape(2, line, wide).transpose(1, 0, 2)[:, None],
+        (0, core, 0, 0),
+    )
+    vector_rows = jnp.stack(
+        [
+            jnp.sum(grad_normed * xhat_mine, axis=0),
+            jnp.sum(grad_normed, axis=0),
+            place_columns(bias_sums[0]),
+            place_columns(bias_sums[2]),
+            jnp.sum(grad_mid_mine, axis=0),
+            jnp.sum(hidden_mine * my_half(xhat_two, place), axis=0),
+            jnp.sum(hidden_mine, axis=0),
+            jnp.sum(my_half(grad_low, place), axis=0, dtype=jnp.float32),
+        ]
+    )
+    vector_local = jnp.concatenate([vector_rows, hidden_grad.reshape(-1, width)], axis=0)
+    padding = jnp.zeros((4, width), jnp.float32)
+    low = jnp.bfloat16
+    attn_sum, mlp_sum, vector_sum = sum_gradients(
+        grad_down.astype(low),
+        grad_up.astype(low),
+        grad_out.astype(low)[None],
+        grad_proj.astype(low),
+        jnp.concatenate([vector_local, padding], axis=0),
+        line,
+    )
+    vector_grads = vector_sum[: vector_local.shape[0]]
+    attn_mom_new = 0.5 * attn_mom + attn_sum.astype(jnp.float32)
+    mlp_mom_new = 0.5 * mlp_mom + mlp_sum.astype(jnp.float32)
+    attn_ortho, mlp_ortho = newton_schulz(attn_mom_new.astype(low), mlp_mom_new.astype(low), line)
+    attn_new = attn_w - attn_ortho.astype(jnp.float32)
+    mlp_new = mlp_w - math.sqrt(FF / D) * mlp_ortho.astype(jnp.float32)
+    vector_mom_new = 0.5 * vector_mom + vector_grads
+    vector_new = vectors - 0.1 / math.sqrt(total_tokens) * vector_mom_new
+    return (
+        output,
+        grad_tokens,
+        attn_mom_new,
+        attn_new,
+        mlp_mom_new,
+        mlp_new,
+        vector_mom_new,
+        vector_new,
+    )
+
+
 def solution(mesh):
     in_specs = (
         P(("dp", "tensor"), None),
@@ -400,6 +1441,7 @@
         P(),
         P(),
     )
+    chips_of_two = (mesh.shape["dp"], mesh.shape["tensor"]) == (8, 4)
     return jax.shard_map(
-        on_device, mesh=mesh, in_specs=in_specs, out_specs=out_specs, check_vma=False
-    )
+        on_chip_pair if chips_of_two else on_device, mesh=mesh, in_specs=in_specs, out_specs=out_specs, check_vma=False
+    )

time: 2550 us -> 689 us (0.27)
  the two profiles are of different devices: /device:TPU:0 before, /device:TPU:31 now
where the time goes in v1:
time: 689 us; the launch traced here: 680 us
  Pallas kernels  519 us (75%)
  matrix products  70.3 us (10%)
  other arithmetic  40.7 us (6%)
  starting transfers between devices  24.9 us (4%)
  local copies, waits for them, and re-layouts  21 us (3%)
    pallas_call x1, Pallas kernels, newton_schulz(): pl.pallas_call(functools.partial(newton_kernel, line), out_shape=[jax.Sha...  186 us
    pallas_call x1, Pallas kernels, sum_gradients(): pl.pallas_call(functools.partial(sum_kernel, line), out_shape=[jax.ShapeD...  153 us
    pallas_call x1, Pallas kernels, gather_weights(): pl.pallas_call(functools.partial(gather_kernel, line), out_shape=[jax.Sha...  141 us
    pallas_call x1, Pallas kernels, attend_back(): pl.pallas_call(attend_back_kernel, grid=(width // (2 * HD),), out_shape=j...  21.1 us
    ppermute x7, starting transfers between devices, pair_swap(): return lax.ppermute(value, ('dp', 'tensor'), pairs)  18.1 us
    pallas_call x1, Pallas kernels, attend(): pl.pallas_call(attend_kernel, grid=(width // (2 * HD),), out_shape=[jax.S...  17.2 us
    unnamed x92, local copies, waits for them, and re-layouts  14.8 us
  transfers between devices with their start and end apart: 11, of which 1 were waited for; matrix products, arithmetic and copies ran while one was open for 11% of the time, Pallas kernels for 76%

profile of v1, /device:TPU:31, one launch (start us, length us, event | category | flops | bytes accessed | tf_op | source)
XLA Modules:
  0.0 680.1 jit_solution(16451643369626613611)
XLA Ops:
  5.3 15.3 %collective-permute-start.1 = (bf16[512,1024]{0,1:T(8,128)(2,1)S(1)}, bf16[512,1024]{0,1:T(8,128)(2,1)}, u32[]{:S(2)}, u32[]{:S(2)}) collective-permute-start(bf16[512,1024]{0,1:T(8,128)(2,1)S(1)} %broadcast_select_fusion.6), channel_id=1, source_target_pairs={{0,4},{1,5},{2,6},{3,7},{4,0},{5,1},{6,2},{7,3},{8,12},{9,13},{10,... | collective-permute-start | bytes 3145736 | tf_op jit(solution)/shard_map/ppermute | solution.py:1250
  26.5 141.2 %gather_weights.1 = (bf16[3,2,2,2,128,512]{5,4,3,2,1,0:T(8,128)(2,1)}, bf16[1,2,2,2,128,512]{5,4,3,2,1,0:T(8,128)(2,1)}, bf16[2,2,2,2,128,1024]{5,4,3,2,1,0:T(8,128)(2,1)}, bf16[2,2,2,2,128,1024]{5,4,3,2,1,0:T(8,128)(2,1)}) custom-call(bf16[4,128,256]{2,1,0:T(8,128)(2,1)} %convert_element_type.133.attn_ref, bf16[2,128,1024]{2,1,0:T(8,128)(2,1)} %convert_element_type.134.mlp_ref), custom_call_target="tpu_custom_call" | custom-call | tf_op jit(solution)/shard_map/gather_weights/pallas_call | solution.py:573
  170.5 5.4 fusion.15.qkv
  175.9 17.2 %attend.1 = (bf16[1024,512]{1,0:T(8,128)(2,1)S(1)}, f32[1024,512]{1,0:T(8,128)S(1)}) custom-call(f32[8]{0:T(128)S(1)} %fusion.37.slopes, s32[1024,1]{1,0:T(8,128)S(1)} %copy.39.seg_rows, s32[1,1024]{1,0:T(1,128)S(1)} %bitcast.125, bf16[3,1024,512]{2,1,0:T(8,128)(2,1)} %fusion.15.qkv), custom_call_target="tpu_custom_call" | custom-call | tf_op jit(solution)/shard_map/attend/pallas_call | solution.py:975
  198.8 3.0 collective-permute-done.7
  204.0 4.8 fusion.46
  210.9 3.2 copy-done.35
  214.1 5.0 fusion.29
  219.1 6.0 bitcast_convert_fusion.2
  225.0 10.6 %convert_reduce_fusion = (f32[2,1024]{1,0:T(2,128)S(1)}, bf16[2,1024,1024]{2,1,0:T(8,128)(2,1)S(1)}) fusion(f32[2,1024,1024]{1,2,0:T(8,128)S(1)} %fusion.29, f32[2,1024]{1,0:T(2,128)S(1)} %bitcast.152, bf16[2,1024,1024]{2,1,0:T(8,128)(2,1)S(1)} %bitcast.162, bf16[512,1024]{0,1:T(8,128)(2,1)S(1)} %get-tuple-element.67, ...), kind=kOutput, calls=%fused_computation.16 | convolution fusion | flops 4347394048 | bytes 18890752 | tf_op jit(solution)/shard_map/td,sdc->stc/dot_general | solution.py:1353
  235.7 6.2 bitcast_convert_fusion.1
  243.8 10.9 %convolution_convert_fusion.1 = bf16[2,1024,1024]{1,2,0:T(8,128)(2,1)} fusion(bf16[512,1024]{0,1:T(8,128)(2,1)} %copy-done.17, bf16[512,1024]{0,1:T(8,128)(2,1)} %copy-done.15, f32[2,1024,1024]{1,2,0:T(8,128)} %copy-done.41, f32[2,1024]{1,0:T(2,128)S(1)} %bitcast.153), kind=kOutput, calls=%fused_computation.40 | convolution fusion | flops 4322230272 | bytes 14688256 | tf_op jit(solution)/shard_map/td,stc->sdc/dot_general | solution.py:1352
  254.8 6.3 convolution_convert_fusion
  264.3 3.3 multiply_reduce_fusion.2
  272.2 21.1 %attend_back.1 = bf16[3,1024,512]{2,1,0:T(8,128)(2,1)} custom-call(f32[8]{0:T(128)S(1)} %fusion.37.slopes, s32[1024,1]{1,0:T(8,128)S(1)} %copy.39.seg_rows, s32[1,1024]{1,0:T(1,128)S(1)} %bitcast.126, bf16[3,1024,512]{2,1,0:T(8,128)(2,1)} %fusion.15.qkv, bf16[1024,512]{1,0:T(8,128)(2,1)S(1)} %convolution_convert_fusion.4.grad, ...), custom_call_target="tpu_custom_call" | custom-call | tf_op jit(solution)/shard_map/attend_back/pallas_call | solution.py:993
  293.3 5.7 bitcast_convert_fusion
  299.1 5.8 convert_bitcast_fusion
  306.8 3.2 copy.51
  310.1 2.7 dynamic-slice_reduce_fusion
  312.9 4.4 convolution_convert_fusion.3
  322.3 3.3 multiply_reduce_fusion.4
  325.7 4.1 dynamic-slice_reduce_fusion.1
  332.8 153.1 %sum_gradients.1 = (bf16[4,128,256]{2,1,0:T(8,128)(2,1)S(1)}, bf16[2,128,1024]{2,1,0:T(8,128)(2,1)S(1)}, f32[16,1024]{1,0:T(8,128)S(1)}) custom-call(bf16[2,2,2,2,128,1024]{5,4,3,2,1,0:T(8,128)(2,1)} %bitcast.127, bf16[2,2,2,2,128,1024]{5,4,3,2,1,0:T(8,128)(2,1)} %bitcast.128, bf16[1,2,2,2,128,512]{5,4,3,2,1,0:T(8,128)(2,1)S(1)} %bitcast.123, ...), custom_call_target="tpu_custom_call" | custom-call | tf_op jit(solution)/shard_map/sum_gradients/pallas_call | solution.py:836
  488.0 186.1 %newton_schulz.1 = (bf16[4,128,256]{2,1,0:T(8,128)(2,1)S(1)}, bf16[2,128,1024]{2,1,0:T(8,128)(2,1)S(1)}) custom-call(bf16[4,128,256]{2,1,0:T(8,128)(2,1)S(1)} %get-tuple-element.58.attn_ref, bf16[2,128,1024]{2,1,0:T(8,128)(2,1)S(1)} %get-tuple-element.56.mlp_ref), custom_call_target="tpu_custom_call" | custom-call | tf_op jit(solution)/shard_map/newton_schulz/pallas_call | solution.py:1215
  (168 shorter events, 50.7 us)
Async XLA Ops:
  0.6 20.0 %copy-start.34 = (s32[2048]{0:T(1024)S(1)}, s32[2048]{0:T(1024)}, u32[]{:S(2)}) copy-start(s32[2048]{0:T(1024)} %param.11) | copy-start | bytes 24580
  0.6 24.1 %copy-start.32 = (f32[12,1024]{1,0:T(8,128)S(1)}, f32[12,1024]{1,0:T(8,128)}, u32[]{:S(2)}) copy-start(f32[12,1024]{1,0:T(8,128)} %param.14) | copy-start | bytes 147460
  0.7 24.2 %copy-start.28 = (f32[4,128,256]{2,1,0:T(8,128)S(1)}, f32[4,128,256]{2,1,0:T(8,128)}, u32[]{:S(2)}) copy-start(f32[4,128,256]{2,1,0:T(8,128)} %param.12) | copy-start | bytes 1572868
  0.7 25.0 %copy-start.23 = (f32[2,128,1024]{2,1,0:T(8,128)S(1)}, f32[2,128,1024]{2,1,0:T(8,128)}, u32[]{:S(2)}) copy-start(f32[2,128,1024]{2,1,0:T(8,128)} %param.13) | copy-start | bytes 3145732
  2.3 1.7 collective-permute-start
  5.3 162.6 %collective-permute-start.1 = (bf16[512,1024]{0,1:T(8,128)(2,1)S(1)}, bf16[512,1024]{0,1:T(8,128)(2,1)}, u32[]{:S(2)}, u32[]{:S(2)}) collective-permute-start(bf16[512,1024]{0,1:T(8,128)(2,1)S(1)} %broadcast_select_fusion.6), channel_id=1, source_target_pairs={{0,4},{1,5},{2,6},{3,7},{4,0},{5,1},{6,2},{7,3},{8,12},{9,13},{10,... | collective-permute-start | bytes 3145736 | tf_op jit(solution)/shard_map/ppermute | solution.py:1250
  20.7 147.0 %collective-permute-start.2 = (s32[1024]{0:T(1024)S(1)}, s32[1024]{0:T(1024)S(1)}, u32[]{:S(2)}, u32[]{:S(2)}) collective-permute-start(s32[1024]{0:T(1024)S(1)} %bitcast.141), channel_id=1, source_target_pairs={{0,4},{1,5},{2,6},{3,7},{4,0},{5,1},{6,2},{7,3},{8,12},{9,13},{10,... | collective-permute-start | bytes 12296 | tf_op jit(solution)/shard_map/ppermute | solution.py:1250
  23.0 172.8 %collective-permute-start.6 = (bf16[512,1024]{0,1:T(8,128)(2,1)}, bf16[512,1024]{0,1:T(8,128)(2,1)}, u32[]{:S(2)}, u32[]{:S(2)}) collective-permute-start(bf16[512,1024]{0,1:T(8,128)(2,1)} %copy.44), channel_id=1, source_target_pairs={{4,1},{1,4},{6,3},{3,6},{12,9},{9,12},{14,11},{11,14},{20,17},{17,... | collective-permute-start | bytes 3145736 | tf_op jit(solution)/shard_map/ppermute | solution.py:1259
  170.5 22.7 %copy-start.39 = (bf16[1,2,2,2,128,512]{5,4,3,2,1,0:T(8,128)(2,1)S(1)}, bf16[1,2,2,2,128,512]{5,4,3,2,1,0:T(8,128)(2,1)}, u32[]{:S(2)}) copy-start(bf16[1,2,2,2,128,512]{5,4,3,2,1,0:T(8,128)(2,1)} %get-tuple-element.21) | copy-start | bytes 3145732
  195.8 8.2 %collective-permute-start.3 = (bf16[1024,1024]{0,1:T(8,128)(2,1)}, bf16[1024,1024]{0,1:T(8,128)(2,1)}, u32[]{:S(2)}, u32[]{:S(2)}) collective-permute-start(bf16[1024,1024]{0,1:T(8,128)(2,1)} %convolution_convert_fusion.2), channel_id=1, source_target_pairs={{0,4},{1,5},{2,6},{3,7},{4,0},{5,1},{6,2},{7,3},{8,12},{9,13},{10,... | collective-permute-start | bytes 6291464 | tf_op jit(solution)/shard_map/ppermute | solution.py:1250
  196.9 4.9 collective-permute-start.7
  203.5 21.5 %copy-start.15 = (bf16[512,1024]{0,1:T(8,128)(2,1)}, bf16[512,1024]{0,1:T(8,128)(2,1)S(1)}, u32[]{:S(2)}) copy-start(bf16[512,1024]{0,1:T(8,128)(2,1)S(1)} %get-tuple-element.66) | copy-start | bytes 3145732
  203.5 21.5 %copy-start.17 = (bf16[512,1024]{0,1:T(8,128)(2,1)}, bf16[512,1024]{0,1:T(8,128)(2,1)S(1)}, u32[]{:S(2)}) copy-start(bf16[512,1024]{0,1:T(8,128)(2,1)S(1)} %get-tuple-element.67) | copy-start | bytes 3145732
  243.3 17.9 %collective-permute-start.4 = (bf16[512,1024]{0,1:T(8,128)(2,1)S(1)}, bf16[512,1024]{0,1:T(8,128)(2,1)S(1)}, u32[]{:S(2)}, u32[]{:S(2)}) collective-permute-start(bf16[512,1024]{0,1:T(8,128)(2,1)S(1)} %constant_dynamic-slice_fusion.1), channel_id=1, source_target_pairs={{0,4},{1,5},{2,6},{3,7},{4,0},{5,1},{6,2},{7,3},{8,12},{9,13},{10,... | collective-permute-start | bytes 3145736 | tf_op jit(solution)/shard_map/ppermute | solution.py:1250
  243.5 20.9 %collective-permute-start.8 = (bf16[1024,1024]{0,1:T(8,128)(2,1)}, bf16[1024,1024]{0,1:T(8,128)(2,1)S(1)}, u32[]{:S(2)}, u32[]{:S(2)}) collective-permute-start(bf16[1024,1024]{0,1:T(8,128)(2,1)} %bitcast_convert_fusion.1), channel_id=1, source_target_pairs={{0,4},{1,5},{2,6},{3,7},{4,0},{5,1},{6,2},{7,3},{8,12},{9,13},{10,... | collective-permute-start | bytes 6291464 | tf_op jit(solution)/shard_map/ppermute | solution.py:1250
  262.5 54.8 %collective-permute-start.5 = (bf16[512,1024]{0,1:T(8,128)(2,1)}, bf16[512,1024]{0,1:T(8,128)(2,1)}, u32[]{:S(2)}, u32[]{:S(2)}) collective-permute-start(bf16[512,1024]{0,1:T(8,128)(2,1)} %add_convert_fusion.4), channel_id=1, source_target_pairs={{4,1},{1,4},{6,3},{3,6},{12,9},{9,12},{14,11},{11,14},{20,17},{17,... | collective-permute-start | bytes 3145736 | tf_op jit(solution)/shard_map/ppermute | solution.py:1259
  272.2 21.1 %copy-start.38 = (bf16[3,2,2,2,128,512]{5,4,3,2,1,0:T(8,128)(2,1)S(1)}, bf16[3,2,2,2,128,512]{5,4,3,2,1,0:T(8,128)(2,1)}, u32[]{:S(2)}) copy-start(bf16[3,2,2,2,128,512]{5,4,3,2,1,0:T(8,128)(2,1)} %get-tuple-element.19) | copy-start | bytes 9437188
  305.9 16.3 %collective-permute-start.9 = (bf16[512,1024]{0,1:T(8,128)(2,1)}, bf16[512,1024]{0,1:T(8,128)(2,1)}, u32[]{:S(2)}, u32[]{:S(2)}) collective-permute-start(bf16[512,1024]{0,1:T(8,128)(2,1)} %constant_dynamic-slice_fusion), channel_id=1, source_target_pairs={{0,4},{1,5},{2,6},{3,7},{4,0},{5,1},{6,2},{7,3},{8,12},{9,13},{10,... | collective-permute-start | bytes 3145736 | tf_op jit(solution)/shard_map/ppermute | solution.py:1250
  329.8 347.0 %collective-permute-start.10 = (bf16[512,1024]{0,1:T(8,128)(2,1)}, bf16[512,1024]{0,1:T(8,128)(2,1)}, u32[]{:S(2)}, u32[]{:S(2)}) collective-permute-start(bf16[512,1024]{0,1:T(8,128)(2,1)} %get-tuple-element.64), channel_id=1, source_target_pairs={{4,1},{1,4},{6,3},{3,6},{12,9},{9,12},{14,11},{11,14},{20,17},{17,... | collective-permute-start | bytes 3145736 | tf_op jit(solution)/shard_map/ppermute | solution.py:1259
  332.8 153.2 %copy-start.30 = (f32[2,128,1024]{2,1,0:T(8,128)S(1)}, f32[2,128,1024]{2,1,0:T(8,128)}, u32[]{:S(2)}) copy-start(f32[2,128,1024]{2,1,0:T(8,128)} %param.16) | copy-start | bytes 3145732
  332.8 154.4 %copy-start.31 = (f32[4,128,256]{2,1,0:T(8,128)S(1)}, f32[4,128,256]{2,1,0:T(8,128)}, u32[]{:S(2)}) copy-start(f32[4,128,256]{2,1,0:T(8,128)} %param.15) | copy-start | bytes 1572868
  485.9 188.2 %copy-start.33 = (f32[12,1024]{1,0:T(8,128)S(1)}, f32[12,1024]{1,0:T(8,128)}, u32[]{:S(2)}) copy-start(f32[12,1024]{1,0:T(8,128)} %param.17) | copy-start | bytes 147460
  485.9 188.8 %copy-start.29 = (f32[4,128,256]{2,1,0:T(8,128)S(1)}, f32[4,128,256]{2,1,0:T(8,128)}, u32[]{:S(2)}) copy-start(f32[4,128,256]{2,1,0:T(8,128)} %param.12) | copy-start | bytes 1572868
  485.9 189.7 %copy-start.24 = (f32[2,128,1024]{2,1,0:T(8,128)S(1)}, f32[2,128,1024]{2,1,0:T(8,128)}, u32[]{:S(2)}) copy-start(f32[2,128,1024]{2,1,0:T(8,128)} %param.13) | copy-start | bytes 3145732
  (32 other events, 157.9 us)

commit v2 on v1

--- a/solution.py
+++ b/solution.py
@@ -470,8 +470,25 @@
         return ref.at[:, y, x, half, :, columns(t * width, width)]
 
     both = pl.ds(0, 2)
-    steps = range(1, line)
+    last = len(groups) - 1
     to_right, to_left, half_x, half_y, rest_y, rest_x = 1, line, 2 * line - 1, 2 * line, 2 * line + 1, 2 * line + 2
+
+    def chunk(group, index):
+        ref, width, _ = groups[group]
+        cols = columns(index * width, width)
+        if group == last:
+            return ref.at[:, :, :, :, :, cols]
+        return ref.at[:, y, x, :, :, cols]
+
+    def corner(group, ys, xs, half):
+        ref, width, _ = groups[group]
+        if group == last:
+            return ref.at[:, ys, xs, half, :, columns(t * width, width)]
+        return ref.at[:, ys, xs, half]
+
+    def entry(group, half):
+        ref, width, _ = groups[group]
+        return ref.at[:, y, x, half, :, columns(t * width, width)]
 
     def own(group):
         return pltpu.make_async_copy(
@@ -482,10 +499,11 @@
         target = entry(group, place.core)
         return copy(group, 0, groups[group][2](1 - place.core), target, place.twin)
 
-    def start_line(group):
+    def enter(group):
         own(group).wait()
         same(group, 0, entry(group, 1 - place.core), place.twin).wait_recv()
 
+    def line_start(group):
         @pl.when(t < line - 1)
         def _():
             same(group, to_right, chunk(group, t), place.right).start()
@@ -494,44 +512,42 @@
         def _():
             same(group, to_left, chunk(group, t), place.left).start()
 
-    def run_line(group):
-        for step in steps:
-
-            @pl.when(t >= step)
-            def _():
-                same(group, to_right + step - 1, chunk(group, t - step), place.left).wait_recv()
-                if step < line - 1:
-
-                    @pl.when(t < line - 1)
-                    def _():
-                        same(group, to_right + step, chunk(group, t - step), place.right).start()
-
-            @pl.when(t + step <= line - 1)
-            def _():
-                same(group, to_left + step - 1, chunk(group, t + step), place.right).wait_recv()
-                if step < line - 1:
-
-                    @pl.when(t > 0)
-                    def _():
-                        same(group, to_left + step, chunk(group, t + step), place.left).start()
-
-    def start_plane(group):
+    def line_step(group, step):
+        @pl.when(t >= step)
+        def _():
+            same(group, to_right + step - 1, chunk(group, t - step), place.left).wait_recv()
+            if step < line - 1:
+
+                @pl.when(t < line - 1)
+                def _():
+                    same(group, to_right + step, chunk(group, t - step), place.right).start()
+
+        @pl.when(t + step <= line - 1)
+        def _():
+            same(group, to_left + step - 1, chunk(group, t + step), place.right).wait_recv()
+            if step < line - 1:
+
+                @pl.when(t > 0)
+                def _():
+                    same(group, to_left + step, chunk(group, t + step), place.left).start()
+
+    def plane_start(group):
         same(group, half_x, corner(group, y, x, 0), place.across_x).start()
         same(group, half_y, corner(group, y, x, 1), place.across_y).start()
 
-    def run_plane(group):
+    def plane_step(group):
         same(group, half_x, corner(group, y, 1 - x, 0), place.across_x).wait_recv()
         same(group, rest_y, corner(group, y, both, 0), place.across_y).start()
         same(group, half_y, corner(group, 1 - y, x, 1), place.across_y).wait_recv()
         same(group, rest_x, corner(group, both, x, 1), place.across_x).start()
 
-    def end_plane(group):
+    def plane_end(group):
         same(group, rest_y, corner(group, 1 - y, both, 0), place.across_y).wait_recv()
         same(group, rest_x, corner(group, both, 1 - x, 1), place.across_x).wait_recv()
 
     def wait_sends(group):
         first(group).wait_send()
-        for step in steps:
+        for step in range(1, line):
 
             @pl.when((t - step + 1 >= 0) & (t < line - 1))
             def _():
@@ -546,21 +562,50 @@
         same(group, rest_y, corner(group, y, both, 0), place.across_y).wait_send()
         same(group, rest_x, corner(group, both, x, 1), place.across_x).wait_send()
 
-    count = len(groups)
-    for group in range(count):
+    def line_tail(group, after):
+        for step in range(1, line - 1):
+            line_step(group, step)
+        if after is not None:
+            enter(after)
+            line_start(after)
+        line_step(group, line - 1)
+
+    out, qkv, up_a, up_b, down_a = 1, 0, 2, 3, 4
+    for group in (out, last, qkv, up_a, up_b, down_a):
         own(group).start()
         first(group).start()
-    for group in range(count):
-        start_line(group)
-    for group in range(count + 1):
-        if group < count:
-            run_line(group)
-            start_plane(group)
-        if group >= 1:
-            run_plane(group - 1)
-    for group in range(count):
-        end_plane(group)
-    for group in range(count):
+    enter(out)
+    line_start(out)
+    enter(last)
+    plane_start(last)
+    line_tail(out, qkv)
+    plane_start(out)
+    plane_step(last)
+    plane_step(out)
+    line_tail(qkv, up_a)
+    plane_start(qkv)
+    plane_end(last)
+    line_tail(up_a, up_b)
+    plane_end(out)
+    plane_step(qkv)
+    plane_start(up_a)
+    line_tail(up_b, down_a)
+    plane_end(qkv)
+    line_tail(down_a, None)
+    line_start(last)
+    plane_step(up_a)
+    plane_start(up_b)
+    line_step(last, 1)
+    plane_end(up_a)
+    plane_step(up_b)
+    plane_start(down_a)
+    for step in range(2, line - 1):
+        line_step(last, step)
+    plane_end(up_b)
+    line_step(last, line - 1)
+    plane_step(down_a)
+    plane_end(down_a)
+    for group in range(len(groups)):
         wait_sends(group)
 
 
@@ -589,274 +634,306 @@
 
 
 def add_blocks(target, sources):
-    count, rows = target.shape[0], target.shape[1]
+    lead, rows = target.shape[:-2], target.shape[-2]
     per = rows // 32
 
     def body(step, carry):
-        at = (step // per, pl.ds(pl.multiple_of(lax.rem(step, per) * 32, 32), 32))
+        block, at = step // per, []
+        for size in lead[::-1]:
+            at.insert(0, lax.rem(block, size))
+            block = block // size
+        at = tuple(at) + (pl.ds(pl.multiple_of(lax.rem(step, per) * 32, 32), 32),)
         total = sources[0][at].astype(jnp.float32)
         for source in sources[1:]:
             total = total + source[at].astype(jnp.float32)
         target[at] = total.astype(target.dtype)
         return carry
 
-    lax.fori_loop(0, count * per, body, 0)
-
-
-def sum_kernel(line, down_ref, up_ref, out_ref, qkv_ref, vec_ref, attn_home, mlp_home, vec_out, *scratch):
-    place = Place()
-    x, y, t, core = place.x, place.y, place.tensor, place.core
-    group_count = 6
-    names = ("own_a", "own_b", "got_a", "got_b", "last_a", "last_b", "plane", "from_left", "from_right", "done")
-    buffers = []
-    for group in range(group_count):
-        start = group * len(names)
-        buffers.append(dict(zip(names, scratch[start : start + len(names)])))
-    own_sem, send_sem, recv_sem, vec_sum, vec_got, vec_line, vec_sem = scratch[group_count * len(names) :]
-    narrow = attn_home.shape[2] // 2
-    wide = mlp_home.shape[2] // 4
-
-    def attn_target(lo, hi):
-        return lambda: attn_home.at[lo:hi, :, columns(core * narrow, narrow)]
-
-    def mlp_target(index, part):
-        return lambda: mlp_home.at[index : index + 1, :, columns((2 * core + part) * wide, wide)]
-
-    groups = [
-        (down_ref.at[0:1], wide, mlp_target(1, 0)),
-        (down_ref.at[1:2], wide, mlp_target(1, 1)),
-        (up_ref.at[0:1], wide, mlp_target(0, 0)),
-        (up_ref.at[1:2], wide, mlp_target(0, 1)),
-        (out_ref, narrow, attn_target(3, 4)),
-        (qkv_ref, narrow, attn_target(0, 3)),
-    ]
-    greet(place, line)
-    both = pl.ds(0, 2)
-    one_a, one_b, two_a, two_b, home_slot = 0, 1, 2, 3, 4
-    rightward, leftward = 5, 5 + line
-
-    def copy(group, slot, source, target, device):
+    lax.fori_loop(0, math.prod(lead) * per, body, 0)
+
+
+class PlaneSum:
+    @staticmethod
+    def scratch(count, rows, width):
+        pair = pltpu.VMEM((count, 2, rows, width), jnp.bfloat16)
+        single = pltpu.VMEM((count, rows, width), jnp.bfloat16)
+        dma = pltpu.SemaphoreType.DMA
+        return [pair] * 4 + [single] * 2 + [dma((2,)), dma((4,)), dma((4,))]
+
+    SCRATCH = 9
+
+    def __init__(self, place, source, result, scratch):
+        self.place, self.source, self.result = place, source, result
+        self.own, self.got, self.last = scratch[0:2], scratch[2:4], scratch[4:6]
+        self.own_sem, self.send_sem, self.recv_sem = scratch[6:9]
+
+    def copy(self, slot, source, target, device):
         return pltpu.make_async_remote_copy(
             src_ref=source,
             dst_ref=target,
-            send_sem=send_sem.at[group, slot],
-            recv_sem=recv_sem.at[group, slot],
+            send_sem=self.send_sem.at[slot],
+            recv_sem=self.recv_sem.at[slot],
             device_id=device,
             device_id_type=MESH,
         )
 
-    def loads(group):
-        ref, held = groups[group][0], buffers[group]
-        return (
-            pltpu.make_async_copy(ref.at[:, y, both, 0], held["own_a"], own_sem.at[group, 0]),
-            pltpu.make_async_copy(ref.at[:, both, x, 1], held["own_b"], own_sem.at[group, 1]),
-        )
-
-    def first_copies(group):
-        ref, held = groups[group][0], buffers[group]
-        return (
-            copy(group, one_a, ref.at[:, 1 - y, both, 0], held["got_a"], place.across_y),
-            copy(group, one_b, ref.at[:, both, 1 - x, 1], held["got_b"], place.across_x),
-        )
-
-    def second_copies(group):
-        held = buffers[group]
-        return (
-            copy(group, two_a, held["own_a"].at[:, 1 - x], held["last_a"], place.across_x),
-            copy(group, two_b, held["own_b"].at[:, 1 - y], held["last_b"], place.across_y),
-        )
-
-    def start(group):
-        for each in first_copies(group) + loads(group):
-            each.start()
-
-    def plane_one(group):
-        held = buffers[group]
-        sends = second_copies(group)
-        for part, other, mine in (("a", 1 - x, x), ("b", 1 - y, y)):
-            index = 0 if part == "a" else 1
-            loads(group)[index].wait()
-            first_copies(group)[index].wait_recv()
-            own, got = held["own_" + part], held["got_" + part]
-            add_blocks(own.at[:, other], (own.at[:, other], got.at[:, other]))
-            sends[index].start()
+    def cut(self, index, mine):
+        both, place = pl.ds(0, 2), self.place
+        if index == 0:
+            return self.source.at[:, place.y if mine else 1 - place.y, both, 0]
+        return self.source.at[:, both, place.x if mine else 1 - place.x, 1]
+
+    def load(self, index):
+        return pltpu.make_async_copy(self.cut(index, True), self.own[index], self.own_sem.at[index])
+
+    def first(self, index):
+        device = self.place.across_x if index else self.place.across_y
+        return self.copy(index, self.cut(index, False), self.got[index], device)
+
+    def second(self, index):
+        mine = self.place.y if index else self.place.x
+        device = self.place.across_y if index else self.place.across_x
+        return self.copy(2 + index, self.own[index].at[:, 1 - mine], self.last[index], device)
+
+    def start(self):
+        for index in range(2):
+            self.first(index).start()
+            self.load(index).start()
+
+    def one(self):
+        for index in range(2):
+            mine = self.place.y if index else self.place.x
+            self.load(index).wait()
+            self.first(index).wait_recv()
+            own, got = self.own[index], self.got[index]
+            add_blocks(own.at[:, 1 - mine], (own.at[:, 1 - mine], got.at[:, 1 - mine]))
+            self.second(index).start()
             add_blocks(own.at[:, mine], (own.at[:, mine], got.at[:, mine]))
 
-    def plane_two(group):
-        held = buffers[group]
-        for index, (part, mine) in enumerate((("a", x), ("b", y))):
-            second_copies(group)[index].wait_recv()
-            add_blocks(held["plane"].at[:, index], (held["own_" + part].at[:, mine], held["last_" + part]))
-
-    def piece(group, name, index, half):
-        width = groups[group][1]
-        return buffers[group][name].at[:, half, :, index * width : (index + 1) * width]
-
-    def hop(group, index, right):
-        width = groups[group][1]
-        cut = slice(index * width, (index + 1) * width)
-        held = buffers[group]
-        slot = (rightward if right else leftward) + index
-        target = held["from_left" if right else "from_right"]
-        return copy(
-            group, slot, held["plane"].at[:, :, :, cut], target.at[:, :, :, cut], place.right if right else place.left
-        )
-
-    def run_line(group):
-        for step in range(line - 1):
-            for right in (True, False):
-                index = line - 1 - step if right else step
-                name = "from_left" if right else "from_right"
-
-                @pl.when((t < index) if right else (t > index))
+    def two(self):
+        for index in range(2):
+            mine = self.place.y if index else self.place.x
+            self.second(index).wait_recv()
+            add_blocks(self.result.at[:, index], (self.own[index].at[:, mine], self.last[index]))
+
+    def sent(self):
+        for index in range(2):
+            self.first(index).wait_send()
+            self.second(index).wait_send()
+
+
+class LineSum:
+    @staticmethod
+    def scratch(shape, line):
+        dma = pltpu.SemaphoreType.DMA
+        return [pltpu.VMEM(shape, jnp.bfloat16)] * 2 + [dma((2, line)), dma((2, line))]
+
+    SCRATCH = 4
+
+    def __init__(self, place, line, value, result, scratch):
+        self.place, self.line, self.value, self.result = place, line, value, result
+        self.got = scratch[0:2]
+        self.send_sem, self.recv_sem = scratch[2:4]
+        self.width = value.shape[-1] // line
+
+    def part(self, ref, index):
+        return ref.at[(slice(None),) * (len(ref.shape) - 1) + (slice(index * self.width, (index + 1) * self.width),)]
+
+    def hop(self, index, left):
+        return pltpu.make_async_remote_copy(
+            src_ref=self.part(self.value, index),
+            dst_ref=self.part(self.got[left], index),
+            send_sem=self.send_sem.at[left, index],
+            recv_sem=self.recv_sem.at[left, index],
+            device_id=self.place.left if left else self.place.right,
+            device_id_type=MESH,
+        )
+
+    def step(self, step):
+        for left in range(2):
+            for index in range(self.line):
+                away = index if left else self.line - 1 - index
+                order = step - away
+                plane = self.line - 1 - order if left else order
+                if order < 0 or (plane <= index if left else plane >= index):
+                    continue
+
+                @pl.when(self.place.tensor == plane)
                 def _():
-                    @pl.when((t > 0) if right else (t < line - 1))
-                    def _():
-                        hop(group, index, right).wait_recv()
-                        for half in range(2):
-                            plane = piece(group, "plane", index, half)
-                            add_blocks(plane, (plane, piece(group, name, index, half)))
-
-                    hop(group, index, right).start()
-
-    def end_line(group):
-        held = buffers[group]
-        for index in range(line):
-
-            @pl.when(t == index)
+                    if order > 0:
+                        self.hop(index, left).wait_recv()
+                        value = self.part(self.value, index)
+                        add_blocks(value, (value, self.part(self.got[left], index)))
+                    if away > 0:
+                        self.hop(index - 1 if left else index + 1, left).wait_send()
+                    self.hop(index, left).start()
+
+    def end(self):
+        for index in range(self.line):
+
+            @pl.when(self.place.tensor == index)
             def _():
-                names = ["plane"]
+                sources = [self.part(self.value, index)]
+                for left in range(2):
+                    if index < self.line - 1 if left else index > 0:
+                        self.hop(index, left).wait_recv()
+                        sources.append(self.part(self.got[left], index))
+                add_blocks(self.result, sources)
+
+    def sent(self):
+        for index in range(self.line):
+
+            @pl.when(self.place.tensor == index)
+            def _():
                 if index > 0:
-                    hop(group, index, True).wait_recv()
-                    names.append("from_left")
-                if index < line - 1:
-                    hop(group, index, False).wait_recv()
-                    names.append("from_right")
-                for half in range(2):
-                    add_blocks(held["done"].at[:, half], [piece(group, name, index, half) for name in names])
-
-        for each in homes(group):
-            each.start()
-
-    def homes(group):
-        done, target = buffers[group]["done"], groups[group][2]
-        return (
-            pltpu.make_async_copy(done.at[:, core], target(), own_sem.at[group, 2]),
-            copy(group, home_slot, done.at[:, 1 - core], target(), place.twin),
-        )
-
-    def finish(group):
-        local, remote = homes(group)
-        local.wait()
-        remote.wait()
-        for each in first_copies(group) + second_copies(group):
-            each.wait_send()
-        for step in range(line - 1):
-            for right in (True, False):
-                index = line - 1 - step if right else step
-
-                @pl.when((t < index) if right else (t > index))
-                def _():
-                    hop(group, index, right).wait_send()
-
-    partners = (place.twin, place.across_x, place.across_y)
-
-    def vec_copy(stage):
+                    self.hop(index - 1, 1).wait_send()
+                if index < self.line - 1:
+                    self.hop(index + 1, 0).wait_send()
+
+
+class HomeCopy:
+    def __init__(self, place, value, target, scratch):
+        self.place, self.value, self.target = place, value, target
+        self.own_sem, self.sem = scratch
+
+    SCRATCH = 2
+
+    @staticmethod
+    def scratch():
+        return [pltpu.SemaphoreType.DMA((1,)), pltpu.SemaphoreType.DMA((2,))]
+
+    def keep(self):
+        return pltpu.make_async_copy(self.value.at[:, self.place.core], self.target, self.own_sem.at[0])
+
+    def give(self):
         return pltpu.make_async_remote_copy(
-            src_ref=vec_sum.at[stage],
-            dst_ref=vec_got.at[stage],
-            send_sem=vec_sem.at[0, stage],
-            recv_sem=vec_sem.at[1, stage],
-            device_id=partners[stage],
+            src_ref=self.value.at[:, 1 - self.place.core],
+            dst_ref=self.target,
+            send_sem=self.sem.at[0],
+            recv_sem=self.sem.at[1],
+            device_id=self.place.twin,
             device_id_type=MESH,
         )
 
-    def vec_hop(other, source):
+    def start(self):
+        self.keep().start()
+        self.give().start()
+
+    def wait(self):
+        self.keep().wait()
+        self.give().wait()
+
+
+class GroupSum:
+    @staticmethod
+    def scratch(count, rows, width, line, line_first=False):
+        low = jnp.bfloat16
+        part = width // line
+        done = pltpu.VMEM((count, 2, rows, part), low)
+        if line_first:
+            whole = (count, 2, 2, 2, rows, width)
+            held = [pltpu.VMEM(whole, low), pltpu.VMEM(whole[:-1] + (part,), low), pltpu.SemaphoreType.DMA((1,))]
+            plane, along = PlaneSum.scratch(count, rows, part), LineSum.scratch(whole, line)
+        else:
+            middle = (count, 2, rows, width)
+            held = [pltpu.VMEM(middle, low)]
+            plane, along = PlaneSum.scratch(count, rows, width), LineSum.scratch(middle, line)
+        return held + [done] + plane + along + HomeCopy.scratch()
+
+    def __init__(self, place, line, source, target, scratch, line_first=False):
+        scratch = list(scratch)
+
+        def take(count):
+            taken = scratch[:count]
+            del scratch[:count]
+            return taken
+
+        if line_first:
+            whole, middle, load_sem = take(3)
+            self.load = lambda: pltpu.make_async_copy(source, whole, load_sem.at[0])
+        else:
+            (middle,) = take(1)
+        (done,) = take(1)
+        plane, along = take(PlaneSum.SCRATCH), take(LineSum.SCRATCH)
+        if line_first:
+            self.line = LineSum(place, line, whole, middle, along)
+            self.plane = PlaneSum(place, middle, done, plane)
+        else:
+            self.plane = PlaneSum(place, source, middle, plane)
+            self.line = LineSum(place, line, middle, done, along)
+        self.home = HomeCopy(place, done, target, take(HomeCopy.SCRATCH))
+
+    def finish(self):
+        self.home.wait()
+        self.plane.sent()
+        self.line.sent()
+
+
+class VectorSum:
+    @staticmethod
+    def scratch(shape, line):
+        return [
+            pltpu.VMEM((4,) + shape, jnp.float32),
+            pltpu.VMEM((3,) + shape, jnp.float32),
+            pltpu.VMEM((line,) + shape, jnp.float32),
+            pltpu.SemaphoreType.DMA((4, max(line, 3))),
+        ]
+
+    def __init__(self, place, line, scratch):
+        self.place, self.line = place, line
+        self.sums, self.got, self.along, self.sem = scratch
+
+    def copy(self, stage):
+        place = self.place
         return pltpu.make_async_remote_copy(
-            src_ref=vec_sum.at[3],
-            dst_ref=vec_line.at[source],
-            send_sem=vec_sem.at[2, other],
-            recv_sem=vec_sem.at[3, source],
-            device_id=(place.dp, other),
+            src_ref=self.sums.at[stage],
+            dst_ref=self.got.at[stage],
+            send_sem=self.sem.at[0, stage],
+            recv_sem=self.sem.at[1, stage],
+            device_id=(place.twin, place.across_x, place.across_y)[stage],
             device_id_type=MESH,
         )
 
-    def vec_step(stage):
-        if 0 < stage <= 3:
-            vec_copy(stage - 1).wait()
-            vec_sum[stage] = vec_sum[stage - 1] + vec_got[stage - 1]
-        if stage < 3:
-            vec_copy(stage).start()
-        if stage == 3:
-            vec_line[t] = vec_sum[3]
-        for other in range(line):
+    def hop(self, other, source):
+        return pltpu.make_async_remote_copy(
+            src_ref=self.sums.at[3],
+            dst_ref=self.along.at[source],
+            send_sem=self.sem.at[2, other],
+            recv_sem=self.sem.at[3, source],
+            device_id=(self.place.dp, other),
+            device_id_type=MESH,
+        )
+
+    def start(self, value):
+        self.sums[0] = value
+        self.copy(0).start()
+
+    def step(self, stage):
+        self.copy(stage).wait()
+        self.sums[stage + 1] = self.sums[stage] + self.got[stage]
+        if stage < 2:
+            self.copy(stage + 1).start()
+            return
+        self.along[self.place.tensor] = self.sums[3]
+        for other in range(self.line):
+
+            @pl.when(self.place.tensor != other)
+            def _():
+                self.hop(other, self.place.tensor).start()
+
+    def end(self):
+        t = self.place.tensor
+        for other in range(self.line):
 
             @pl.when(t != other)
             def _():
-                if stage == 3:
-                    vec_hop(other, t).start()
-                if stage == 4:
-                    vec_hop(other, t).wait_send()
-                    vec_hop(t, other).wait_recv()
-
-        if stage == 4:
-            total = vec_line[0]
-            for other in range(1, line):
-                total = total + vec_line[other]
-            vec_out[...] = total
-
-    vec_sum[0] = vec_ref[...]
-    for group in range(group_count):
-        start(group)
-    for group in range(group_count + 2):
-        if group < 5:
-            vec_step(group)
-        if group < group_count:
-            plane_one(group)
-        if 1 <= group <= group_count:
-            plane_two(group - 1)
-            run_line(group - 1)
-        if group >= 2:
-            end_line(group - 2)
-    for group in range(group_count):
-        finish(group)
-
-
-def sum_gradients(down, up, out, qkv, vec, line):
-    rows = qkv.shape[1] // 8
-    narrow, wide = qkv.shape[2], down.shape[2]
-    counts = [(1, wide)] * 4 + [(1, narrow), (3, narrow)]
-    scratch = []
-    for count, width in counts:
-        pair = pltpu.VMEM((count, 2, rows, width), jnp.bfloat16)
-        single = pltpu.VMEM((count, rows, width), jnp.bfloat16)
-        done = pltpu.VMEM((count, 2, rows, width // line), jnp.bfloat16)
-        scratch += [pair] * 4 + [single] * 2 + [pair] * 3 + [done]
-    slots = 5 + 2 * line
-    return pl.pallas_call(
-        functools.partial(sum_kernel, line),
-        out_shape=[
-            jax.ShapeDtypeStruct((4, rows, 2 * narrow // line), jnp.bfloat16),
-            jax.ShapeDtypeStruct((2, rows, 4 * wide // line), jnp.bfloat16),
-            jax.ShapeDtypeStruct(vec.shape, jnp.float32),
-        ],
-        in_specs=[pl.BlockSpec(memory_space=pl.ANY)] * 4 + [pl.BlockSpec(memory_space=pltpu.VMEM)],
-        out_specs=[pl.BlockSpec(memory_space=pl.ANY)] * 2 + [pl.BlockSpec(memory_space=pltpu.VMEM)],
-        scratch_shapes=scratch
-        + [
-            pltpu.SemaphoreType.DMA((6, 3)),
-            pltpu.SemaphoreType.DMA((6, slots)),
-            pltpu.SemaphoreType.DMA((6, slots)),
-            pltpu.VMEM((4,) + vec.shape, jnp.float32),
-            pltpu.VMEM((3,) + vec.shape, jnp.float32),
-            pltpu.VMEM((line,) + vec.shape, jnp.float32),
-            pltpu.SemaphoreType.DMA((4, max(line, 3))),
-        ],
-        compiler_params=pltpu.CompilerParams(
-            collective_id=2, has_side_effects=True, vmem_limit_bytes=48 * 1024 * 1024
-        ),
-        name="sum_gradients",
-    )(*(each.reshape(each.shape[0], 2, 2, 2, rows, each.shape[2]) for each in (down, up, out, qkv)), vec)
+                self.hop(other, t).wait_send()
+                self.hop(t, other).wait_recv()
+
+        total = self.along[0]
+        for other in range(1, self.line):
+            total = total + self.along[other]
+        return total
 
 
 LOG2E = 1.4426950408889634
@@ -917,47 +994,108 @@
         lse[rows, :] = jnp.where(first, sums[0], sums[1])
 
 
-def attend_back_kernel(slopes, seg_rows, seg_cols, qkv, grad, mixed, lse, out, distance, dk_acc, dv_acc):
-    group = pl.program_id(0)
+def attend_back_group(group, slopes, qkv, grad, mixed, lse, out, distance, dk_acc, dv_acc):
     length = qkv.shape[1]
-
-    @pl.when(group == 0)
-    def _():
-        fill_distance(seg_rows, seg_cols, distance)
-
+    cols = columns(group * 2 * HD, 2 * HD)
     masks = head_lanes(jnp.bfloat16)
     wide_masks = head_lanes(jnp.float32)
     first = wide_masks[0] > 0.5
     factor = LOG2E / math.sqrt(HD)
     shrink = 1.0 / math.sqrt(HD)
-    keys_t = qkv[1].T
-    values_t = qkv[2].T
+    keys, values = qkv[1, :, cols], qkv[2, :, cols]
+    keys_t = keys.T
+    values_t = values.T
     dk_acc[...] = jnp.zeros_like(dk_acc)
     dv_acc[...] = jnp.zeros_like(dv_acc)
     for start in range(0, length, ROW_BLOCK):
         stop = start + ROW_BLOCK
         rows = slice(start, stop)
-        query, grads = qkv[0, rows, :], grad[rows, :]
+        query, grads, log_sums = qkv[0, rows, cols], grad[rows, cols], lse[rows, cols]
         query_t, grads_t = query.T, grads.T
-        product = grads.astype(jnp.float32) * mixed[rows, :].astype(jnp.float32)
+        product = grads.astype(jnp.float32) * mixed[rows, cols].astype(jnp.float32)
         parts = []
         for head in range(2):
             slope = slopes[2 * group + head] * LOG2E
             lanes = slice(head * HD, (head + 1) * HD)
             scores = jnp.dot(query * masks[head], keys_t[:, :stop], preferred_element_type=jnp.float32)
-            log_sum = lse[rows, head * HD : head * HD + 1]
+            log_sum = log_sums[:, head * HD : head * HD + 1]
             probs = jnp.exp2(scores * factor - slope * distance[rows, :stop] - log_sum)
             grad_probs = jnp.dot(grads * masks[head], values_t[:, :stop], preferred_element_type=jnp.float32)
             inner = jnp.sum(product * wide_masks[head], axis=1, keepdims=True)
             grad_scores = (probs * (grad_probs - inner)).astype(jnp.bfloat16)
-            parts.append(jnp.dot(grad_scores, qkv[1, :stop, :], preferred_element_type=jnp.float32))
+            parts.append(jnp.dot(grad_scores, keys[:stop], preferred_element_type=jnp.float32))
             dk_acc[lanes, :stop] += jnp.dot(query_t[lanes, :], grad_scores, preferred_element_type=jnp.float32)
             dv_acc[lanes, :stop] += jnp.dot(
                 grads_t[lanes, :], probs.astype(jnp.bfloat16), preferred_element_type=jnp.float32
             )
-        out[0, rows, :] = (jnp.where(first, parts[0], parts[1]) * shrink).astype(jnp.bfloat16)
-    out[1] = (dk_acc[...].T * shrink).astype(jnp.bfloat16)
-    out[2] = dv_acc[...].T.astype(jnp.bfloat16)
+        out[0, rows, cols] = (jnp.where(first, parts[0], parts[1]) * shrink).astype(jnp.bfloat16)
+    out[1, :, cols] = (dk_acc[...].T * shrink).astype(jnp.bfloat16)
+    out[2, :, cols] = dv_acc[...].T.astype(jnp.bfloat16)
+
+
+def back_kernel(
+    line, down_ref, up_ref, slopes, seg_rows, seg_cols, qkv, grad, mixed, lse, mlp_home, out, distance, dk_acc, dv_acc, *scratch
+):
+    place = Place()
+    wide = mlp_home.shape[2] // 4
+    groups = []
+    for order, (ref, index, part) in enumerate(((down_ref, 1, 0), (down_ref, 1, 1), (up_ref, 0, 0), (up_ref, 0, 1))):
+        target = mlp_home.at[index : index + 1, :, columns((2 * place.core + part) * wide, wide)]
+        groups.append(
+            GroupSum(place, line, ref.at[part : part + 1], target, scratch[order], line_first=order == 3)
+        )
+    one, two, three, last = groups
+
+    def attend(group):
+        attend_back_group(group, slopes, qkv, grad, mixed, lse, out, distance, dk_acc, dv_acc)
+
+    greet(place, line)
+    one.plane.start()
+    last.load().start()
+    last.load().wait()
+    last.line.step(0)
+    fill_distance(seg_rows, seg_cols, distance)
+    pairs = qkv.shape[2] // (2 * HD)
+
+    def body(group, carry):
+        attend(group)
+        return carry
+
+    lax.fori_loop(0, pairs // 2, body, 0)
+    one.plane.one()
+    two.plane.start()
+    last.line.step(1)
+    lax.fori_loop(pairs // 2, pairs, body, 0)
+    one.plane.two()
+    one.line.step(0)
+    two.plane.one()
+    three.plane.start()
+    for step in range(2, line - 1):
+        last.line.step(step)
+    for step in range(1, line - 1):
+        one.line.step(step)
+    two.plane.two()
+    two.line.step(0)
+    one.line.end()
+    one.home.start()
+    last.line.end()
+    last.plane.start()
+    three.plane.one()
+    for step in range(1, line - 1):
+        two.line.step(step)
+    last.plane.one()
+    three.plane.two()
+    three.line.step(0)
+    two.line.end()
+    two.home.start()
+    last.plane.two()
+    last.home.start()
+    for step in range(1, line - 1):
+        three.line.step(step)
+    three.line.end()
+    three.home.start()
+    for group in groups:
+        group.finish()
 
 
 def attention_specs(length):
@@ -987,40 +1125,60 @@
     )(slopes, seg_ids.reshape(-1, 1), seg_ids.reshape(1, -1), qkv)
 
 
-def attend_back(slopes, seg_ids, qkv, grad, mixed, lse):
+def attend_back(down, up, slopes, seg_ids, qkv, grad, mixed, lse, line):
     _, length, width = qkv.shape
-    rows = pl.BlockSpec((length, 2 * HD), lambda g: (0, g))
+    rows, wide = down.shape[1] // 8, down.shape[2]
+    vmem = pl.BlockSpec(memory_space=pltpu.VMEM)
+    hbm = pl.BlockSpec(memory_space=pl.ANY)
     return pl.pallas_call(
-        attend_back_kernel,
-        grid=(width // (2 * HD),),
-        out_shape=jax.ShapeDtypeStruct(qkv.shape, jnp.bfloat16),
-        in_specs=attention_specs(length) + [rows] * 3,
-        out_specs=pl.BlockSpec((3, length, 2 * HD), lambda g: (0, 0, g)),
+        functools.partial(back_kernel, line),
+        out_shape=[
+            jax.ShapeDtypeStruct((2, rows, 4 * wide // line), jnp.bfloat16),
+            jax.ShapeDtypeStruct(qkv.shape, jnp.bfloat16),
+        ],
+        in_specs=[hbm] * 2 + [pl.BlockSpec(memory_space=pltpu.SMEM)] + [vmem] * 6,
+        out_specs=[hbm, vmem],
         scratch_shapes=[
             pltpu.VMEM((length, length), jnp.float32),
             pltpu.VMEM((2 * HD, length), jnp.float32),
             pltpu.VMEM((2 * HD, length), jnp.float32),
-        ],
-        compiler_params=pltpu.CompilerParams(vmem_limit_bytes=48 * 1024 * 1024),
+        ]
+        + [GroupSum.scratch(1, rows, wide, line, line_first=order == 3) for order in range(4)],
+        compiler_params=pltpu.CompilerParams(
+            collective_id=2, has_side_effects=True, vmem_limit_bytes=56 * 1024 * 1024
+        ),
         name="attend_back",
-    )(slopes, seg_ids.reshape(-1, 1), seg_ids.reshape(1, -1), qkv, grad, mixed, lse)
-
-
-OWNERS = ((0, 0), (3, 0), (1, 3), (2, 3), (0, 1), (3, 2))
-
-
-def newton_kernel(line, attn_ref, mlp_ref, attn_home, mlp_home, thin, full, gram, sent, got, poly, norm_own, norm_got,
-                  home_sem, start_sem, send_sem, back_sem, norm_sem, block_send, block_recv):
+    )(
+        *(each.reshape(2, 2, 2, 2, rows, wide) for each in (down, up)),
+        slopes,
+        seg_ids.reshape(-1, 1),
+        seg_ids.reshape(1, -1),
+        qkv,
+        grad,
+        mixed,
+        lse,
+    )
+
+
+OWNERS = ((1, 0, 0), (1, 0, 3), (0, 1, 0), (0, 1, 3), (0, 0, 1), (1, 1, 2))
+
+
+def finish_kernel(line, out_ref, qkv_ref, vec_ref, mom_ref, mlp_ref, mom_out, vec_out, attn_home, mlp_home, *scratch):
+    (thin, full, gram, sent, got, poly, norm_own, norm_got, attn_sum, attn_ref) = scratch[:10]
+    (home_sem, start_sem, send_sem, back_sem, norm_sem, block_send, block_recv, pass_send, pass_recv) = scratch[10:19]
     place = Place()
-    d, t, core = place.dp, place.tensor, place.core
-    me = d * line + t
+    x, y, t, core = place.x, place.y, place.tensor, place.core
+    me = place.dp * line + t
     devices = 8 * line
-    rows = attn_ref.shape[1]
+    rows = mlp_ref.shape[1]
     narrow, wide = attn_ref.shape[2] // 2, mlp_ref.shape[2] // 2
     barrier = pltpu.get_barrier_semaphore()
 
     def place_of(index):
         return (index // line, lax.rem(index, line))
+
+    def index_of(xs, ys, cores, z):
+        return ((2 * ys + xs) * 2 + cores) * line + z
 
     def meet(step, carry):
         pl.semaphore_signal(
@@ -1031,10 +1189,16 @@
     lax.fori_loop(1, devices, meet, 0)
     pl.semaphore_wait(barrier, devices - 1)
 
-    jobs = []
-    for order, (chip, z) in enumerate(OWNERS):
-        for half in range(2):
-            jobs.append((order, half, (2 * chip + half) * line + min(z, line - 1)))
+    part = attn_ref.shape[2] // 2
+
+    def target_sum(lo, hi):
+        return attn_sum.at[lo:hi, :, columns(core * part, part)]
+
+    sums = (
+        GroupSum(place, line, out_ref, target_sum(3, 4), scratch[23]),
+        GroupSum(place, line, qkv_ref, target_sum(0, 3), scratch[24]),
+    )
+    vector = VectorSum(place, line, scratch[19:23])
 
     def source(order, half):
         if order < 4:
@@ -1053,35 +1217,129 @@
             return attn_home.at[order, :, half * narrow : (half + 1) * narrow]
         return mlp_home.at[order - 4, :, half * wide : (half + 1) * wide]
 
-    def remote(order, half, index):
+    def remote(source_ref, target_ref, send, recv, index):
         return pltpu.make_async_remote_copy(
-            src_ref=source(order, half),
-            dst_ref=held(order, me),
-            send_sem=home_sem.at[order, half],
-            recv_sem=start_sem.at[0],
+            src_ref=source_ref,
+            dst_ref=target_ref,
+            send_sem=send,
+            recv_sem=recv,
             device_id=place_of(index),
             device_id_type=MESH,
         )
 
-    def local(order, half):
+    def owner_of(order, half):
+        ox, oy, oz = OWNERS[order]
+        return index_of(ox, oy, half, oz)
+
+    def collect(order, half):
+        return remote(source(order, half), held(order, me), home_sem.at[order, half], start_sem.at[0], owner_of(order, half))
+
+    def collect_own(order, half):
         return pltpu.make_async_copy(source(order, half), held(order, me), start_sem.at[0])
 
-    for order, half, owner in jobs:
-
-        @pl.when(me == owner)
-        def _():
-            local(order, half).start()
-
-        @pl.when(me != owner)
-        def _():
-            remote(order, half, owner).start()
+    def sides(order):
+        oz = OWNERS[order][2]
+        above, below = list(range(oz + 1, line)), list(range(oz))
+        return (above, below) if len(above) > len(below) else (below, above)
+
+    def is_one_of(value, options):
+        found = value < 0
+        for option in options:
+            found = found | (value == option)
+        return found
+
+    def by_way(order):
+        ox, oy, oz = OWNERS[order]
+        return (y != oy) & (t != oz) & ((x != ox) | is_one_of(t, sides(order)[1]))
+
+    def to_way(order, half):
+        ox, oy, _ = OWNERS[order]
+        which = jnp.where(x == ox, 1, 0)
+        return remote(
+            source(order, half),
+            held(order, me),
+            home_sem.at[order, half],
+            pass_recv.at[which, core],
+            index_of(ox, oy, half, t),
+        )
+
+    def pass_on(order, which, cores):
+        ox, oy, oz = OWNERS[order]
+        region = held(order, index_of(1 - ox if which == 0 else ox, 1 - oy, cores, t))
+        return remote(
+            region, region, pass_send.at[which, cores], start_sem.at[0], index_of(ox, oy, core, oz)
+        )
+
+    def pass_in(order, which, cores):
+        ox, oy, _ = OWNERS[order]
+        index = index_of(1 - ox if which == 0 else ox, 1 - oy, cores, t)
+        region = held(order, index)
+        return remote(region, region, pass_send.at[which, cores], pass_recv.at[which, cores], index)
+
+    def when_passing(order, action):
+        ox, oy, oz = OWNERS[order]
+        here = (x == ox) & (y == oy)
+        far, lone = sides(order)
+        for which, planes in ((0, far + lone), (1, lone)):
+
+            @pl.when(here & is_one_of(t, planes))
+            def _():
+                for cores in range(2):
+                    action(order, which, cores)
+
+    for order in (5, 4):
+        for half in range(2):
+
+            @pl.when(by_way(order))
+            def _():
+                to_way(order, half).start()
+
+            @pl.when((me != owner_of(order, half)) & jnp.logical_not(by_way(order)))
+            def _():
+                collect(order, half).start()
+
+            @pl.when(me == owner_of(order, half))
+            def _():
+                collect_own(order, half).start()
+
+    vector.start(vec_ref[...])
+
+    def forward(order, which, cores):
+        pass_in(order, which, cores).wait_recv()
+        pass_on(order, which, cores).start()
+
+    for order in (5, 4):
+        when_passing(order, forward)
+
+    for order in (4, 5):
+        for half in range(2):
+
+            @pl.when(me != owner_of(order, half))
+            def _():
+                collect(order, half).wait_send()
+
+    for group in sums:
+        group.plane.start()
+    for stage in range(3):
+        vector.step(stage)
 
     def contract_rows(left, right):
         return lax.dot_general(left, right, (((1,), (1,)), ((), ())), preferred_element_type=jnp.float32)
 
-    def orthogonalize(matrix):
+    block = 256
+
+    def swap_block(slot, index):
+        return pltpu.make_async_remote_copy(
+            src_ref=sent.at[index],
+            dst_ref=got.at[slot, index],
+            send_sem=block_send.at[index],
+            recv_sem=block_recv.at[slot, index],
+            device_id=place.twin,
+            device_id_type=MESH,
+        )
+
+    def begin(matrix):
         size, width = matrix.shape
-        block = 256
         pltpu.make_async_copy(matrix, matrix, start_sem.at[0]).wait()
 
         def add_squares(step, total):
@@ -1110,138 +1368,270 @@
             return carry
 
         lax.fori_loop(0, size // 32, scale_rows, 0)
+
+    def iterate(matrix, repeat, part):
+        size, width = matrix.shape
         blocks = size // block
-
-        def swap_block(slot, index):
-            return pltpu.make_async_remote_copy(
-                src_ref=sent.at[index],
-                dst_ref=got.at[slot, index],
-                send_sem=block_send.at[index],
-                recv_sem=block_recv.at[slot, index],
-                device_id=place.twin,
-                device_id_type=MESH,
-            )
-
-        for repeat in range(NS_STEPS):
-            slot = repeat % 2
-
-            def share(index, carry):
-                at = pl.ds(pl.multiple_of(index * block, block), block)
-                sent[index] = contract_rows(matrix[at, :], matrix[...]).astype(jnp.bfloat16)
-                swap_block(slot, index).start()
-                return carry
-
-            lax.fori_loop(0, blocks, share, 0)
-
-            def add(index, carry):
-                at = pl.ds(pl.multiple_of(index * block, block), block)
-                swap_block(slot, index).wait()
-                total = sent[index].astype(jnp.float32) + got[slot, index].astype(jnp.float32)
-                gram[at, :] = total.astype(jnp.bfloat16)
-                return carry
-
-            lax.fori_loop(0, blocks, add, 0)
-
-            def polynomial(index, carry):
-                at = pl.ds(pl.multiple_of(index * block, block), block)
-                square = jnp.dot(gram[at, :], gram[...], preferred_element_type=jnp.float32)
-                poly[at, :] = (coeff_b * gram[at, :].astype(jnp.float32) + coeff_c * square).astype(jnp.bfloat16)
-                return carry
-
-            lax.fori_loop(0, blocks, polynomial, 0)
-
-            def advance(index, carry):
-                at = columns(index * block, block)
-                piece = matrix[:, at]
-                moved = jnp.dot(poly[...], piece, preferred_element_type=jnp.float32)
-                matrix[:, at] = (coeff_a * piece.astype(jnp.float32) + moved).astype(jnp.bfloat16)
-                return carry
-
-            lax.fori_loop(0, width // block, advance, 0)
-
-    def back(order, half, index):
-        return pltpu.make_async_remote_copy(
-            src_ref=held(order, index),
-            dst_ref=target(order, half),
-            send_sem=send_sem.at[0],
-            recv_sem=back_sem.at[order, half],
-            device_id=place_of(index),
-            device_id_type=MESH,
-        )
+        slot = repeat % 2
+        if part == 0:
+            make_gram(matrix, blocks, slot)
+        else:
+            make_next(matrix, blocks, width)
+
+    def make_gram(matrix, blocks, slot):
+
+        def share(index, carry):
+            at = pl.ds(pl.multiple_of(index * block, block), block)
+            sent[index] = contract_rows(matrix[at, :], matrix[...]).astype(jnp.bfloat16)
+            swap_block(slot, index).start()
+            return carry
+
+        lax.fori_loop(0, blocks, share, 0)
+
+        def add(index, carry):
+            at = pl.ds(pl.multiple_of(index * block, block), block)
+            swap_block(slot, index).wait()
+            total = sent[index].astype(jnp.float32) + got[slot, index].astype(jnp.float32)
+            gram[at, :] = total.astype(jnp.bfloat16)
+            return carry
+
+        lax.fori_loop(0, blocks, add, 0)
+
+    def make_next(matrix, blocks, width):
+        def polynomial(index, carry):
+            at = pl.ds(pl.multiple_of(index * block, block), block)
+            square = jnp.dot(gram[at, :], gram[...], preferred_element_type=jnp.float32)
+            poly[at, :] = (coeff_b * gram[at, :].astype(jnp.float32) + coeff_c * square).astype(jnp.bfloat16)
+            return carry
+
+        lax.fori_loop(0, blocks, polynomial, 0)
+
+        def advance(index, carry):
+            at = columns(index * block, block)
+            piece = matrix[:, at]
+            moved = jnp.dot(poly[...], piece, preferred_element_type=jnp.float32)
+            matrix[:, at] = (coeff_a * piece.astype(jnp.float32) + moved).astype(jnp.bfloat16)
+            return carry
+
+        lax.fori_loop(0, width // block, advance, 0)
+
+    def owns(order):
+        ox, oy, oz = OWNERS[order]
+        return (x == ox) & (y == oy) & (t == oz)
+
+    owns_full = owns(4) | owns(5)
+    owns_thin = owns(0) | owns(1) | owns(2) | owns(3)
+
+    def update_attn():
+        for group in sums:
+            group.finish()
+        fresh = 0.5 * mom_ref[...] + attn_sum[...].astype(jnp.float32)
+        mom_out[...] = fresh
+        attn_ref[...] = fresh.astype(jnp.bfloat16)
+        for order in range(4):
+            for half in range(2):
+
+                @pl.when(me == owner_of(order, half))
+                def _():
+                    collect_own(order, half).start()
+
+                @pl.when(me != owner_of(order, half))
+                def _():
+                    collect(order, half).start()
+
+    def between(repeat, part):
+        if repeat == 0 and part == 0:
+            for group in sums:
+                group.plane.two()
+                group.line.step(0)
+        if repeat == 0 and part == 1:
+            for step in range(1, line - 1):
+                for group in sums:
+                    group.line.step(step)
+        if repeat == 1 and part == 0:
+            for group in sums:
+                group.line.end()
+                group.home.start()
+        if repeat == 1 and part == 1:
+            update_attn()
+
+    @pl.when(owns_full)
+    def _():
+        begin(full)
+
+    for group in sums:
+        group.plane.one()
+    vec_out[...] = vector.end()
+    for repeat in range(NS_STEPS):
+        for part in range(2):
+
+            @pl.when(owns_full)
+            def _():
+                iterate(full, repeat, part)
+
+            between(repeat, part)
 
     def keep(order, half):
         return pltpu.make_async_copy(held(order, me), target(order, half), back_sem.at[order, half])
 
-    for kind, orders in ((thin, range(4)), (full, range(4, 6))):
-        owns = functools.reduce(lambda a, b: a | b, [me == owner for order, _, owner in jobs if order in orders])
-
-        @pl.when(owns)
-        def _():
-            orthogonalize(kind)
-
-    for order, half, owner in jobs:
-
-        @pl.when(me == owner)
-        def _():
-            def send(step, carry):
-                back(order, half, lax.rem(me + step, devices)).start()
-                return carry
-
-            keep(order, half).start()
-            lax.fori_loop(1, devices, send, 0)
-
-    for order, half, owner in jobs:
-        keep(order, half).wait()
-
-    for order, half, owner in jobs:
-
-        @pl.when(me == owner)
-        def _():
-            def sent_one(step, carry):
-                back(order, half, lax.rem(me + step, devices)).wait_send()
-                return carry
-
-            lax.fori_loop(1, devices, sent_one, 0)
-
-        @pl.when(me != owner)
-        def _():
-            remote(order, half, owner).wait_send()
-
-
-def newton_schulz(attn_round, mlp_round, line):
-    rows = attn_round.shape[1] * 8
-    narrow, wide = attn_round.shape[2] // 2 * line, mlp_round.shape[2] // 2 * line
+    def back(order, half, index):
+        return remote(held(order, index), target(order, half), send_sem.at[0], back_sem.at[order, half], index)
+
+    def place_in(index):
+        dp, z = place_of(index)
+        return lax.rem(dp // 2, 2), dp // 4, z, lax.rem(dp, 2)
+
+    def one_aside(order, xs, ys):
+        ox, oy, _ = OWNERS[order]
+        return (xs != ox) != (ys != oy)
+
+    def back_by_way(order, index):
+        xs, ys, z, _ = place_in(index)
+        return one_aside(order, xs, ys) & is_one_of(z, sides(order)[0])
+
+    def to_back_way(order, half, index):
+        xs, ys, z, cores = place_in(index)
+        region = held(order, index)
+        first = sides(order)[0][0]
+        return remote(
+            region, region, send_sem.at[0], pass_recv.at[z - first, cores], index_of(xs, ys, half, OWNERS[order][2])
+        )
+
+    def back_in(order, which, cores):
+        index = index_of(x, y, cores, sides(order)[0][which])
+        region = held(order, index)
+        return remote(region, region, pass_send.at[which, cores], pass_recv.at[which, cores], index)
+
+    def back_on(order, half, which, cores):
+        index = index_of(x, y, cores, sides(order)[0][which])
+        return remote(
+            held(order, index), target(order, half), pass_send.at[which, cores], back_sem.at[order, half], index
+        )
+
+    def when_back_way(order, action):
+        for half in range(2):
+
+            @pl.when(one_aside(order, x, y) & (t == OWNERS[order][2]) & (core == half))
+            def _():
+                for which in range(len(sides(order)[0])):
+                    for cores in range(2):
+                        action(order, half, which, cores)
+
+    def each_device(order, half, action, passed):
+        def body(step, carry):
+            index = lax.rem(me + step, devices)
+            if order < 4:
+                action(order, half, index)
+            else:
+
+                @pl.when(back_by_way(order, index) == passed)
+                def _():
+                    action(order, half, index)
+
+            return carry
+
+        lax.fori_loop(1, devices, body, 0)
+
+    def give_back(orders):
+        for order in orders:
+            for half in range(2):
+
+                @pl.when(me == owner_of(order, half))
+                def _():
+                    if order >= 4:
+                        each_device(order, half, lambda *at: to_back_way(*at).start(), True)
+                    each_device(order, half, lambda *at: back(*at).start(), False)
+                    keep(order, half).start()
+
+    give_back((4, 5))
+
+    @pl.when(owns_thin)
+    def _():
+        begin(thin)
+        for repeat in range(NS_STEPS):
+            for part in range(2):
+                iterate(thin, repeat, part)
+
+    give_back(range(4))
+
+    def return_rows(order, half, which, cores):
+        back_in(order, which, cores).wait_recv()
+        back_on(order, half, which, cores).start()
+
+    for order in (4, 5):
+        when_back_way(order, return_rows)
+
+    for order in range(6):
+        for half in range(2):
+            keep(order, half).wait()
+
+            @pl.when(me == owner_of(order, half))
+            def _():
+                if order >= 4:
+                    each_device(order, half, lambda *at: to_back_way(*at).wait_send(), True)
+                each_device(order, half, lambda *at: back(*at).wait_send(), False)
+
+            if order < 4:
+
+                @pl.when(me != owner_of(order, half))
+                def _():
+                    collect(order, half).wait_send()
+
+    for order in (4, 5):
+        when_passing(order, lambda *at: pass_on(*at).wait_send())
+        when_back_way(order, lambda *at: back_on(*at).wait_send())
+
+
+def finish(out, qkv, vec, attn_mom, mlp_round, line):
+    rows = attn_mom.shape[1]
+    size, part = 8 * rows, attn_mom.shape[2] // 2
+    narrow, wide = part * line, mlp_round.shape[2] // 2 * line
     low, dma = jnp.bfloat16, pltpu.SemaphoreType.DMA
+    hbm = pl.BlockSpec(memory_space=pl.ANY)
+    vmem = pl.BlockSpec(memory_space=pltpu.VMEM)
     return pl.pallas_call(
-        functools.partial(newton_kernel, line),
+        functools.partial(finish_kernel, line),
         out_shape=[
-            jax.ShapeDtypeStruct(attn_round.shape, low),
+            jax.ShapeDtypeStruct(attn_mom.shape, jnp.float32),
+            jax.ShapeDtypeStruct(vec.shape, jnp.float32),
+            jax.ShapeDtypeStruct(attn_mom.shape, low),
             jax.ShapeDtypeStruct(mlp_round.shape, low),
         ],
-        in_specs=[pl.BlockSpec(memory_space=pl.ANY)] * 2,
-        out_specs=[pl.BlockSpec(memory_space=pl.ANY)] * 2,
+        in_specs=[hbm, hbm, vmem, vmem, hbm],
+        out_specs=[vmem, vmem, hbm, hbm],
         scratch_shapes=[
-            pltpu.VMEM((rows, narrow), low),
-            pltpu.VMEM((rows, wide), low),
-            pltpu.VMEM((rows, rows), low),
-            pltpu.VMEM((rows // 256, 256, rows), low),
-            pltpu.VMEM((2, rows // 256, 256, rows), low),
-            pltpu.VMEM((rows, rows), low),
+            pltpu.VMEM((size, narrow), low),
+            pltpu.VMEM((size, wide), low),
+            pltpu.VMEM((size, size), low),
+            pltpu.VMEM((size // 256, 256, size), low),
+            pltpu.VMEM((2, size // 256, 256, size), low),
+            pltpu.VMEM((size, size), low),
             pltpu.VMEM((8, 128), jnp.float32),
             pltpu.VMEM((8, 128), jnp.float32),
+            pltpu.VMEM(attn_mom.shape, low),
+            pltpu.VMEM(attn_mom.shape, low),
             dma((6, 2)),
             dma((1,)),
             dma((1,)),
             dma((6, 2)),
             dma((2,)),
-            dma((rows // 256,)),
-            dma((2, rows // 256)),
-        ],
+            dma((size // 256,)),
+            dma((2, size // 256)),
+            dma((2, 2)),
+            dma((2, 2)),
+        ]
+        + VectorSum.scratch(vec.shape, line)
+        + [GroupSum.scratch(count, rows, narrow, line) for count in (1, 3)],
         compiler_params=pltpu.CompilerParams(
-            collective_id=3, has_side_effects=True, vmem_limit_bytes=48 * 1024 * 1024
+            collective_id=3, has_side_effects=True, vmem_limit_bytes=54 * 1024 * 1024
         ),
-        name="newton_schulz",
-    )(attn_round, mlp_round)
+        name="finish",
+    )(
+        *(each.reshape(each.shape[0], 2, 2, 2, rows, narrow) for each in (out, qkv)),
+        vec,
+        attn_mom,
+        mlp_round,
+    )
 
 
 def pair_swap(value):
@@ -1360,7 +1750,10 @@
     grad_mid_low = grad_middle.astype(jnp.bfloat16)
     grad_out = contract_first(grad_mid_low, mixed)
     grad_mixed = jnp.dot(grad_mid_low, wout, preferred_element_type=jnp.float32).astype(jnp.bfloat16)
-    grad_qkv = attend_back(slopes, seg_ids, qkv, grad_mixed, mixed, log_sums)
+    low = jnp.bfloat16
+    mlp_sum, grad_qkv = attend_back(
+        grad_down.astype(low), grad_up.astype(low), slopes, seg_ids, qkv, grad_mixed, mixed, log_sums, line
+    )
     grad_proj = jnp.einsum("td,mtc->mdc", normed, grad_qkv, preferred_element_type=jnp.float32)
     bias_sums = jnp.sum(grad_qkv, axis=1, dtype=jnp.float32)
     normed_part = jnp.einsum("mtc,mdc->td", grad_qkv, wqkv, preferred_element_type=jnp.float32)
@@ -1390,19 +1783,16 @@
     )
     vector_local = jnp.concatenate([vector_rows, hidden_grad.reshape(-1, width)], axis=0)
     padding = jnp.zeros((4, width), jnp.float32)
-    low = jnp.bfloat16
-    attn_sum, mlp_sum, vector_sum = sum_gradients(
-        grad_down.astype(low),
-        grad_up.astype(low),
+    mlp_mom_new = 0.5 * mlp_mom + mlp_sum.astype(jnp.float32)
+    attn_mom_new, vector_sum, attn_ortho, mlp_ortho = finish(
         grad_out.astype(low)[None],
         grad_proj.astype(low),
         jnp.concatenate([vector_local, padding], axis=0),
+        attn_mom,
+        mlp_mom_new.astype(low),
         line,
     )
     vector_grads = vector_sum[: vector_local.shape[0]]
-    attn_mom_new = 0.5 * attn_mom + attn_sum.astype(jnp.float32)
-    mlp_mom_new = 0.5 * mlp_mom + mlp_sum.astype(jnp.float32)
-    attn_ortho, mlp_ortho = newton_schulz(attn_mom_new.astype(low), mlp_mom_new.astype(low), line)
     attn_new = attn_w - attn_ortho.astype(jnp.float32)
     mlp_new = mlp_w - math.sqrt(FF / D) * mlp_ortho.astype(jnp.float32)
     vector_mom_new = 0.5 * vector_mom + vector_grads

time: 689 us -> 568 us (0.82)
  the two profiles are of different devices: /device:TPU:31 before, /device:TPU:0 now
where the time goes in v2:
time: 568 us; the launch traced here: 558 us
  Pallas kernels  399 us (70%)
  matrix products  69.7 us (12%)
  other arithmetic  35 us (6%)
  starting transfers between devices  25.6 us (5%)
  local copies, waits for them, and re-layouts  23.1 us (4%)
    pallas_call x1, Pallas kernels, finish(): pl.pallas_call(functools.partial(finish_kernel, line), out_shape=[jax.Sha...  179 us
    pallas_call x1, Pallas kernels, gather_weights(): pl.pallas_call(functools.partial(gather_kernel, line), out_shape=[jax.Sha...  114 us
    pallas_call x1, Pallas kernels, attend_back(): pl.pallas_call(functools.partial(back_kernel, line), out_shape=[jax.Shape...  88.6 us
    ppermute x7, starting transfers between devices, pair_swap(): return lax.ppermute(value, ('dp', 'tensor'), pairs)  18.8 us
    pallas_call x1, Pallas kernels, attend(): pl.pallas_call(attend_kernel, grid=(width // (2 * HD),), out_shape=[jax.S...  17.2 us
    unnamed x91, local copies, waits for them, and re-layouts  14 us
  transfers between devices with their start and end apart: 11, of which 1 were waited for; matrix products, arithmetic and copies ran while one was open for 15% of the time, Pallas kernels for 72%

profile of v2, /device:TPU:0, one launch (start us, length us, event | category | flops | bytes accessed | tf_op | source)
XLA Modules:
  0.0 557.6 jit_solution(15269183416063104974)
XLA Ops:
  5.3 16.0 %collective-permute-start.1 = (bf16[512,1024]{0,1:T(8,128)(2,1)S(1)}, bf16[512,1024]{0,1:T(8,128)(2,1)}, u32[]{:S(2)}, u32[]{:S(2)}) collective-permute-start(bf16[512,1024]{0,1:T(8,128)(2,1)S(1)} %broadcast_select_fusion.6), channel_id=1, source_target_pairs={{0,4},{1,5},{2,6},{3,7},{4,0},{5,1},{6,2},{7,3},{8,12},{9,13},{10,... | collective-permute-start | bytes 3145736 | tf_op jit(solution)/shard_map/ppermute | solution.py:1640
  21.5 2.3 copy.44
  27.3 114.4 %gather_weights.1 = (bf16[3,2,2,2,128,512]{5,4,3,2,1,0:T(8,128)(2,1)}, bf16[1,2,2,2,128,512]{5,4,3,2,1,0:T(8,128)(2,1)}, bf16[2,2,2,2,128,1024]{5,4,3,2,1,0:T(8,128)(2,1)}, bf16[2,2,2,2,128,1024]{5,4,3,2,1,0:T(8,128)(2,1)}) custom-call(bf16[4,128,256]{2,1,0:T(8,128)(2,1)} %convert_element_type.127.attn_ref, bf16[2,128,1024]{2,1,0:T(8,128)(2,1)} %convert_element_type.128.mlp_ref), custom_call_target="tpu_custom_call" | custom-call | tf_op jit(solution)/shard_map/gather_weights/pallas_call | solution.py:618
  144.6 5.4 fusion.15.qkv
  150.0 17.2 %attend.1 = (bf16[1024,512]{1,0:T(8,128)(2,1)S(1)}, f32[1024,512]{1,0:T(8,128)S(1)}) custom-call(f32[8]{0:T(128)S(1)} %fusion.37.slopes, s32[1024,1]{1,0:T(8,128)S(1)} %copy.39.seg_rows, s32[1,1024]{1,0:T(1,128)S(1)} %bitcast.123, bf16[3,1024,512]{2,1,0:T(8,128)(2,1)} %fusion.15.qkv), custom_call_target="tpu_custom_call" | custom-call | tf_op jit(solution)/shard_map/attend/pallas_call | solution.py:1113
  167.3 2.6 convolution_convert_fusion.2
  172.8 3.0 collective-permute-done.7
  178.1 4.8 fusion.45
  184.9 3.2 copy-done.35
  188.1 5.0 fusion.29
  193.1 6.0 %bitcast_convert_fusion.2 = bf16[1024,1024]{0,1:T(8,128)(2,1)} fusion(bf16[2,1024,1024]{2,1,0:T(8,128)(2,1)S(1)} %bitcast.161, f32[2,1024,1024]{1,2,0:T(8,128)S(1)} %fusion.29, f32[2,1024]{1,0:T(2,128)S(1)} %bitcast.151), kind=kOutput, calls=%fused_computation.28 | convolution fusion | flops 4316987392 | bytes 14688256 | tf_op jit(solution)/shard_map/stc,sdc->td/dot_general | solution.py:1738
  199.1 10.6 %convert_reduce_fusion = (f32[2,1024]{1,0:T(2,128)S(1)}, bf16[2,1024,1024]{2,1,0:T(8,128)(2,1)S(1)}) fusion(f32[2,1024,1024]{1,2,0:T(8,128)S(1)} %fusion.29, f32[2,1024]{1,0:T(2,128)S(1)} %bitcast.152, bf16[2,1024,1024]{2,1,0:T(8,128)(2,1)S(1)} %bitcast.162, bf16[512,1024]{0,1:T(8,128)(2,1)S(1)} %get-tuple-element.67, ...), kind=kOutput, calls=%fused_computation.16 | convolution fusion | flops 4347394048 | bytes 18890752 | tf_op jit(solution)/shard_map/td,sdc->stc/dot_general | solution.py:1743
  209.7 5.9 %bitcast_convert_fusion.1 = bf16[1024,1024]{0,1:T(8,128)(2,1)} fusion(bf16[2,1024,1024]{2,1,0:T(8,128)(2,1)S(1)} %get-tuple-element.81, bf16[2,1024,1024]{2,1,0:T(8,128)(2,1)S(1)} %bitcast.160), kind=kOutput, calls=%fused_computation.27 | convolution fusion | flops 4296015872 | bytes 10485760 | tf_op jit(solution)/shard_map/stc,sdc->td/dot_general | solution.py:1747
  217.6 10.9 %convolution_convert_fusion.1 = bf16[2,1024,1024]{1,2,0:T(8,128)(2,1)} fusion(bf16[512,1024]{0,1:T(8,128)(2,1)} %copy-done.13, bf16[512,1024]{0,1:T(8,128)(2,1)} %copy-done.11, f32[2,1024,1024]{1,2,0:T(8,128)} %copy-done.40, f32[2,1024]{1,0:T(2,128)S(1)} %bitcast.153), kind=kOutput, calls=%fused_computation.40 | convolution fusion | flops 4322230272 | bytes 14688256 | tf_op jit(solution)/shard_map/td,stc->sdc/dot_general | solution.py:1742
  228.6 6.5 %convolution_convert_fusion = bf16[2,1024,1024]{1,2,0:T(8,128)(2,1)} fusion(bf16[2,1024,1024]{2,1,0:T(8,128)(2,1)S(1)} %copy-done.42, f32[1024,1024]{0,1:T(8,128)S(1)} %copy-done.16, f32[1024]{0:T(1024)S(1)} %bitcast.158, f32[1024]{0:T(1024)S(1)} %bitcast.130), kind=kOutput, calls=%fused_computation.39 | convolution fusion | flops 4300210176 | bytes 12591104 | tf_op jit(solution)/shard_map/td,stc->sdc/dot_general | solution.py:1745
  239.6 2.7 multiply_add_fusion
  242.4 2.3 convolution_convert_fusion.4.grad
  247.0 88.6 %attend_back.1 = (bf16[2,128,1024]{2,1,0:T(8,128)(2,1)}, bf16[3,1024,512]{2,1,0:T(8,128)(2,1)}) custom-call(bf16[2,2,2,2,128,1024]{5,4,3,2,1,0:T(8,128)(2,1)} %bitcast.126, bf16[2,2,2,2,128,1024]{5,4,3,2,1,0:T(8,128)(2,1)} %bitcast.127, f32[8]{0:T(128)} %copy-done.4, s32[1024,1]{1,0:T(8,128)} %copy-done, s32[1,1024]{1,0:T(1,128)} %bitcast.124, ...), custom_call_target="tpu_custom_call" | custom-call | tf_op jit(solution)/shard_map/attend_back/pallas_call | solution.py:1133
  335.6 6.4 %bitcast_convert_fusion = bf16[1024,1024]{0,1:T(8,128)(2,1)S(1)} fusion(bf16[3,1024,512]{2,1,0:T(8,128)(2,1)} %get-tuple-element.26, bf16[3,1024,512]{2,1,0:T(8,128)(2,1)} %bitcast.163), kind=kOutput, calls=%fused_computation.26 | convolution fusion | flops 3222274048 | bytes 8388608 | tf_op jit(solution)/shard_map/mtc,mdc->td/dot_general | solution.py:1759
  345.9 5.8 %convert_bitcast_fusion = bf16[3,1024,512]{1,2,0:T(8,128)(2,1)} fusion(bf16[3,1024,512]{2,1,0:T(8,128)(2,1)S(1)} %copy-done.26, f32[1024]{0:T(1024)S(1)} %bitcast.156, f32[1024]{0:T(1024)S(1)} %bitcast.134, f32[1024]{0:T(1024)S(1)} %add_rsqrt_fusion.1, f32[1024]{0:T(1024)S(1)} %broadcast_multiply_fusion.3, bf16[512,1024]{0,1:T(8,128)(2,1)S(1)} %copy-done.8, ...), kind=kOutput, calls=%fused_computation.38 | convolution fusion | flops 3232235520 | bytes 8404992 | tf_op jit(solution)/shard_map/td,mtc->mdc/dot_general | solution.py:1757
  352.2 4.8 copy.51
  357.1 2.9 multiply_reduce_fusion.4
  360.3 2.8 dynamic-slice_reduce_fusion.1
  368.7 179.2 %finish.1 = (f32[4,128,256]{2,1,0:T(8,128)}, f32[16,1024]{1,0:T(8,128)}, bf16[4,128,256]{2,1,0:T(8,128)(2,1)}, bf16[2,128,1024]{2,1,0:T(8,128)(2,1)}) custom-call(bf16[1,2,2,2,128,512]{5,4,3,2,1,0:T(8,128)(2,1)} %bitcast.128, bf16[3,2,2,2,128,512]{5,4,3,2,1,0:T(8,128)(2,1)} %bitcast.125, f32[16,1024]{1,0:T(8,128)} %concatenate.11.vec_ref, ...), custom_call_target="tpu_custom_call" | custom-call | tf_op jit(solution)/shard_map/finish/pallas_call | solution.py:1592
  (165 shorter events, 46.5 us)
Async XLA Ops:
  0.6 20.7 %copy-start.34 = (s32[2048]{0:T(1024)S(1)}, s32[2048]{0:T(1024)}, u32[]{:S(2)}) copy-start(s32[2048]{0:T(1024)} %param.11) | copy-start | bytes 24580
  0.6 24.9 %copy-start.32 = (f32[12,1024]{1,0:T(8,128)S(1)}, f32[12,1024]{1,0:T(8,128)}, u32[]{:S(2)}) copy-start(f32[12,1024]{1,0:T(8,128)} %param.14) | copy-start | bytes 147460
  0.7 25.0 %copy-start.28 = (f32[4,128,256]{2,1,0:T(8,128)S(1)}, f32[4,128,256]{2,1,0:T(8,128)}, u32[]{:S(2)}) copy-start(f32[4,128,256]{2,1,0:T(8,128)} %param.12) | copy-start | bytes 1572868
  0.7 25.7 %copy-start.22 = (f32[2,128,1024]{2,1,0:T(8,128)S(1)}, f32[2,128,1024]{2,1,0:T(8,128)}, u32[]{:S(2)}) copy-start(f32[2,128,1024]{2,1,0:T(8,128)} %param.13) | copy-start | bytes 3145732
  2.3 1.7 collective-permute-start
  5.3 136.6 %collective-permute-start.1 = (bf16[512,1024]{0,1:T(8,128)(2,1)S(1)}, bf16[512,1024]{0,1:T(8,128)(2,1)}, u32[]{:S(2)}, u32[]{:S(2)}) collective-permute-start(bf16[512,1024]{0,1:T(8,128)(2,1)S(1)} %broadcast_select_fusion.6), channel_id=1, source_target_pairs={{0,4},{1,5},{2,6},{3,7},{4,0},{5,1},{6,2},{7,3},{8,12},{9,13},{10,... | collective-permute-start | bytes 3145736 | tf_op jit(solution)/shard_map/ppermute | solution.py:1640
  21.4 120.3 %collective-permute-start.2 = (s32[1024]{0:T(1024)S(1)}, s32[1024]{0:T(1024)S(1)}, u32[]{:S(2)}, u32[]{:S(2)}) collective-permute-start(s32[1024]{0:T(1024)S(1)} %bitcast.141), channel_id=1, source_target_pairs={{0,4},{1,5},{2,6},{3,7},{4,0},{5,1},{6,2},{7,3},{8,12},{9,13},{10,... | collective-permute-start | bytes 12296 | tf_op jit(solution)/shard_map/ppermute | solution.py:1640
  23.8 146.1 %collective-permute-start.6 = (bf16[512,1024]{0,1:T(8,128)(2,1)}, bf16[512,1024]{0,1:T(8,128)(2,1)}, u32[]{:S(2)}, u32[]{:S(2)}) collective-permute-start(bf16[512,1024]{0,1:T(8,128)(2,1)} %copy.44), channel_id=1, source_target_pairs={{4,1},{1,4},{6,3},{3,6},{12,9},{9,12},{14,11},{11,14},{20,17},{17,... | collective-permute-start | bytes 3145736 | tf_op jit(solution)/shard_map/ppermute | solution.py:1649
  25.6 124.3 %copy-start.4 = (f32[8]{0:T(128)}, f32[8]{0:T(128)S(1)}, u32[]{:S(2)}) copy-start(f32[8]{0:T(128)S(1)} %fusion.37.slopes) | copy-start | bytes 100
  144.6 22.7 %copy-start.38 = (bf16[1,2,2,2,128,512]{5,4,3,2,1,0:T(8,128)(2,1)S(1)}, bf16[1,2,2,2,128,512]{5,4,3,2,1,0:T(8,128)(2,1)}, u32[]{:S(2)}) copy-start(bf16[1,2,2,2,128,512]{5,4,3,2,1,0:T(8,128)(2,1)} %get-tuple-element.22) | copy-start | bytes 3145732
  167.2 77.5 %copy-start.2 = (bf16[1024,512]{1,0:T(8,128)(2,1)}, bf16[1024,512]{1,0:T(8,128)(2,1)S(1)}, u32[]{:S(2)}) copy-start(bf16[1024,512]{1,0:T(8,128)(2,1)S(1)} %get-tuple-element.21.mixed) | copy-start | bytes 3145732
  169.9 8.2 %collective-permute-start.3 = (bf16[1024,1024]{0,1:T(8,128)(2,1)}, bf16[1024,1024]{0,1:T(8,128)(2,1)}, u32[]{:S(2)}, u32[]{:S(2)}) collective-permute-start(bf16[1024,1024]{0,1:T(8,128)(2,1)} %convolution_convert_fusion.2), channel_id=1, source_target_pairs={{0,4},{1,5},{2,6},{3,7},{4,0},{5,1},{6,2},{7,3},{8,12},{9,13},{10,... | collective-permute-start | bytes 6291464 | tf_op jit(solution)/shard_map/ppermute | solution.py:1640
  171.0 4.9 collective-permute-start.7
  177.5 21.5 %copy-start.11 = (bf16[512,1024]{0,1:T(8,128)(2,1)}, bf16[512,1024]{0,1:T(8,128)(2,1)S(1)}, u32[]{:S(2)}) copy-start(bf16[512,1024]{0,1:T(8,128)(2,1)S(1)} %get-tuple-element.66) | copy-start | bytes 3145732
  177.6 21.5 %copy-start.13 = (bf16[512,1024]{0,1:T(8,128)(2,1)}, bf16[512,1024]{0,1:T(8,128)(2,1)S(1)}, u32[]{:S(2)}) copy-start(bf16[512,1024]{0,1:T(8,128)(2,1)S(1)} %get-tuple-element.67) | copy-start | bytes 3145732
  217.0 11.5 %copy-start.16 = (f32[1024,1024]{0,1:T(8,128)S(1)}, f32[1024,1024]{0,1:T(8,128)}, u32[]{:S(2)}) copy-start(f32[1024,1024]{0,1:T(8,128)} %copy-done.15) | copy-start | bytes 12582916
  217.0 18.0 %collective-permute-start.4 = (bf16[512,1024]{0,1:T(8,128)(2,1)S(1)}, bf16[512,1024]{0,1:T(8,128)(2,1)S(1)}, u32[]{:S(2)}, u32[]{:S(2)}) collective-permute-start(bf16[512,1024]{0,1:T(8,128)(2,1)S(1)} %constant_dynamic-slice_fusion.1), channel_id=1, source_target_pairs={{0,4},{1,5},{2,6},{3,7},{4,0},{5,1},{6,2},{7,3},{8,12},{9,13},{10,... | collective-permute-start | bytes 3145736 | tf_op jit(solution)/shard_map/ppermute | solution.py:1640
  217.2 21.0 %collective-permute-start.8 = (bf16[1024,1024]{0,1:T(8,128)(2,1)}, bf16[1024,1024]{0,1:T(8,128)(2,1)S(1)}, u32[]{:S(2)}, u32[]{:S(2)}) collective-permute-start(bf16[1024,1024]{0,1:T(8,128)(2,1)} %bitcast_convert_fusion.1), channel_id=1, source_target_pairs={{0,4},{1,5},{2,6},{3,7},{4,0},{5,1},{6,2},{7,3},{8,12},{9,13},{10,... | collective-permute-start | bytes 6291464 | tf_op jit(solution)/shard_map/ppermute | solution.py:1640
  236.4 128.3 %collective-permute-start.5 = (bf16[512,1024]{0,1:T(8,128)(2,1)}, bf16[512,1024]{0,1:T(8,128)(2,1)}, u32[]{:S(2)}, u32[]{:S(2)}) collective-permute-start(bf16[512,1024]{0,1:T(8,128)(2,1)} %add_convert_fusion.4), channel_id=1, source_target_pairs={{4,1},{1,4},{6,3},{3,6},{12,9},{9,12},{14,11},{11,14},{20,17},{17,... | collective-permute-start | bytes 3145736 | tf_op jit(solution)/shard_map/ppermute | solution.py:1649
  343.6 13.4 %collective-permute-start.9 = (bf16[512,1024]{0,1:T(8,128)(2,1)}, bf16[512,1024]{0,1:T(8,128)(2,1)S(1)}, u32[]{:S(2)}, u32[]{:S(2)}) collective-permute-start(bf16[512,1024]{0,1:T(8,128)(2,1)} %constant_dynamic-slice_fusion), channel_id=1, source_target_pairs={{0,4},{1,5},{2,6},{3,7},{4,0},{5,1},{6,2},{7,3},{8,12},{9,13},{10,... | collective-permute-start | bytes 3145736 | tf_op jit(solution)/shard_map/ppermute | solution.py:1640
  363.0 190.3 %collective-permute-start.10 = (bf16[512,1024]{0,1:T(8,128)(2,1)S(1)}, bf16[512,1024]{0,1:T(8,128)(2,1)}, u32[]{:S(2)}, u32[]{:S(2)}) collective-permute-start(bf16[512,1024]{0,1:T(8,128)(2,1)S(1)} %get-tuple-element.64), channel_id=1, source_target_pairs={{4,1},{1,4},{6,3},{3,6},{12,9},{9,12},{14,11},{11,14},{20,17},{17,... | collective-permute-start | bytes 3145736 | tf_op jit(solution)/shard_map/ppermute | solution.py:1649
  366.1 181.8 %copy-start.33 = (f32[12,1024]{1,0:T(8,128)S(1)}, f32[12,1024]{1,0:T(8,128)}, u32[]{:S(2)}) copy-start(f32[12,1024]{1,0:T(8,128)} %param.17) | copy-start | bytes 147460
  366.1 185.1 %copy-start.23 = (f32[2,128,1024]{2,1,0:T(8,128)S(1)}, f32[2,128,1024]{2,1,0:T(8,128)}, u32[]{:S(2)}) copy-start(f32[2,128,1024]{2,1,0:T(8,128)} %param.13) | copy-start | bytes 3145732
  367.4 182.0 %copy-start.29 = (f32[4,128,256]{2,1,0:T(8,128)S(1)}, f32[4,128,256]{2,1,0:T(8,128)}, u32[]{:S(2)}) copy-start(f32[4,128,256]{2,1,0:T(8,128)} %param.12) | copy-start | bytes 1572868
  (31 other events, 149.8 us)

commit v3 on v2

--- a/solution.py
+++ b/solution.py
@@ -398,6 +398,8 @@
         self.across_y = (self.dp + 4 - 8 * self.y, self.tensor)
         self.right = (self.dp, self.tensor + 1)
         self.left = (self.dp, self.tensor - 1)
+        self.stays = self.core == lax.rem(self.tensor, 2)
+        self.corner = (self.dp + 1 - 2 * self.core, self.tensor - 1 + 2 * self.core)
 
 
 def greet(place, line):
@@ -416,221 +418,212 @@
         def _():
             signal((place.dp, other))
 
-    pl.semaphore_wait(barrier, 3 + line - 1)
+    @pl.when(jnp.logical_not(place.stays))
+    def _():
+        signal(place.corner)
+
+    pl.semaphore_wait(barrier, jnp.where(place.stays, 3 + line - 1, 3 + line))
 
 
 def columns(start, size):
     return pl.ds(pl.multiple_of(start, 128), size)
 
 
-def gather_kernel(line, attn_ref, mlp_ref, qkv_ref, out_ref, up_ref, down_ref, own_sem, send_sem, recv_sem):
-    place = Place()
-    x, y, t = place.x, place.y, place.tensor
-    narrow = attn_ref.shape[2] // 2
-    wide = mlp_ref.shape[2] // 4
-
-    def attn_source(lo, hi):
-        return lambda core: attn_ref.at[lo:hi, :, columns(core * narrow, narrow)]
-
-    def mlp_source(index, part):
-        return lambda core: mlp_ref.at[index : index + 1, :, columns((2 * core + part) * wide, wide)]
-
-    groups = [
-        (qkv_ref, narrow, attn_source(0, 3)),
-        (out_ref, narrow, attn_source(3, 4)),
-        (up_ref.at[0:1], wide, mlp_source(0, 0)),
-        (up_ref.at[1:2], wide, mlp_source(0, 1)),
-        (down_ref.at[0:1], wide, mlp_source(1, 0)),
-        (down_ref.at[1:2], wide, mlp_source(1, 1)),
-    ]
-    greet(place, line)
-
-    def copy(group, slot, source, target, device):
+class RowSwap:
+    SCRATCH = 2
+
+    @staticmethod
+    def scratch():
+        return [pltpu.SemaphoreType.DMA((1,)), pltpu.SemaphoreType.DMA((4,))]
+
+    def __init__(self, place, rows_ref, whole_ref, scratch):
+        self.place, self.rows_ref, self.whole_ref = place, rows_ref, whole_ref
+        self.own_sem, self.sem = scratch
+        self.size = rows_ref.shape[0]
+
+    def at(self, core):
+        return self.whole_ref.at[pl.ds(pl.multiple_of(core * self.size, self.size), self.size), :]
+
+    def copy(self, slot, source, target, device):
         return pltpu.make_async_remote_copy(
             src_ref=source,
             dst_ref=target,
-            send_sem=send_sem.at[group, slot],
-            recv_sem=recv_sem.at[group, slot],
+            send_sem=self.sem.at[slot],
+            recv_sem=self.sem.at[slot + 1],
             device_id=device,
             device_id_type=MESH,
         )
 
-    def same(group, slot, region, device):
-        return copy(group, slot, region, region, device)
-
-    def chunk(group, index):
-        ref, width, _ = groups[group]
-        return ref.at[:, y, x, :, :, columns(index * width, width)]
-
-    def corner(group, ys, xs, half):
-        return groups[group][0].at[:, ys, xs, half]
-
-    def entry(group, half):
-        ref, width, _ = groups[group]
-        return ref.at[:, y, x, half, :, columns(t * width, width)]
-
-    both = pl.ds(0, 2)
-    last = len(groups) - 1
-    to_right, to_left, half_x, half_y, rest_y, rest_x = 1, line, 2 * line - 1, 2 * line, 2 * line + 1, 2 * line + 2
-
-    def chunk(group, index):
-        ref, width, _ = groups[group]
+    def own(self):
+        return pltpu.make_async_copy(self.rows_ref, self.at(self.place.core), self.own_sem.at[0])
+
+    def away(self):
+        return self.copy(0, self.rows_ref, self.at(1 - self.place.core), self.place.corner)
+
+    def hand_own(self):
+        return self.copy(2, self.rows_ref, self.at(self.place.core), self.place.twin)
+
+    def hand_got(self):
+        return self.copy(2, self.at(self.place.core), self.at(self.place.core), self.place.twin)
+
+    def start(self):
+        @pl.when(self.place.stays)
+        def _():
+            self.own().start()
+            self.hand_own().start()
+
+        @pl.when(jnp.logical_not(self.place.stays))
+        def _():
+            self.away().start()
+
+    def step(self):
+        @pl.when(jnp.logical_not(self.place.stays))
+        def _():
+            self.away().wait()
+            self.hand_got().start()
+
+    def end(self):
+        @pl.when(self.place.stays)
+        def _():
+            self.own().wait()
+
+        self.hand_got().wait()
+
+
+class WeightGather:
+    def __init__(self, place, line, groups, scratch):
+        self.place, self.line, self.groups = place, line, groups
+        self.own_sem, self.send_sem, self.recv_sem = scratch
+        self.last = len(groups) - 1
+        self.to_right, self.to_left = 1, line
+        self.half_x, self.half_y, self.rest_y, self.rest_x = (2 * line - 1 + k for k in range(4))
+
+    @staticmethod
+    def scratch(count, line):
+        dma = pltpu.SemaphoreType.DMA
+        return [dma((count,)), dma((count, 2 * line + 3)), dma((count, 2 * line + 3))]
+
+    def copy(self, group, slot, source, target, device):
+        return pltpu.make_async_remote_copy(
+            src_ref=source,
+            dst_ref=target,
+            send_sem=self.send_sem.at[group, slot],
+            recv_sem=self.recv_sem.at[group, slot],
+            device_id=device,
+            device_id_type=MESH,
+        )
+
+    def same(self, group, slot, region, device):
+        return self.copy(group, slot, region, region, device)
+
+    def chunk(self, group, index):
+        ref, width, _ = self.groups[group]
         cols = columns(index * width, width)
-        if group == last:
+        if group == self.last:
             return ref.at[:, :, :, :, :, cols]
-        return ref.at[:, y, x, :, :, cols]
-
-    def corner(group, ys, xs, half):
-        ref, width, _ = groups[group]
-        if group == last:
-            return ref.at[:, ys, xs, half, :, columns(t * width, width)]
+        return ref.at[:, self.place.y, self.place.x, :, :, cols]
+
+    def corner(self, group, ys, xs, half):
+        ref, width, _ = self.groups[group]
+        if group == self.last:
+            return ref.at[:, ys, xs, half, :, columns(self.place.tensor * width, width)]
         return ref.at[:, ys, xs, half]
 
-    def entry(group, half):
-        ref, width, _ = groups[group]
-        return ref.at[:, y, x, half, :, columns(t * width, width)]
-
-    def own(group):
-        return pltpu.make_async_copy(
-            groups[group][2](place.core), entry(group, place.core), own_sem.at[group]
-        )
-
-    def first(group):
-        target = entry(group, place.core)
-        return copy(group, 0, groups[group][2](1 - place.core), target, place.twin)
-
-    def enter(group):
-        own(group).wait()
-        same(group, 0, entry(group, 1 - place.core), place.twin).wait_recv()
-
-    def line_start(group):
-        @pl.when(t < line - 1)
-        def _():
-            same(group, to_right, chunk(group, t), place.right).start()
-
-        @pl.when(t > 0)
-        def _():
-            same(group, to_left, chunk(group, t), place.left).start()
-
-    def line_step(group, step):
-        @pl.when(t >= step)
-        def _():
-            same(group, to_right + step - 1, chunk(group, t - step), place.left).wait_recv()
+    def entry(self, group, half):
+        ref, width, _ = self.groups[group]
+        return ref.at[:, self.place.y, self.place.x, half, :, columns(self.place.tensor * width, width)]
+
+    def own(self, group):
+        core = self.place.core
+        return pltpu.make_async_copy(self.groups[group][2](core), self.entry(group, core), self.own_sem.at[group])
+
+    def first(self, group):
+        core = self.place.core
+        return self.copy(group, 0, self.groups[group][2](1 - core), self.entry(group, core), self.place.twin)
+
+    def begin(self, group):
+        self.own(group).start()
+        self.first(group).start()
+
+    def enter(self, group):
+        self.own(group).wait()
+        self.same(group, 0, self.entry(group, 1 - self.place.core), self.place.twin).wait_recv()
+
+    def hop(self, group, step, left):
+        t = self.place.tensor
+        index = t + step - 1 if left else t - step + 1
+        slot = (self.to_left if left else self.to_right) + step - 1
+        return self.same(group, slot, self.chunk(group, index), self.place.left if left else self.place.right)
+
+    def arrival(self, group, step, left):
+        t = self.place.tensor
+        index = t + step if left else t - step
+        slot = (self.to_left if left else self.to_right) + step - 1
+        return self.same(group, slot, self.chunk(group, index), self.place.right if left else self.place.left)
+
+    def sends(self, step, left):
+        t, line = self.place.tensor, self.line
+        return (t > 0) & (t + step <= line) if left else (t < line - 1) & (t >= step - 1)
+
+    def line_start(self, group):
+        for left in (False, True):
+
+            @pl.when(self.sends(1, left))
+            def _():
+                self.hop(group, 1, left).start()
+
+    def line_step(self, group, step):
+        t, line = self.place.tensor, self.line
+        for left in (False, True):
+
+            @pl.when(t + step <= line - 1 if left else t >= step)
+            def _():
+                self.arrival(group, step, left).wait_recv()
+
             if step < line - 1:
 
-                @pl.when(t < line - 1)
+                @pl.when(self.sends(step + 1, left))
                 def _():
-                    same(group, to_right + step, chunk(group, t - step), place.right).start()
-
-        @pl.when(t + step <= line - 1)
-        def _():
-            same(group, to_left + step - 1, chunk(group, t + step), place.right).wait_recv()
-            if step < line - 1:
-
-                @pl.when(t > 0)
+                    self.hop(group, step + 1, left).start()
+
+    def line_most(self, group):
+        for step in range(1, self.line - 1):
+            self.line_step(group, step)
+
+    def line_end(self, group):
+        self.line_step(group, self.line - 1)
+
+    def plane_start(self, group):
+        place = self.place
+        self.same(group, self.half_x, self.corner(group, place.y, place.x, 0), place.across_x).start()
+        self.same(group, self.half_y, self.corner(group, place.y, place.x, 1), place.across_y).start()
+
+    def plane_step(self, group):
+        place, both = self.place, pl.ds(0, 2)
+        self.same(group, self.half_x, self.corner(group, place.y, 1 - place.x, 0), place.across_x).wait_recv()
+        self.same(group, self.rest_y, self.corner(group, place.y, both, 0), place.across_y).start()
+        self.same(group, self.half_y, self.corner(group, 1 - place.y, place.x, 1), place.across_y).wait_recv()
+        self.same(group, self.rest_x, self.corner(group, both, place.x, 1), place.across_x).start()
+
+    def plane_end(self, group):
+        place, both = self.place, pl.ds(0, 2)
+        self.same(group, self.rest_y, self.corner(group, 1 - place.y, both, 0), place.across_y).wait_recv()
+        self.same(group, self.rest_x, self.corner(group, both, 1 - place.x, 1), place.across_x).wait_recv()
+
+    def wait_sends(self, group):
+        place, both = self.place, pl.ds(0, 2)
+        self.first(group).wait_send()
+        for step in range(1, self.line):
+            for left in (False, True):
+
+                @pl.when(self.sends(step, left))
                 def _():
-                    same(group, to_left + step, chunk(group, t + step), place.left).start()
-
-    def plane_start(group):
-        same(group, half_x, corner(group, y, x, 0), place.across_x).start()
-        same(group, half_y, corner(group, y, x, 1), place.across_y).start()
-
-    def plane_step(group):
-        same(group, half_x, corner(group, y, 1 - x, 0), place.across_x).wait_recv()
-        same(group, rest_y, corner(group, y, both, 0), place.across_y).start()
-        same(group, half_y, corner(group, 1 - y, x, 1), place.across_y).wait_recv()
-        same(group, rest_x, corner(group, both, x, 1), place.across_x).start()
-
-    def plane_end(group):
-        same(group, rest_y, corner(group, 1 - y, both, 0), place.across_y).wait_recv()
-        same(group, rest_x, corner(group, both, 1 - x, 1), place.across_x).wait_recv()
-
-    def wait_sends(group):
-        first(group).wait_send()
-        for step in range(1, line):
-
-            @pl.when((t - step + 1 >= 0) & (t < line - 1))
-            def _():
-                same(group, to_right + step - 1, chunk(group, t - step + 1), place.right).wait_send()
-
-            @pl.when((t + step - 1 <= line - 1) & (t > 0))
-            def _():
-                same(group, to_left + step - 1, chunk(group, t + step - 1), place.left).wait_send()
-
-        same(group, half_x, corner(group, y, x, 0), place.across_x).wait_send()
-        same(group, half_y, corner(group, y, x, 1), place.across_y).wait_send()
-        same(group, rest_y, corner(group, y, both, 0), place.across_y).wait_send()
-        same(group, rest_x, corner(group, both, x, 1), place.across_x).wait_send()
-
-    def line_tail(group, after):
-        for step in range(1, line - 1):
-            line_step(group, step)
-        if after is not None:
-            enter(after)
-            line_start(after)
-        line_step(group, line - 1)
-
-    out, qkv, up_a, up_b, down_a = 1, 0, 2, 3, 4
-    for group in (out, last, qkv, up_a, up_b, down_a):
-        own(group).start()
-        first(group).start()
-    enter(out)
-    line_start(out)
-    enter(last)
-    plane_start(last)
-    line_tail(out, qkv)
-    plane_start(out)
-    plane_step(last)
-    plane_step(out)
-    line_tail(qkv, up_a)
-    plane_start(qkv)
-    plane_end(last)
-    line_tail(up_a, up_b)
-    plane_end(out)
-    plane_step(qkv)
-    plane_start(up_a)
-    line_tail(up_b, down_a)
-    plane_end(qkv)
-    line_tail(down_a, None)
-    line_start(last)
-    plane_step(up_a)
-    plane_start(up_b)
-    line_step(last, 1)
-    plane_end(up_a)
-    plane_step(up_b)
-    plane_start(down_a)
-    for step in range(2, line - 1):
-        line_step(last, step)
-    plane_end(up_b)
-    line_step(last, line - 1)
-    plane_step(down_a)
-    plane_end(down_a)
-    for group in range(len(groups)):
-        wait_sends(group)
-
-
-def gather_weights(attn_low, mlp_low, line):
-    narrow = attn_low.shape[2] // 2 * line
-    wide = mlp_low.shape[2] // 4 * line
-    rows = attn_low.shape[1]
-    shapes = [(3, narrow), (1, narrow), (2, wide), (2, wide)]
-    slots = 2 * line + 3
-    gathered = pl.pallas_call(
-        functools.partial(gather_kernel, line),
-        out_shape=[
-            jax.ShapeDtypeStruct((count, 2, 2, 2, rows, width), jnp.bfloat16) for count, width in shapes
-        ],
-        in_specs=[pl.BlockSpec(memory_space=pl.ANY)] * 2,
-        out_specs=[pl.BlockSpec(memory_space=pl.ANY)] * 4,
-        scratch_shapes=[
-            pltpu.SemaphoreType.DMA((6,)),
-            pltpu.SemaphoreType.DMA((6, slots)),
-            pltpu.SemaphoreType.DMA((6, slots)),
-        ],
-        compiler_params=pltpu.CompilerParams(collective_id=1, has_side_effects=True),
-        name="gather_weights",
-    )(attn_low, mlp_low)
-    return [whole.reshape(whole.shape[0], 8 * rows, -1) for whole in gathered]
+                    self.hop(group, step, left).wait_send()
+
+        self.same(group, self.half_x, self.corner(group, place.y, place.x, 0), place.across_x).wait_send()
+        self.same(group, self.half_y, self.corner(group, place.y, place.x, 1), place.across_y).wait_send()
+        self.same(group, self.rest_y, self.corner(group, place.y, both, 0), place.across_y).wait_send()
+        self.same(group, self.rest_x, self.corner(group, both, place.x, 1), place.across_x).wait_send()
 
 
 def add_blocks(target, sources):
@@ -904,8 +897,10 @@
             device_id_type=MESH,
         )
 
-    def start(self, value):
+    def start(self, value, first_rows):
         self.sums[0] = value
+        for index, row in enumerate(first_rows):
+            self.sums[0, index : index + 1, :] = row
         self.copy(0).start()
 
     def step(self, stage):
@@ -962,36 +957,325 @@
     return (first.astype(dtype), (1.0 - first).astype(dtype))
 
 
-def attend_kernel(slopes, seg_rows, seg_cols, qkv, mixed, lse, distance):
-    group = pl.program_id(0)
+def attend_group(group, slopes, qkv, mixed, lse, distance):
     length = qkv.shape[1]
-
-    @pl.when(group == 0)
-    def _():
-        fill_distance(seg_rows, seg_cols, distance)
-
+    cols = columns(group * 2 * HD, 2 * HD)
     masks = head_lanes(jnp.bfloat16)
     first = head_lanes(jnp.float32)[0] > 0.5
     factor = LOG2E / math.sqrt(HD)
-    keys_t = qkv[1].T
+    keys_t = qkv[1, :, cols].T
+    values = qkv[2, :, cols]
     for start in range(0, length, ROW_BLOCK):
         stop = start + ROW_BLOCK
         rows = slice(start, stop)
+        query = qkv[0, rows, cols]
         parts, sums = [], []
         for head in range(2):
             slope = slopes[2 * group + head] * LOG2E
-            scores = jnp.dot(
-                qkv[0, rows, :] * masks[head], keys_t[:, :stop], preferred_element_type=jnp.float32
-            )
+            scores = jnp.dot(query * masks[head], keys_t[:, :stop], preferred_element_type=jnp.float32)
             scores = scores * factor - slope * distance[rows, :stop]
             top = jnp.max(scores, axis=1, keepdims=True)
             probs = jnp.exp2(scores - top)
             total = jnp.sum(probs, axis=1, keepdims=True)
-            out = jnp.dot(probs.astype(jnp.bfloat16), qkv[2, :stop, :], preferred_element_type=jnp.float32)
+            out = jnp.dot(probs.astype(jnp.bfloat16), values[:stop], preferred_element_type=jnp.float32)
             parts.append(out / total)
             sums.append(top + jnp.log2(total))
-        mixed[rows, :] = jnp.where(first, parts[0], parts[1]).astype(jnp.bfloat16)
-        lse[rows, :] = jnp.where(first, sums[0], sums[1])
+        mixed[rows, cols] = jnp.where(first, parts[0], parts[1]).astype(jnp.bfloat16)
+        lse[rows, cols] = jnp.where(first, sums[0], sums[1])
+
+
+def normalize(rows):
+    centred = rows - jnp.mean(rows, axis=1, keepdims=True)
+    return centred * lax.rsqrt(jnp.mean(centred * centred, axis=1, keepdims=True) + 1e-05)
+
+
+def forward_kernel(
+    line, attn_ref, mlp_ref, tokens_ref, slopes, seg_rows, seg_cols, qkv_bias, hidden_bias, vectors,
+    qkv_w, out_w, up_w, down_w, tokens_out, qkv_out, mixed_out, lse_out, normed_out, middle_out,
+    hidden_out, act_out, bend_out, *scratch
+):
+    (x_v, normed, qkv_wv, out_wv, up_wv, qkv, mixed, lse, distance, part, got, middle, hidden, act, bend) = scratch[:15]
+    load_sem, store_sem, swap_send, swap_recv = scratch[15:19]
+    place = Place()
+    narrow, wide = attn_ref.shape[2] // 2, mlp_ref.shape[2] // 4
+    size = normed.shape[0]
+
+    def attn_source(index):
+        return lambda core: attn_ref.at[index : index + 1, :, columns(core * narrow, narrow)]
+
+    def mlp_source(index, half):
+        return lambda core: mlp_ref.at[index : index + 1, :, columns((2 * core + half) * wide, wide)]
+
+    groups = [(qkv_w.at[index : index + 1], narrow, attn_source(index)) for index in range(3)]
+    groups.append((out_w, narrow, attn_source(3)))
+    groups += [(up_w.at[half : half + 1], wide, mlp_source(0, half)) for half in range(2)]
+    groups += [(down_w.at[half : half + 1], wide, mlp_source(1, half)) for half in range(2)]
+    query, key, value, outer, up_a, up_b, down_a, down_b = range(8)
+    gather = WeightGather(place, line, groups, scratch[19:22])
+    tokens = RowSwap(place, tokens_ref, tokens_out, scratch[22:24])
+
+    def load(group):
+        if group < 3:
+            source, target = qkv_w.at[group], qkv_wv.at[group]
+        elif group == outer:
+            source, target = out_w, out_wv
+        else:
+            source, target = up_w.at[group - up_a], up_wv.at[group - up_a]
+        return pltpu.make_async_copy(source, target, load_sem.at[group])
+
+    x_load = pltpu.make_async_copy(tokens_out, x_v, load_sem.at[7])
+    pairs = (
+        (qkv, qkv_out),
+        (mixed, mixed_out),
+        (lse, lse_out),
+        (normed, normed_out),
+        (middle, middle_out),
+        (hidden, hidden_out),
+        (act.at[0], act_out.at[0]),
+        (act.at[1], act_out.at[1]),
+        (bend.at[0], bend_out.at[0]),
+        (bend.at[1], bend_out.at[1]),
+    )
+
+    def store(index):
+        return pltpu.make_async_copy(*pairs[index], store_sem.at[index])
+
+    def normalize_tokens():
+        def body(step, carry):
+            at = pl.ds(pl.multiple_of(step * 32, 32), 32)
+            normal = normalize(x_v[at, :].astype(jnp.float32))
+            normed[at, :] = (normal * vectors[0:1, :] + vectors[1:2, :]).astype(jnp.bfloat16)
+            return carry
+
+        lax.fori_loop(0, size // 32, body, 0, unroll=4)
+
+    def project(group):
+        load(group).wait()
+        weight = qkv_wv[group].reshape(size, qkv.shape[2])
+
+        def body(step, carry):
+            at = pl.ds(pl.multiple_of(step * 512, 512), 512)
+            out = jnp.dot(normed[at, :], weight, preferred_element_type=jnp.float32)
+            qkv[group, at, :] = (out + qkv_bias[group : group + 1, :]).astype(jnp.bfloat16)
+            return carry
+
+        lax.fori_loop(0, size // 512, body, 0)
+
+    def swap(index):
+        at = pl.ds(pl.multiple_of(index * 256, 256), 256)
+        return pltpu.make_async_remote_copy(
+            src_ref=part.at[at, :],
+            dst_ref=got.at[at, :],
+            send_sem=swap_send.at[index],
+            recv_sem=swap_recv.at[index],
+            device_id=place.twin,
+            device_id_type=MESH,
+        )
+
+    def project_out(index, carry):
+        at = pl.ds(pl.multiple_of(index * 256, 256), 256)
+        weight = out_wv[0].reshape(size, mixed.shape[1])
+        part[at, :] = contract_last(mixed[at, :], weight).astype(jnp.bfloat16)
+        swap(index).start()
+        return carry
+
+    def add_branch(index, carry):
+        swap(index).wait()
+
+        def body(step, carry):
+            at = pl.ds(pl.multiple_of(index * 256 + step * 32, 32), 32)
+            branch = part[at, :].astype(jnp.float32) + got[at, :].astype(jnp.float32)
+            total = x_v[at, :].astype(jnp.float32) + branch + vectors[4:5, :]
+            middle[at, :] = total
+            hidden[at, :] = (normalize(total) * vectors[5:6, :] + vectors[6:7, :]).astype(jnp.bfloat16)
+            return carry
+
+        return lax.fori_loop(0, 8, body, carry, unroll=4)
+
+    def feed(half):
+        load(up_a + half).wait()
+
+        def body(step, carry):
+            at = pl.ds(pl.multiple_of(step * 256, 256), 256)
+            weight = up_wv[half].reshape(size, act.shape[2])
+            pre = jnp.dot(hidden[at, :], weight, preferred_element_type=jnp.float32)
+            pre = pre + hidden_bias[half : half + 1, :]
+            square = pre * pre
+            bent = jnp.tanh(0.7978845608 * pre * (1.0 + 0.044715 * square))
+            inner = 0.7978845608 * (1.0 + 3.0 * 0.044715 * square)
+            act[half, at, :] = (0.5 * pre * (1.0 + bent)).astype(jnp.bfloat16)
+            bend[half, at, :] = (0.5 * (1.0 + bent) + 0.5 * pre * (1.0 - bent * bent) * inner).astype(jnp.bfloat16)
+            return carry
+
+        lax.fori_loop(0, size // 256, body, 0)
+        store(6 + half).start()
+        store(8 + half).start()
+
+    greet(place, line)
+    for group in (query, down_b, key, value, outer, up_a, up_b, down_a):
+        gather.begin(group)
+    gather.enter(query)
+    gather.line_start(query)
+    gather.enter(down_b)
+    gather.plane_start(down_b)
+    gather.enter(key)
+    gather.line_most(query)
+    gather.line_start(key)
+    tokens.start()
+    gather.line_end(query)
+    gather.plane_start(query)
+    gather.plane_step(down_b)
+    gather.enter(value)
+    gather.line_most(key)
+    gather.line_start(value)
+    gather.line_end(key)
+    gather.plane_step(query)
+    gather.plane_start(key)
+    gather.plane_end(down_b)
+    gather.line_most(value)
+    gather.line_end(value)
+    gather.enter(outer)
+    gather.line_start(outer)
+    gather.plane_end(query)
+    load(query).start()
+    gather.plane_step(key)
+    gather.plane_start(value)
+    tokens.step()
+    fill_distance(seg_rows, seg_cols, distance)
+    gather.enter(up_a)
+    gather.line_most(outer)
+    gather.line_start(up_a)
+    gather.plane_end(key)
+    load(key).start()
+    gather.line_end(outer)
+    gather.plane_step(value)
+    gather.plane_start(outer)
+    tokens.end()
+    x_load.start()
+    x_load.wait()
+    normalize_tokens()
+    store(3).start()
+    gather.enter(up_b)
+    gather.line_most(up_a)
+    gather.line_start(up_b)
+    project(query)
+    gather.line_end(up_a)
+    gather.line_start(down_b)
+    gather.plane_end(value)
+    load(value).start()
+    gather.plane_step(outer)
+    gather.plane_start(up_a)
+    project(key)
+    project(value)
+    store(0).start()
+
+    def beside(index):
+        if index == 0:
+            gather.enter(down_a)
+            gather.line_most(up_b)
+            gather.line_start(down_a)
+            gather.plane_end(outer)
+            load(outer).start()
+        if index == 1:
+            gather.line_end(up_b)
+            gather.plane_step(up_a)
+            gather.plane_start(up_b)
+        if index == 2:
+            gather.line_step(down_b, 1)
+        if index == 3:
+            gather.line_most(down_a)
+
+    def attend(index, carry):
+        attend_group(index, slopes, qkv, mixed, lse, distance)
+        for order in range(4):
+
+            @pl.when(index == order)
+            def _():
+                beside(order)
+
+        return carry
+
+    lax.fori_loop(0, qkv.shape[2] // (2 * HD), attend, 0)
+    store(1).start()
+    store(2).start()
+    load(outer).wait()
+    lax.fori_loop(0, size // 256, project_out, 0)
+    gather.plane_step(up_b)
+    gather.line_end(down_a)
+    gather.plane_start(down_a)
+    lax.fori_loop(0, size // 256, add_branch, 0)
+    store(4).start()
+    store(5).start()
+    gather.plane_end(up_a)
+    load(up_a).start()
+    feed(0)
+    for step in range(2, line - 1):
+        gather.line_step(down_b, step)
+    gather.plane_step(down_a)
+    gather.plane_end(up_b)
+    load(up_b).start()
+    feed(1)
+    gather.line_end(down_b)
+    gather.plane_end(down_a)
+    for index in range(len(pairs)):
+        store(index).wait()
+    for group in range(len(groups)):
+        gather.wait_sends(group)
+
+
+def forward(attn_low, mlp_low, tokens, slopes, seg_ids, qkv_bias, hidden_bias, vectors, line):
+    rows = attn_low.shape[1]
+    narrow, wide = attn_low.shape[2] // 2 * line, mlp_low.shape[2] // 4 * line
+    length, width = 2 * tokens.shape[0], tokens.shape[1]
+    low, dma = jnp.bfloat16, pltpu.SemaphoreType.DMA
+    vmem = pl.BlockSpec(memory_space=pltpu.VMEM)
+    hbm = pl.BlockSpec(memory_space=pl.ANY)
+
+    def whole(count, columns_held):
+        return (count, 2, 2, 2, rows, columns_held)
+
+    kept = [
+        ((3, length, narrow), low),
+        ((length, narrow), low),
+        ((length, narrow), jnp.float32),
+        ((length, width), low),
+        ((length, width), jnp.float32),
+        ((length, width), low),
+        ((2, length, wide), low),
+        ((2, length, wide), low),
+    ]
+    outs = [(whole(3, narrow), low), (whole(1, narrow), low), (whole(2, wide), low), (whole(2, wide), low)]
+    outs += [((length, width), low)] + kept
+    held = [(length, width)] * 2 + [whole(3, narrow), whole(1, narrow), whole(2, wide)]
+    results = pl.pallas_call(
+        functools.partial(forward_kernel, line),
+        out_shape=[jax.ShapeDtypeStruct(*each) for each in outs],
+        in_specs=[hbm] * 3 + [pl.BlockSpec(memory_space=pltpu.SMEM)] + [vmem] * 5,
+        out_specs=[hbm] * len(outs),
+        scratch_shapes=[pltpu.VMEM(each, low) for each in held]
+        + [pltpu.VMEM(*each) for each in kept[:3]]
+        + [pltpu.VMEM((length, length), jnp.float32)]
+        + [pltpu.VMEM((length, width), low)] * 2
+        + [pltpu.VMEM(*each) for each in kept[4:]]
+        + [dma((8,)), dma((10,)), dma((length // 256,)), dma((length // 256,))]
+        + WeightGather.scratch(8, line)
+        + RowSwap.scratch(),
+        compiler_params=pltpu.CompilerParams(
+            collective_id=1, has_side_effects=True, vmem_limit_bytes=62 * 1024 * 1024
+        ),
+        name="forward",
+    )(
+        attn_low,
+        mlp_low,
+        tokens,
+        slopes,
+        seg_ids.reshape(-1, 1),
+        seg_ids.reshape(1, -1),
+        qkv_bias,
+        hidden_bias,
+        vectors,
+    )
+    return [each.reshape(each.shape[0], length, -1) for each in results[:4]] + list(results[4:])
 
 
 def attend_back_group(group, slopes, qkv, grad, mixed, lse, out, distance, dk_acc, dv_acc):
@@ -1034,20 +1318,46 @@
 
 
 def back_kernel(
-    line, down_ref, up_ref, slopes, seg_rows, seg_cols, qkv, grad, mixed, lse, mlp_home, out, distance, dk_acc, dv_acc, *scratch
+    line, down_ref, up_ref, out_ref, slopes, seg_rows, seg_cols, qkv, grad, mixed, lse, weights, normed,
+    mlp_home, attn_home, normed_part, bias_sums, grads, projected, distance, dk_acc, dv_acc, *scratch
 ):
     place = Place()
-    wide = mlp_home.shape[2] // 4
-    groups = []
-    for order, (ref, index, part) in enumerate(((down_ref, 1, 0), (down_ref, 1, 1), (up_ref, 0, 0), (up_ref, 0, 1))):
-        target = mlp_home.at[index : index + 1, :, columns((2 * place.core + part) * wide, wide)]
-        groups.append(
-            GroupSum(place, line, ref.at[part : part + 1], target, scratch[order], line_first=order == 3)
-        )
-    one, two, three, last = groups
-
-    def attend(group):
-        attend_back_group(group, slopes, qkv, grad, mixed, lse, out, distance, dk_acc, dv_acc)
+    wide, narrow = mlp_home.shape[2] // 4, attn_home.shape[2] // 2
+
+    def mlp_target(index, part):
+        return mlp_home.at[index : index + 1, :, columns((2 * place.core + part) * wide, wide)]
+
+    def attn_target(lo, hi):
+        return attn_home.at[lo:hi, :, columns(place.core * narrow, narrow)]
+
+    groups = [
+        GroupSum(place, line, down_ref.at[0:1], mlp_target(1, 0), scratch[0]),
+        GroupSum(place, line, down_ref.at[1:2], mlp_target(1, 1), scratch[1]),
+        GroupSum(place, line, up_ref.at[0:1], mlp_target(0, 0), scratch[2]),
+        GroupSum(place, line, out_ref, attn_target(3, 4), scratch[3]),
+        GroupSum(place, line, projected, attn_target(0, 3), scratch[4]),
+        GroupSum(place, line, up_ref.at[1:2], mlp_target(0, 1), scratch[5], line_first=True),
+    ]
+    one, two, three, outer, inner, last = groups
+
+    def attend(group, carry):
+        attend_back_group(group, slopes, qkv, grad, mixed, lse, grads, distance, dk_acc, dv_acc)
+        return carry
+
+    def project(index, carry):
+        left = normed[:, columns(index * 256, 256)].T
+        for order in range(3):
+            piece = jnp.dot(left, grads[order], preferred_element_type=jnp.float32).astype(jnp.bfloat16)
+            projected[order, index // 2, lax.rem(index, 2)] = piece.reshape(2, 128, piece.shape[1])
+        return carry
+
+    def unproject(index, carry):
+        at = pl.ds(pl.multiple_of(index * 256, 256), 256)
+        total = contract_last(grads[0, at, :], weights[0])
+        for order in range(1, 3):
+            total = total + contract_last(grads[order, at, :], weights[order])
+        normed_part[at, :] = total.astype(jnp.bfloat16)
+        return carry
 
     greet(place, line)
     one.plane.start()
@@ -1056,100 +1366,97 @@
     last.line.step(0)
     fill_distance(seg_rows, seg_cols, distance)
     pairs = qkv.shape[2] // (2 * HD)
-
-    def body(group, carry):
-        attend(group)
-        return carry
-
-    lax.fori_loop(0, pairs // 2, body, 0)
+    lax.fori_loop(0, pairs // 2, attend, 0)
     one.plane.one()
     two.plane.start()
     last.line.step(1)
-    lax.fori_loop(pairs // 2, pairs, body, 0)
+    lax.fori_loop(pairs // 2, pairs, attend, 0)
     one.plane.two()
     one.line.step(0)
     two.plane.one()
-    three.plane.start()
+    lax.fori_loop(0, normed.shape[1] // 256, project, 0)
+    inner.plane.start()
     for step in range(2, line - 1):
         last.line.step(step)
     for step in range(1, line - 1):
         one.line.step(step)
     two.plane.two()
     two.line.step(0)
+    lax.fori_loop(0, normed.shape[0] // 256, unproject, 0)
+    for order in range(3):
+        bias_sums[order : order + 1, :] = jnp.sum(grads[order].astype(jnp.float32), axis=0, keepdims=True)
     one.line.end()
     one.home.start()
     last.line.end()
     last.plane.start()
-    three.plane.one()
+    inner.plane.one()
+    three.plane.start()
     for step in range(1, line - 1):
         two.line.step(step)
     last.plane.one()
+    two.line.end()
+    two.home.start()
+    inner.plane.two()
+    inner.line.step(0)
+    last.plane.two()
+    last.home.start()
+    three.plane.one()
+    outer.plane.start()
+    for step in range(1, line - 1):
+        inner.line.step(step)
     three.plane.two()
     three.line.step(0)
-    two.line.end()
-    two.home.start()
-    last.plane.two()
-    last.home.start()
+    inner.line.end()
+    inner.home.start()
+    outer.plane.one()
+    three.line.step(1)
+    outer.plane.two()
+    outer.line.step(0)
+    for step in range(2, line - 1):
+        three.line.step(step)
     for step in range(1, line - 1):
-        three.line.step(step)
+        outer.line.step(step)
     three.line.end()
     three.home.start()
+    outer.line.end()
+    outer.home.start()
     for group in groups:
         group.finish()
 
 
-def attention_specs(length):
-    return [
-        pl.BlockSpec(memory_space=pltpu.SMEM),
-        pl.BlockSpec((length, 1), lambda g: (0, 0)),
-        pl.BlockSpec((1, length), lambda g: (0, 0)),
-        pl.BlockSpec((3, length, 2 * HD), lambda g: (0, 0, g)),
-    ]
-
-
-def attend(slopes, seg_ids, qkv):
-    _, length, width = qkv.shape
-    rows = pl.BlockSpec((length, 2 * HD), lambda g: (0, g))
-    return pl.pallas_call(
-        attend_kernel,
-        grid=(width // (2 * HD),),
-        out_shape=[
-            jax.ShapeDtypeStruct((length, width), jnp.bfloat16),
-            jax.ShapeDtypeStruct((length, width), jnp.float32),
-        ],
-        in_specs=attention_specs(length),
-        out_specs=[rows, rows],
-        scratch_shapes=[pltpu.VMEM((length, length), jnp.float32)],
-        compiler_params=pltpu.CompilerParams(vmem_limit_bytes=48 * 1024 * 1024),
-        name="attend",
-    )(slopes, seg_ids.reshape(-1, 1), seg_ids.reshape(1, -1), qkv)
-
-
-def attend_back(down, up, slopes, seg_ids, qkv, grad, mixed, lse, line):
+def attend_back(down, up, out, slopes, seg_ids, qkv, grad, mixed, lse, weights, normed, line):
     _, length, width = qkv.shape
     rows, wide = down.shape[1] // 8, down.shape[2]
+    size = normed.shape[1]
     vmem = pl.BlockSpec(memory_space=pltpu.VMEM)
     hbm = pl.BlockSpec(memory_space=pl.ANY)
+    low = jnp.bfloat16
     return pl.pallas_call(
         functools.partial(back_kernel, line),
         out_shape=[
-            jax.ShapeDtypeStruct((2, rows, 4 * wide // line), jnp.bfloat16),
-            jax.ShapeDtypeStruct(qkv.shape, jnp.bfloat16),
+            jax.ShapeDtypeStruct((2, rows, 4 * wide // line), low),
+            jax.ShapeDtypeStruct((4, rows, 2 * width // line), low),
+            jax.ShapeDtypeStruct((length, size), low),
+            jax.ShapeDtypeStruct((3, width), jnp.float32),
         ],
-        in_specs=[hbm] * 2 + [pl.BlockSpec(memory_space=pltpu.SMEM)] + [vmem] * 6,
-        out_specs=[hbm, vmem],
+        in_specs=[hbm] * 3 + [pl.BlockSpec(memory_space=pltpu.SMEM)] + [vmem] * 8,
+        out_specs=[hbm, hbm, vmem, vmem],
         scratch_shapes=[
+            pltpu.VMEM(qkv.shape, low),
+            pltpu.VMEM((3, 2, 2, 2, rows, width), low),
             pltpu.VMEM((length, length), jnp.float32),
             pltpu.VMEM((2 * HD, length), jnp.float32),
             pltpu.VMEM((2 * HD, length), jnp.float32),
         ]
-        + [GroupSum.scratch(1, rows, wide, line, line_first=order == 3) for order in range(4)],
+        + [GroupSum.scratch(1, rows, wide, line)] * 3
+        + [GroupSum.scratch(1, rows, width, line), GroupSum.scratch(3, rows, width, line)]
+        + [GroupSum.scratch(1, rows, wide, line, line_first=True)],
         compiler_params=pltpu.CompilerParams(
-            collective_id=2, has_side_effects=True, vmem_limit_bytes=56 * 1024 * 1024
+            collective_id=2, has_side_effects=True, vmem_limit_bytes=62 * 1024 * 1024
         ),
         name="attend_back",
     )(
-        *(each.reshape(2, 2, 2, 2, rows, wide) for each in (down, up)),
+        *(each.reshape(-1, 2, 2, 2, rows, each.shape[2]) for each in (down, up, out)),
         slopes,
         seg_ids.reshape(-1, 1),
         seg_ids.reshape(1, -1),
@@ -1157,15 +1464,19 @@
         grad,
         mixed,
         lse,
+        weights,
+        normed,
     )
 
 
 OWNERS = ((1, 0, 0), (1, 0, 3), (0, 1, 0), (0, 1, 3), (0, 0, 1), (1, 1, 2))
 
 
-def finish_kernel(line, out_ref, qkv_ref, vec_ref, mom_ref, mlp_ref, mom_out, vec_out, attn_home, mlp_home, *scratch):
-    (thin, full, gram, sent, got, poly, norm_own, norm_got, attn_sum, attn_ref) = scratch[:10]
-    (home_sem, start_sem, send_sem, back_sem, norm_sem, block_send, block_recv, pass_send, pass_recv) = scratch[10:19]
+def finish_kernel(
+    line, attn_ref, mlp_ref, vec_ref, gain, part_ref, xhat, spread, grad_mid, attn_home, mlp_home, vec_out, dx_out, *scratch
+):
+    (thin, full, gram, sent, got, poly, norm_own, norm_got, dx, away, mine) = scratch[:11]
+    (home_sem, start_sem, send_sem, back_sem, norm_sem, block_send, block_recv, pass_send, pass_recv, dx_sem) = scratch[11:21]
     place = Place()
     x, y, t, core = place.x, place.y, place.tensor, place.core
     me = place.dp * line + t
@@ -1189,16 +1500,7 @@
     lax.fori_loop(1, devices, meet, 0)
     pl.semaphore_wait(barrier, devices - 1)
 
-    part = attn_ref.shape[2] // 2
-
-    def target_sum(lo, hi):
-        return attn_sum.at[lo:hi, :, columns(core * part, part)]
-
-    sums = (
-        GroupSum(place, line, out_ref, target_sum(3, 4), scratch[23]),
-        GroupSum(place, line, qkv_ref, target_sum(0, 3), scratch[24]),
-    )
-    vector = VectorSum(place, line, scratch[19:23])
+    vector = VectorSum(place, line, scratch[21:25])
 
     def source(order, half):
         if order < 4:
@@ -1287,14 +1589,35 @@
                 for cores in range(2):
                     action(order, which, cores)
 
-    for order in (5, 4):
+    half_rows = dx.shape[0]
+
+    def rows_of(cores):
+        return part_ref.at[pl.ds(pl.multiple_of(cores * half_rows, half_rows), half_rows), :]
+
+    part_swap = pltpu.make_async_remote_copy(
+        src_ref=rows_of(1 - core),
+        dst_ref=away,
+        send_sem=dx_sem.at[0],
+        recv_sem=dx_sem.at[1],
+        device_id=place.twin,
+        device_id_type=MESH,
+    )
+    part_load = pltpu.make_async_copy(rows_of(core), mine, dx_sem.at[2])
+    part_swap.start()
+    part_load.start()
+
+    for order in (5, 4, 0, 1, 2, 3):
         for half in range(2):
-
-            @pl.when(by_way(order))
-            def _():
-                to_way(order, half).start()
-
-            @pl.when((me != owner_of(order, half)) & jnp.logical_not(by_way(order)))
+            direct = me != owner_of(order, half)
+            if order >= 4:
+
+                @pl.when(by_way(order))
+                def _():
+                    to_way(order, half).start()
+
+                direct = direct & jnp.logical_not(by_way(order))
+
+            @pl.when(direct)
             def _():
                 collect(order, half).start()
 
@@ -1302,8 +1625,6 @@
             def _():
                 collect_own(order, half).start()
 
-    vector.start(vec_ref[...])
-
     def forward(order, which, cores):
         pass_in(order, which, cores).wait_recv()
         pass_on(order, which, cores).start()
@@ -1311,17 +1632,49 @@
     for order in (5, 4):
         when_passing(order, forward)
 
-    for order in (4, 5):
-        for half in range(2):
-
-            @pl.when(me != owner_of(order, half))
-            def _():
-                collect(order, half).wait_send()
-
-    for group in sums:
-        group.plane.start()
-    for stage in range(3):
-        vector.step(stage)
+    part_swap.wait()
+    part_load.wait()
+    step_rows = 16
+
+    def dx_rows(step, sums):
+        at = pl.ds(pl.multiple_of(step * step_rows, step_rows), step_rows)
+        grad = mine[at, :].astype(jnp.float32) + away[at, :].astype(jnp.float32)
+        hat = xhat[at, :]
+        product = grad * hat
+        scaled = grad * gain[...]
+        inner = jnp.mean(scaled * hat, axis=1, keepdims=True)
+        back_grad = spread[at, :] * (scaled - jnp.mean(scaled, axis=1, keepdims=True) - hat * inner)
+        dx[at, :] = (grad_mid[at, :] + back_grad).astype(jnp.bfloat16)
+        fold = (step_rows // 8, 8, grad.shape[1])
+        return (
+            sums[0] + jnp.sum(product.reshape(fold), axis=0),
+            sums[1] + jnp.sum(grad.reshape(fold), axis=0),
+        )
+
+    empty = jnp.zeros((8, gain.shape[1]), jnp.float32)
+    gain_sum, shift_sum = lax.fori_loop(0, half_rows // step_rows, dx_rows, (empty, empty))
+    dx_keep = pltpu.make_async_copy(dx, dx_out, dx_sem.at[2])
+    dx_away = pltpu.make_async_remote_copy(
+        src_ref=dx,
+        dst_ref=dx_out,
+        send_sem=dx_sem.at[3],
+        recv_sem=dx_sem.at[4],
+        device_id=place.corner,
+        device_id_type=MESH,
+    )
+
+    @pl.when(place.stays)
+    def _():
+        dx_keep.start()
+
+    @pl.when(jnp.logical_not(place.stays))
+    def _():
+        dx_away.start()
+
+    vector.start(
+        vec_ref[...],
+        (jnp.sum(gain_sum, axis=0, keepdims=True), jnp.sum(shift_sum, axis=0, keepdims=True)),
+    )
 
     def contract_rows(left, right):
         return lax.dot_general(left, right, (((1,), (1,)), ((), ())), preferred_element_type=jnp.float32)
@@ -1369,16 +1722,10 @@
 
         lax.fori_loop(0, size // 32, scale_rows, 0)
 
-    def iterate(matrix, repeat, part):
+    def iterate(matrix, repeat):
         size, width = matrix.shape
         blocks = size // block
         slot = repeat % 2
-        if part == 0:
-            make_gram(matrix, blocks, slot)
-        else:
-            make_next(matrix, blocks, width)
-
-    def make_gram(matrix, blocks, slot):
 
         def share(index, carry):
             at = pl.ds(pl.multiple_of(index * block, block), block)
@@ -1396,24 +1743,17 @@
             return carry
 
         lax.fori_loop(0, blocks, add, 0)
-
-    def make_next(matrix, blocks, width):
-        def polynomial(index, carry):
-            at = pl.ds(pl.multiple_of(index * block, block), block)
-            square = jnp.dot(gram[at, :], gram[...], preferred_element_type=jnp.float32)
-            poly[at, :] = (coeff_b * gram[at, :].astype(jnp.float32) + coeff_c * square).astype(jnp.bfloat16)
+        square = jnp.dot(gram[...], gram[...], preferred_element_type=jnp.float32)
+        poly[...] = (coeff_b * gram[...].astype(jnp.float32) + coeff_c * square).astype(jnp.bfloat16)
+        step_width = min(width, 1024)
+
+        def advance(index, carry):
+            at = columns(index * step_width, step_width)
+            moved = jnp.dot(poly[...], matrix[:, at], preferred_element_type=jnp.float32)
+            matrix[:, at] = (coeff_a * matrix[:, at].astype(jnp.float32) + moved).astype(jnp.bfloat16)
             return carry
 
-        lax.fori_loop(0, blocks, polynomial, 0)
-
-        def advance(index, carry):
-            at = columns(index * block, block)
-            piece = matrix[:, at]
-            moved = jnp.dot(poly[...], piece, preferred_element_type=jnp.float32)
-            matrix[:, at] = (coeff_a * piece.astype(jnp.float32) + moved).astype(jnp.bfloat16)
-            return carry
-
-        lax.fori_loop(0, width // block, advance, 0)
+        lax.fori_loop(0, width // step_width, advance, 0)
 
     def owns(order):
         ox, oy, oz = OWNERS[order]
@@ -1422,54 +1762,28 @@
     owns_full = owns(4) | owns(5)
     owns_thin = owns(0) | owns(1) | owns(2) | owns(3)
 
-    def update_attn():
-        for group in sums:
-            group.finish()
-        fresh = 0.5 * mom_ref[...] + attn_sum[...].astype(jnp.float32)
-        mom_out[...] = fresh
-        attn_ref[...] = fresh.astype(jnp.bfloat16)
-        for order in range(4):
-            for half in range(2):
-
-                @pl.when(me == owner_of(order, half))
-                def _():
-                    collect_own(order, half).start()
-
-                @pl.when(me != owner_of(order, half))
-                def _():
-                    collect(order, half).start()
-
-    def between(repeat, part):
-        if repeat == 0 and part == 0:
-            for group in sums:
-                group.plane.two()
-                group.line.step(0)
-        if repeat == 0 and part == 1:
-            for step in range(1, line - 1):
-                for group in sums:
-                    group.line.step(step)
-        if repeat == 1 and part == 0:
-            for group in sums:
-                group.line.end()
-                group.home.start()
-        if repeat == 1 and part == 1:
-            update_attn()
+    @pl.when(owns_thin)
+    def _():
+        begin(thin)
 
     @pl.when(owns_full)
     def _():
         begin(full)
 
-    for group in sums:
-        group.plane.one()
-    vec_out[...] = vector.end()
     for repeat in range(NS_STEPS):
-        for part in range(2):
-
-            @pl.when(owns_full)
-            def _():
-                iterate(full, repeat, part)
-
-            between(repeat, part)
+
+        @pl.when(owns_thin)
+        def _():
+            iterate(thin, repeat)
+
+        @pl.when(owns_full)
+        def _():
+            iterate(full, repeat)
+
+        if repeat < 3:
+            vector.step(repeat)
+        if repeat == 3:
+            vec_out[...] = vector.end()
 
     def keep(order, half):
         return pltpu.make_async_copy(held(order, me), target(order, half), back_sem.at[order, half])
@@ -1543,16 +1857,7 @@
                     each_device(order, half, lambda *at: back(*at).start(), False)
                     keep(order, half).start()
 
-    give_back((4, 5))
-
-    @pl.when(owns_thin)
-    def _():
-        begin(thin)
-        for repeat in range(NS_STEPS):
-            for part in range(2):
-                iterate(thin, repeat, part)
-
-    give_back(range(4))
+    give_back((4, 5, 0, 1, 2, 3))
 
     def return_rows(order, half, which, cores):
         back_in(order, which, cores).wait_recv()
@@ -1571,34 +1876,41 @@
                     each_device(order, half, lambda *at: to_back_way(*at).wait_send(), True)
                 each_device(order, half, lambda *at: back(*at).wait_send(), False)
 
-            if order < 4:
-
-                @pl.when(me != owner_of(order, half))
-                def _():
-                    collect(order, half).wait_send()
+            @pl.when(me != owner_of(order, half))
+            def _():
+                collect(order, half).wait_send()
 
     for order in (4, 5):
         when_passing(order, lambda *at: pass_on(*at).wait_send())
         when_back_way(order, lambda *at: back_on(*at).wait_send())
 
-
-def finish(out, qkv, vec, attn_mom, mlp_round, line):
-    rows = attn_mom.shape[1]
-    size, part = 8 * rows, attn_mom.shape[2] // 2
-    narrow, wide = part * line, mlp_round.shape[2] // 2 * line
+    @pl.when(place.stays)
+    def _():
+        dx_keep.wait()
+
+    @pl.when(jnp.logical_not(place.stays))
+    def _():
+        dx_away.wait()
+
+
+def finish(attn_round, mlp_round, vec, gain, normed_part, xhat, spread, grad_mid, line):
+    rows = attn_round.shape[1]
+    size = 8 * rows
+    narrow, wide = attn_round.shape[2] // 2 * line, mlp_round.shape[2] // 2 * line
     low, dma = jnp.bfloat16, pltpu.SemaphoreType.DMA
     hbm = pl.BlockSpec(memory_space=pl.ANY)
     vmem = pl.BlockSpec(memory_space=pltpu.VMEM)
+    half = xhat.shape
     return pl.pallas_call(
         functools.partial(finish_kernel, line),
         out_shape=[
-            jax.ShapeDtypeStruct(attn_mom.shape, jnp.float32),
+            jax.ShapeDtypeStruct(attn_round.shape, low),
+            jax.ShapeDtypeStruct(mlp_round.shape, low),
             jax.ShapeDtypeStruct(vec.shape, jnp.float32),
-            jax.ShapeDtypeStruct(attn_mom.shape, low),
-            jax.ShapeDtypeStruct(mlp_round.shape, low),
+            jax.ShapeDtypeStruct(half, low),
         ],
-        in_specs=[hbm, hbm, vmem, vmem, hbm],
-        out_specs=[vmem, vmem, hbm, hbm],
+        in_specs=[hbm, hbm, vmem, vmem, hbm, vmem, vmem, vmem],
+        out_specs=[hbm, hbm, vmem, hbm],
         scratch_shapes=[
             pltpu.VMEM((size, narrow), low),
             pltpu.VMEM((size, wide), low),
@@ -1608,8 +1920,9 @@
             pltpu.VMEM((size, size), low),
             pltpu.VMEM((8, 128), jnp.float32),
             pltpu.VMEM((8, 128), jnp.float32),
-            pltpu.VMEM(attn_mom.shape, low),
-            pltpu.VMEM(attn_mom.shape, low),
+            pltpu.VMEM(half, low),
+            pltpu.VMEM(half, low),
+            pltpu.VMEM(half, low),
             dma((6, 2)),
             dma((1,)),
             dma((1,)),
@@ -1619,19 +1932,14 @@
             dma((2, size // 256)),
             dma((2, 2)),
             dma((2, 2)),
+            dma((5,)),
         ]
-        + VectorSum.scratch(vec.shape, line)
-        + [GroupSum.scratch(count, rows, narrow, line) for count in (1, 3)],
+        + VectorSum.scratch(vec.shape, line),
         compiler_params=pltpu.CompilerParams(
-            collective_id=3, has_side_effects=True, vmem_limit_bytes=54 * 1024 * 1024
+            collective_id=3, has_side_effects=True, vmem_limit_bytes=56 * 1024 * 1024
         ),
         name="finish",
-    )(
-        *(each.reshape(each.shape[0], 2, 2, 2, rows, narrow) for each in (out, qkv)),
-        vec,
-        attn_mom,
-        mlp_round,
-    )
+    )(attn_round, mlp_round, vec, gain.reshape(1, -1), normed_part, xhat, spread, grad_mid)
 
 
 def pair_swap(value):
@@ -1694,11 +2002,6 @@
     narrow, wide = attn_w.shape[2] // 2, mlp_w.shape[2] // 4
     total_tokens = tokens.shape[0] * line * lax.axis_size("dp")
 
-    wqkv, wout, w_up, w_down = gather_weights(
-        attn_w.astype(jnp.bfloat16), mlp_w.astype(jnp.bfloat16), line
-    )
-    wout = wout[0]
-
     def my_columns(row):
         return lax.dynamic_index_in_dim(row.reshape(line, 2, narrow), core, 1, False).reshape(-1)
 
@@ -1709,39 +2012,41 @@
     hidden_bias = lax.dynamic_index_in_dim(vectors[8:].reshape(line, 2, 2, wide), core, 1, False)
     hidden_bias = hidden_bias.transpose(1, 0, 2).reshape(2, line * wide)
 
-    x_rows = both_halves(corner_swap(tokens, place), place).astype(jnp.float32)
-    grad_low = both_halves(corner_swap(cotangent, place), place)
     seg_pairs = segments.reshape(-1, SEQ)
     seg_own = lax.dynamic_index_in_dim(seg_pairs, t // 2, 0, False)
     seg_ids = jnp.where(core == lax.rem(t, 2), seg_own, pair_swap(seg_own))
 
-    xhat_one, spread_one = norm_parts(x_rows)
-    normed = (xhat_one * vectors[0] + vectors[1]).astype(jnp.bfloat16)
-    projected = jnp.einsum("td,mdc->mtc", normed, wqkv, preferred_element_type=jnp.float32)
     biases = jnp.stack([my_columns(vectors[2]), jnp.zeros((narrow * line,), jnp.float32), my_columns(vectors[3])])
-    qkv = (projected + biases[:, None]).astype(jnp.bfloat16)
-    local_heads = qkv.shape[2] // HD
     per = narrow // HD
-    local_ids = jnp.arange(local_heads)
+    local_ids = jnp.arange(per * line)
     head_ids = (local_ids // per) * (2 * per) + core * per + local_ids % per
     slopes = jnp.exp2(-(8.0 / HEADS) * (head_ids.astype(jnp.float32) + 1.0))
-    mixed, log_sums = attend(slopes, seg_ids, qkv)
-    branch = sum_whole(contract_last(mixed, wout).astype(jnp.bfloat16))
-    middle = x_rows + branch + vectors[4]
+    low = jnp.bfloat16
+    (
+        wqkv, wout, w_up, w_down, x_low, qkv, mixed, log_sums, normed, middle, hidden_low, hidden_act, bend
+    ) = forward(
+        attn_w.astype(low),
+        mlp_w.astype(low),
+        tokens,
+        slopes,
+        seg_ids,
+        biases,
+        hidden_bias,
+        vectors,
+        line,
+    )
+    wout = wout[0]
+    cotangent, middle = lax.optimization_barrier((cotangent, middle))
+    grad_low = both_halves(corner_swap(cotangent, place), place)
+    xhat_one, spread_one = norm_parts(x_low.astype(jnp.float32))
     xhat_two, spread_two = norm_parts(middle)
-    hidden_low = (xhat_two * vectors[5] + vectors[6]).astype(jnp.bfloat16)
-    hidden_pre = (
-        jnp.einsum("td,sdc->stc", hidden_low, w_up, preferred_element_type=jnp.float32) + hidden_bias[:, None]
-    )
-    act_float, gelu_pull = jax.vjp(gelu_tanh, hidden_pre)
-    hidden_act = act_float.astype(jnp.bfloat16)
     out_part = jnp.einsum("stc,sdc->td", hidden_act, w_down, preferred_element_type=jnp.float32)
     output = my_half(middle, place) + sum_rows(out_part.astype(jnp.bfloat16), place) + vectors[7]
     output = corner_swap(output.astype(jnp.bfloat16), place)
 
     grad_down = jnp.einsum("td,stc->sdc", grad_low, hidden_act, preferred_element_type=jnp.float32)
     grad_act = jnp.einsum("td,sdc->stc", grad_low, w_down, preferred_element_type=jnp.float32)
-    grad_pre = gelu_pull(grad_act)[0].astype(jnp.bfloat16)
+    grad_pre = (grad_act * bend.astype(jnp.float32)).astype(jnp.bfloat16)
     grad_up = jnp.einsum("td,stc->sdc", hidden_low, grad_pre, preferred_element_type=jnp.float32)
     hidden_sums = jnp.sum(grad_pre, axis=1, dtype=jnp.float32)
     hidden_part = jnp.einsum("stc,sdc->td", grad_pre, w_up, preferred_element_type=jnp.float32)
@@ -1750,19 +2055,21 @@
     grad_mid_low = grad_middle.astype(jnp.bfloat16)
     grad_out = contract_first(grad_mid_low, mixed)
     grad_mixed = jnp.dot(grad_mid_low, wout, preferred_element_type=jnp.float32).astype(jnp.bfloat16)
-    low = jnp.bfloat16
-    mlp_sum, grad_qkv = attend_back(
-        grad_down.astype(low), grad_up.astype(low), slopes, seg_ids, qkv, grad_mixed, mixed, log_sums, line
-    )
-    grad_proj = jnp.einsum("td,mtc->mdc", normed, grad_qkv, preferred_element_type=jnp.float32)
-    bias_sums = jnp.sum(grad_qkv, axis=1, dtype=jnp.float32)
-    normed_part = jnp.einsum("mtc,mdc->td", grad_qkv, wqkv, preferred_element_type=jnp.float32)
-    grad_normed = sum_rows(normed_part.astype(jnp.bfloat16), place)
-    xhat_mine, spread_mine = my_half(xhat_one, place), my_half(spread_one, place)
+    mlp_sum, attn_sum, normed_part, bias_sums = attend_back(
+        grad_down.astype(low),
+        grad_up.astype(low),
+        grad_out.astype(low)[None],
+        slopes,
+        seg_ids,
+        qkv,
+        grad_mixed,
+        mixed,
+        log_sums,
+        wqkv,
+        normed,
+        line,
+    )
     grad_mid_mine = my_half(grad_middle, place)
-    grad_tokens = grad_mid_mine + norm_back(grad_normed, vectors[0], xhat_mine, spread_mine)
-    grad_tokens = corner_swap(grad_tokens.astype(jnp.bfloat16), place).astype(jnp.float32)
-
     hidden_mine = my_half(grad_hidden, place)
     hidden_grad = lax.dynamic_update_slice(
         jnp.zeros((line, 2, 2, wide), jnp.float32),
@@ -1771,8 +2078,8 @@
     )
     vector_rows = jnp.stack(
         [
-            jnp.sum(grad_normed * xhat_mine, axis=0),
-            jnp.sum(grad_normed, axis=0),
+            jnp.zeros((width,), jnp.float32),
+            jnp.zeros((width,), jnp.float32),
             place_columns(bias_sums[0]),
             place_columns(bias_sums[2]),
             jnp.sum(grad_mid_mine, axis=0),
@@ -1783,13 +2090,17 @@
     )
     vector_local = jnp.concatenate([vector_rows, hidden_grad.reshape(-1, width)], axis=0)
     padding = jnp.zeros((4, width), jnp.float32)
+    attn_mom_new = 0.5 * attn_mom + attn_sum.astype(jnp.float32)
     mlp_mom_new = 0.5 * mlp_mom + mlp_sum.astype(jnp.float32)
-    attn_mom_new, vector_sum, attn_ortho, mlp_ortho = finish(
-        grad_out.astype(low)[None],
-        grad_proj.astype(low),
+    attn_ortho, mlp_ortho, vector_sum, grad_tokens = finish(
+        attn_mom_new.astype(low),
+        mlp_mom_new.astype(low),
         jnp.concatenate([vector_local, padding], axis=0),
-        attn_mom,
-        mlp_mom_new.astype(low),
+        vectors[0],
+        normed_part,
+        my_half(xhat_one, place),
+        my_half(spread_one, place),
+        grad_mid_mine,
         line,
     )
     vector_grads = vector_sum[: vector_local.shape[0]]
@@ -1799,7 +2110,7 @@
     vector_new = vectors - 0.1 / math.sqrt(total_tokens) * vector_mom_new
     return (
         output,
-        grad_tokens,
+        grad_tokens.astype(jnp.float32),
         attn_mom_new,
         attn_new,
         mlp_mom_new,

time: 568 us -> 501 us (0.88)
  matrix products: 69.7 us -> 40.6 us
  starting transfers between devices: 25.6 us -> 5.4 us
  local copies, waits for them, and re-layouts: 23.1 us -> 8.08 us
    pallas_call x1, Pallas kernels: 179 us -> 139 us  [finish(): pl.pallas_call(functools.partial(finish_kernel, line), out_shape=[jax.Sha...]
    pallas_call x1, Pallas kernels: 88.6 us -> 126 us  [attend_back(): pl.pallas_call(functools.partial(back_kernel, line), out_shape=[jax.Shape...]
    dot_general x5 -> x0, matrix products: 25.2 us -> none  [the longest x1 6.42 us: on_chip_pair(): jnp.einsum('mtc,mdc->td', grad_qkv, wqkv, preferred_element_type=jnp.floa...]
    ppermute x7 -> x4, starting transfers between devices: 18.8 us -> 1.51 us  [pair_swap(): return lax.ppermute(value, ('dp', 'tensor'), pairs)]
    unnamed x91 -> x41, local copies, waits for them, and re-layouts: 14 us -> 0.69 us
    convert_element_type x3 -> x4, other arithmetic: 1.74 us -> 8.55 us  [the longest x1 2.79 us: on_chip_pair(): grad_tokens.astype(jnp.float32)]
    pallas_call x2 -> x1, Pallas kernels: 132 us -> 132 us  [forward(): pl.pallas_call(functools.partial(forward_kernel, line), out_shape=[jax.Sh...]
  transfers between devices with their start and end apart: 11 -> 6, of which waited for: 1 -> 0; matrix products, arithmetic and copies ran while one was open for 15% -> 12% of each run, Pallas kernels for 72% -> 0%
where the time goes in v3:
time: 501 us; the launch traced here: 493 us
  Pallas kernels  397 us (79%)
  matrix products  40.6 us (8%)
  other arithmetic  40 us (8%)
  local copies, waits for them, and re-layouts  8.08 us (2%)
  starting transfers between devices  5.4 us (1%)
    pallas_call x1, Pallas kernels, finish(): pl.pallas_call(functools.partial(finish_kernel, line), out_shape=[jax.Sha...  139 us
    pallas_call x1, Pallas kernels, forward(): pl.pallas_call(functools.partial(forward_kernel, line), out_shape=[jax.Sh...  132 us
    pallas_call x1, Pallas kernels, attend_back(): pl.pallas_call(functools.partial(back_kernel, line), out_shape=[jax.Shape...  126 us
  transfers between devices with their start and end apart: 6, of which 0 were waited for; matrix products, arithmetic and copies ran while one was open for 12% of the time, Pallas kernels for 0%

profile of v3, /device:TPU:0, one launch (start us, length us, event | category | flops | bytes accessed | tf_op | source)
XLA Modules:
  0.0 492.5 jit_solution(7883474863086080356)
XLA Ops:
  8.0 2.1 convert_element_type.91.mlp_ref
  11.1 131.7 %forward.1 = (bf16[3,2,2,2,128,512]{5,4,3,2,1,0:T(8,128)(2,1)}, bf16[1,2,2,2,128,512]{5,4,3,2,1,0:T(8,128)(2,1)}, bf16[2,2,2,2,128,1024]{5,4,3,2,1,0:T(8,128)(2,...) custom-call(bf16[4,128,256]{2,1,0:T(8,128)(2,1)} %convert_element_ty, ...), custom_call_target="tpu_custom_call" | custom-call | tf_op jit(solution)/shard_map/forward/pallas_call | solution.py:1250
  142.8 1.9 convert_reduce_fusion.1
  144.8 2.1 collective-permute-start.3
  146.9 8.1 %bitcast_convert_fusion.1 = bf16[1024,1024]{1,0:T(8,128)(2,1)S(1)} fusion(bf16[2,1024,1024]{2,1,0:T(8,128)(2,1)} %get-tuple-element.33, bf16[2,1024,1024]{2,1,0:T(8,128)(2,1)} %bitcast.107), kind=kOutput, calls=%fused_computation.6 | convolution fusion | flops 4296015872 | bytes 10485760 | tf_op jit(solution)/shard_map/stc,sdc->td/dot_general | solution.py:2043
  155.2 2.7 multiply_reduce_fusion
  158.8 2.4 reduce_sum.99
  163.3 3.0 multiply_reduce_fusion.2
  167.9 2.0 add_convert_fusion
  169.9 1.8 collective-permute-start.2
  171.9 7.4 %convert_reduce_fusion = (f32[2,1024]{1,0:T(2,128)S(1)}, bf16[2,1024,1024]{2,1,0:T(8,128)(2,1)}) fusion(bf16[2,1024,1024]{2,1,0:T(8,128)(2,1)S(1)} %copy-done.16, bf16[2,1024,1024]{2,1,0:T(8,128)(2,1)S(1)} %bitcast.108, bf16[512,1024]{1,0:T(8,128)(2,1)S(1)} %get-tuple-element.71, bf16[512,1024]{1,0:T(8,128)(2,1)S(1)} %get-tuple-element.70), kind=kOutput, calls=%fused_computation.2 | convolution fusion | flops 4309645312 | bytes 14688256 | tf_op jit(solution)/shard_map/td,sdc->stc/dot_general | solution.py:2048
  179.3 8.0 %bitcast_convert_fusion = bf16[1024,1024]{1,0:T(8,128)(2,1)S(1)} fusion(bf16[2,1024,1024]{2,1,0:T(8,128)(2,1)} %get-tuple-element.80, bf16[2,1024,1024]{2,1,0:T(8,128)(2,1)} %bitcast.106), kind=kOutput, calls=%fused_computation.5 | convolution fusion | flops 4296015872 | bytes 10485760 | tf_op jit(solution)/shard_map/stc,sdc->td/dot_general | solution.py:2052
  189.8 6.4 %convolution_convert_fusion.1 = bf16[2,1024,1024]{1,2,0:T(8,128)(2,1)} fusion(bf16[2,1024,1024]{2,1,0:T(8,128)(2,1)S(1)} %copy-done.14, bf16[512,1024]{1,0:T(8,128)(2,1)S(1)} %get-tuple-element.71, bf16[512,1024]{1,0:T(8,128)(2,1)S(1)} %get-tuple-element.70), kind=kOutput, calls=%fused_computation.15 | convolution fusion | flops 4301258752 | bytes 10485760 | tf_op jit(solution)/shard_map/td,stc->sdc/dot_general | solution.py:2047
  196.2 6.3 %convolution_convert_fusion = bf16[2,1024,1024]{1,2,0:T(8,128)(2,1)} fusion(bf16[2,1024,1024]{2,1,0:T(8,128)(2,1)S(1)} %copy-done.19, bf16[1024,1024]{1,0:T(8,128)(2,1)S(1)} %copy-done.17), kind=kOutput, calls=%fused_computation.14 | convolution fusion | flops 4297064448 | bytes 10485760 | tf_op jit(solution)/shard_map/td,stc->sdc/dot_general | solution.py:2050
  202.5 2.3 multiply_reduce_fusion.3
  205.3 2.4 multiply_add_fusion
  209.3 2.2 convolution_convert_fusion.2.grad
  211.5 2.3 convolution_convert_fusion.3
  213.8 126.2 %attend_back.1 = (bf16[2,128,1024]{2,1,0:T(8,128)(2,1)}, bf16[4,128,256]{2,1,0:T(8,128)(2,1)}, bf16[1024,1024]{1,0:T(8,128)(2,1)}, f32[3,512]{1,0:T(4,128)}) custom-call(bf16[2,2,2,2,128,1024]{5,4,3,2,1,0:T(8,128)(2,1)} %bitcast.82, bf16[2,2,2,2,128,1024]{5,4,3,2,1,0:T(8,128)(2,1)} %bitcast.83, bf16[1,2,2,2,128,512]{5,4,3,2,1,0:T(8,128)(2,1)} %bitcast.85, ...), custom_call_target="tpu_custom_call" | custom-call | tf_op jit(solution)/shard_map/attend_back/pallas_call | solution.py:1434
  340.9 1.9 fusion.20
  342.8 2.4 fusion.19
  346.5 139.0 %finish.1 = (bf16[4,128,256]{2,1,0:T(8,128)(2,1)}, bf16[2,128,1024]{2,1,0:T(8,128)(2,1)}, f32[16,1024]{1,0:T(8,128)}, bf16[512,1024]{1,0:T(8,128)(2,1)}) custom-call(bf16[4,128,256]{2,1,0:T(8,128)(2,1)} %get-tuple-element.64.attn_ref, bf16[2,128,1024]{2,1,0:T(8,128)(2,1)} %get-tuple-element.62.mlp_ref, f32[16,1024]{1,0:T(8,128)} %concatenate.7.vec_ref, ...), custom_call_target="tpu_custom_call" | custom-call | tf_op jit(solution)/shard_map/finish/pallas_call | solution.py:1904
  485.6 1.9 convert_subtract_fusion.1
  487.4 2.8 convert_element_type.117
  (94 shorter events, 21.7 us)
Async XLA Ops:
  1.4 8.7 %collective-permute-start = (s32[1024]{0:T(1024)S(1)}, s32[1024]{0:T(1024)S(1)}, u32[]{:S(2)}, u32[]{:S(2)}) collective-permute-start(s32[1024]{0:T(1024)S(1)} %bitcast.97), channel_id=1, source_target_pairs={{0,4},{1,5},{2,6},{3,7},{4,0},{5,1},{6,2},{7,3},{8,12},{9,13},{10,... | collective-permute-start | bytes 12296 | tf_op jit(solution)/shard_map/ppermute | solution.py:1948
  144.8 16.5 %collective-permute-start.3 = (bf16[512,1024]{1,0:T(8,128)(2,1)}, bf16[512,1024]{1,0:T(8,128)(2,1)}, u32[]{:S(2)}, u32[]{:S(2)}) collective-permute-start(bf16[512,1024]{1,0:T(8,128)(2,1)} %param.10), channel_id=1, source_target_pairs={{4,1},{1,4},{6,3},{3,6},{12,9},{9,12},{14,11},{11,14},{20,17},{17,... | collective-permute-start | bytes 3145736 | tf_op jit(solution)/shard_map/ppermute | solution.py:1957
  146.9 8.3 %copy-start.3 = (bf16[1024,1024]{1,0:T(8,128)(2,1)S(1)}, bf16[1024,1024]{1,0:T(8,128)(2,1)}, u32[]{:S(2)}) copy-start(bf16[1024,1024]{1,0:T(8,128)(2,1)} %get-tuple-element.49) | copy-start | bytes 6291460
  155.1 12.8 %collective-permute-start.1 = (bf16[512,1024]{1,0:T(8,128)(2,1)S(1)}, bf16[512,1024]{1,0:T(8,128)(2,1)}, u32[]{:S(2)}, u32[]{:S(2)}) collective-permute-start(bf16[512,1024]{1,0:T(8,128)(2,1)S(1)} %constant_dynamic-slice_fusion.1), channel_id=1, source_target_pairs={{0,4},{1,5},{2,6},{3,7},{4,0},{5,1},{6,2},{7,3},{8,12},{9,13},{10,... | collective-permute-start | bytes 3145736 | tf_op jit(solution)/shard_map/ppermute | solution.py:1948
  161.3 5.1 %copy-start.2 = (f32[1024,1024]{1,0:T(8,128)S(1)}, f32[1024,1024]{1,0:T(8,128)}, u32[]{:S(2)}) copy-start(f32[1024,1024]{1,0:T(8,128)} %get-tuple-element.69) | copy-start | bytes 12582916
  162.8 5.1 %copy-start = (f32[1024,1024]{1,0:T(8,128)S(1)}, f32[1024,1024]{1,0:T(8,128)}, u32[]{:S(2)}) copy-start(f32[1024,1024]{1,0:T(8,128)} %get-tuple-element.32) | copy-start | bytes 12582916
  162.8 8.9 %collective-permute-start.4 = (bf16[512,1024]{1,0:T(8,128)(2,1)S(1)}, bf16[512,1024]{1,0:T(8,128)(2,1)S(1)}, u32[]{:S(2)}, u32[]{:S(2)}) collective-permute-start(bf16[512,1024]{1,0:T(8,128)(2,1)S(1)} %broadcast_select_fusion.2), channel_id=1, source_target_pairs={{0,4},{1,5},{2,6},{3,7},{4,0},{5,1},{6,2},{7,3},{8,12},{9,13},{10,... | collective-permute-start | bytes 3145736 | tf_op jit(solution)/shard_map/ppermute | solution.py:1948
  167.9 3.9 copy-start.15
  167.9 3.9 copy-start.16
  169.9 18.8 %collective-permute-start.2 = (bf16[512,1024]{1,0:T(8,128)(2,1)S(1)}, bf16[512,1024]{1,0:T(8,128)(2,1)}, u32[]{:S(2)}, u32[]{:S(2)}) collective-permute-start(bf16[512,1024]{1,0:T(8,128)(2,1)S(1)} %add_convert_fusion), channel_id=1, source_target_pairs={{4,1},{1,4},{6,3},{3,6},{12,9},{9,12},{14,11},{11,14},{20,17},{17,... | collective-permute-start | bytes 3145736 | tf_op jit(solution)/shard_map/ppermute | solution.py:1957
  187.3 2.5 copy-start.14
  187.3 15.2 %collective-permute-start.5 = (bf16[1024,1024]{1,0:T(8,128)(2,1)S(1)}, bf16[1024,1024]{1,0:T(8,128)(2,1)S(1)}, u32[]{:S(2)}, u32[]{:S(2)}) collective-permute-start(bf16[1024,1024]{1,0:T(8,128)(2,1)S(1)} %bitcast_convert_fusion), channel_id=1, source_target_pairs={{0,4},{1,5},{2,6},{3,7},{4,0},{5,1},{6,2},{7,3},{8,12},{9,13},{10,... | collective-permute-start | bytes 6291464 | tf_op jit(solution)/shard_map/ppermute | solution.py:1948
  189.8 6.4 %copy-start.17 = (bf16[1024,1024]{1,0:T(8,128)(2,1)S(1)}, bf16[1024,1024]{1,0:T(8,128)(2,1)}, u32[]{:S(2)}) copy-start(bf16[1024,1024]{1,0:T(8,128)(2,1)} %get-tuple-element.37) | copy-start | bytes 6291460
  189.8 6.4 %copy-start.19 = (bf16[2,1024,1024]{2,1,0:T(8,128)(2,1)S(1)}, bf16[2,1024,1024]{2,1,0:T(8,128)(2,1)}, u32[]{:S(2)}) copy-start(bf16[2,1024,1024]{2,1,0:T(8,128)(2,1)} %get-tuple-element.80) | copy-start | bytes 12582916
  196.2 6.3 %copy-start.1 = (f32[1024,1024]{1,0:T(8,128)S(1)}, f32[1024,1024]{1,0:T(8,128)}, u32[]{:S(2)}) copy-start(f32[1024,1024]{1,0:T(8,128)} %get-tuple-element.32) | copy-start | bytes 12582916
  209.3 2.2 copy-start.7
  213.8 127.1 %copy-start.8 = (f32[4,128,256]{2,1,0:T(8,128)S(1)}, f32[4,128,256]{2,1,0:T(8,128)}, u32[]{:S(2)}) copy-start(f32[4,128,256]{2,1,0:T(8,128)} %param.15) | copy-start | bytes 1572868
  213.8 129.0 %copy-start.6 = (f32[2,128,1024]{2,1,0:T(8,128)S(1)}, f32[2,128,1024]{2,1,0:T(8,128)}, u32[]{:S(2)}) copy-start(f32[2,128,1024]{2,1,0:T(8,128)} %param.16) | copy-start | bytes 3145732
  345.2 140.4 %copy-start.5 = (f32[4,128,256]{2,1,0:T(8,128)S(1)}, f32[4,128,256]{2,1,0:T(8,128)}, u32[]{:S(2)}) copy-start(f32[4,128,256]{2,1,0:T(8,128)} %param.12) | copy-start | bytes 1572868
  346.5 143.8 %copy-start.4 = (f32[2,128,1024]{2,1,0:T(8,128)S(1)}, f32[2,128,1024]{2,1,0:T(8,128)}, u32[]{:S(2)}) copy-start(f32[2,128,1024]{2,1,0:T(8,128)} %param.13) | copy-start | bytes 3145732
  485.5 4.7 copy-start.9
  485.5 5.9 %copy-start.10 = (f32[12,1024]{1,0:T(8,128)S(1)}, f32[12,1024]{1,0:T(8,128)}, u32[]{:S(2)}) copy-start(f32[12,1024]{1,0:T(8,128)} %vectors.1) | copy-start | bytes 147460
  485.6 5.8 %copy-start.11 = (f32[12,1024]{1,0:T(8,128)S(1)}, f32[12,1024]{1,0:T(8,128)}, u32[]{:S(2)}) copy-start(f32[12,1024]{1,0:T(8,128)} %param.17) | copy-start | bytes 147460
  485.6 5.8 %copy-start.12 = (f32[16,1024]{1,0:T(8,128)S(1)}, f32[16,1024]{1,0:T(8,128)}, u32[]{:S(2)}) copy-start(f32[16,1024]{1,0:T(8,128)} %get-tuple-element.53) | copy-start | bytes 196612
  (2 other events, 2.6 us)
